TPU v7x, 32 devices: a whole 2x2x4 slice. The times are simulated.
32 devices in a mesh: parts: 2 (over x), band: 8 (over z, y), depth: 2 (over core).
Axes of the slice: x: 2, y: 2, z: 4, core: 2. Of those that a mesh axis runs over, the one named last changes fastest.
Arguments:
- estimate: float32 [4, 1024, 3072], P('depth', 'parts', 'band'), parts along dimension 1, may hold values from 0.5 to 1.5
- psf_blocks: bfloat16 [4, 9, 361, 512], P('depth'), may hold values from 1.9520521e-06 to 0.001953125
- offset_ids: int32 [4, 9], P('depth'), may hold values from 0 to 8, as said below
- block_counts: int32 [4], P('depth'), may hold values from 1 to 9, as said below
- measured: float32 [722, 3072], P('parts', 'band'), parts along dimension 0, may hold values from 0.5 to 6
- background: float32 [722, 3072], P('parts', 'band'), parts along dimension 0, may hold values from 0.2 to 1
Outputs:
- volume: float32 [4, 1024, 3072], P('depth', 'parts', 'band'), parts along dimension 1
There are 2 independent parts, one for each index of `parts`. A program takes and returns all parts, laid end to end along the dimension named above; an argument that names none is the same for every part. Nothing has to cross between parts.
Inputs may be any that keep to these rules, and one draw needn't show every extreme that they name: `offset_ids`: each row lists 9 distinct offset ids; the first is 4, the lenslet itself. `block_counts`: the deepest slab uses all 9 blocks.
All inputs are finite; a program needn't handle non-finite values.
Results may differ from a plain program's by a relative error of at most 0.0003.
Values may be sent and summed in bfloat16 or wider, within the bound.
No kernel may reach another device: no remote copies, remote signals or barrier semaphores. Data moves between devices by JAX's collectives and lax.ppermute only.
A program may use at most 64 MiB of HBM per device.

v0:
```python
import functools
import jax
import jax.numpy as jnp
from jax import lax
from jax.experimental import pallas as pl
from jax.experimental.pallas import tpu as pltpu
from jax.sharding import PartitionSpec as P

LX = 96
BF = jnp.bfloat16
F32 = jnp.float32
MAIN = 256
PADW = 384
TAIL = PADW - MAIN

SMEM = pl.BlockSpec(memory_space=pltpu.SMEM)
VMEM = pl.BlockSpec(memory_space=pltpu.VMEM)
ANY = pl.BlockSpec(memory_space=pl.ANY)


def dot(a, b):
    return lax.dot_general(a, b, (((1,), (0,)), ((), ())), preferred_element_type=F32)


def dot_t(a, b):
    return lax.dot_general(a, b, (((1,), (1,)), ((), ())), preferred_element_type=F32)


def place(ids, counts, plane, slot):
    ident = ids[plane, jnp.minimum(slot, ids.shape[1] - 1)]
    start = pl.multiple_of((2 - ident // 3) * LX, LX)
    return start, jnp.where(slot < counts[plane], ident % 3, 3)


def pair_blocks(kp, plane, a):
    tails = kp[plane, pl.ds(a, 2), MAIN:PADW, :].reshape(2 * TAIL, kp.shape[3])
    return jnp.concatenate([kp[plane, a, 0:MAIN, :], kp[plane, a + 1, 0:MAIN, :], tails], axis=0)


def project_pair(ids, counts, plane, p, x, kp, acc):
    rows = x.shape[0]
    row_a, dx_a = place(ids, counts, plane, 2 * p)
    row_b, dx_b = place(ids, counts, plane, 2 * p + 1)
    out = dot_t(x, pair_blocks(kp, plane, 2 * p))
    acc[dx_a, pl.ds(row_a, rows), 0:MAIN] += out[:, 0:MAIN]
    acc[dx_b, pl.ds(row_b, rows), 0:MAIN] += out[:, MAIN : 2 * MAIN]
    acc[dx_a, pl.ds(row_a, rows), MAIN:PADW] += out[:, 2 * MAIN : 2 * MAIN + TAIL]
    acc[dx_b, pl.ds(row_b, rows), MAIN:PADW] += out[:, 2 * MAIN + TAIL :]


def column_of(rows, width):
    return lax.rem(lax.broadcasted_iota(jnp.int32, (rows, width), 0), LX)


def fold_dx(acc):
    rows = acc.shape[1]
    col = column_of(rows, PADW)
    left = jnp.where(col > 0, pltpu.roll(acc[0], 1, 0), 0.0)
    right = jnp.where(col < LX - 1, pltpu.roll(acc[2], rows - 1, 0), 0.0)
    return acc[1] + left + right


def first_kernel(ids, counts, est, psf, part_out, est_out, kp, kraw, ev, xs, acc, ksem, esem):
    planes = est.shape[0]
    slots, pix = psf.shape[0], psf.shape[1]
    kcopies = [pltpu.make_async_copy(psf.at[s], kraw.at[s], ksem.at[s]) for s in range(slots)]
    ecopies = [pltpu.make_async_copy(est.at[z], ev.at[z], esem.at[z]) for z in range(planes)]
    kcopies[0].start()
    kcopies[1].start()
    for c in ecopies:
        c.start()
    for c in kcopies[2:]:
        c.start()
    acc[0:3] = jnp.zeros((3,) + acc.shape[1:], F32)
    full = pix // 16 * 16
    kp[:, :, full:PADW, :] = jnp.zeros(kp.shape[:2] + (PADW - full, kp.shape[3]), BF)
    if slots % 2:
        kp[:, slots, 0:full, :] = jnp.zeros((planes, full, kp.shape[3]), BF)

    def split(s):
        both = jnp.swapaxes(kraw[s], 0, 1)
        for z in range(planes):
            kp[z, s, 0:pix, :] = both[z]

    for s in range(2):
        kcopies[s].wait()
        split(s)
    for z in range(planes):
        ecopies[z].wait()
        t = ev[z].T
        est_out[z] = t
        xs[z] = t.astype(BF)
    pairs = kp.shape[1] // 2
    for p in range(pairs):
        for s in (2 * p + 2, 2 * p + 3):
            if s < slots:
                kcopies[s].wait()
        for s in (2 * p + 2, 2 * p + 3):
            if s < slots:
                split(s)
        for z in range(planes):
            project_pair(ids, counts, z, p, xs[z], kp, acc)
    part_out[...] = fold_dx(acc)


def first_call(estimate, psf, ids, counts):
    planes, vox, lens = estimate.shape
    slots, pix = psf.shape[1:3]
    rows = lens + 2 * LX
    even = slots + slots % 2
    return pl.pallas_call(
        first_kernel,
        out_shape=(
            jax.ShapeDtypeStruct((rows, PADW), F32),
            jax.ShapeDtypeStruct((planes, lens, vox), F32),
            jax.ShapeDtypeStruct((planes, even, PADW, vox), BF),
        ),
        in_specs=[SMEM, SMEM, ANY, ANY],
        out_specs=(VMEM, VMEM, VMEM),
        scratch_shapes=[
            pltpu.VMEM((slots, pix, planes, vox), BF),
            pltpu.VMEM((planes, vox, lens), F32),
            pltpu.VMEM((planes, lens, vox), BF),
            pltpu.VMEM((4, rows, PADW), F32),
            pltpu.SemaphoreType.DMA((slots,)),
            pltpu.SemaphoreType.DMA((planes,)),
        ],
        compiler_params=pltpu.CompilerParams(vmem_limit_bytes=36 << 20),
        name="project_first",
    )(ids, counts, estimate, jnp.transpose(psf, (1, 2, 0, 3)))


def sensor_kernel(meas, bg, out):
    pix = meas.shape[0]
    out[...] = jnp.zeros(out.shape, F32)
    out[0, :, 0:pix] = meas[...].T
    out[1, :, 0:pix] = bg[...].T


def sensor_call(measured, background):
    lens = measured.shape[1]
    return pl.pallas_call(
        sensor_kernel,
        out_shape=jax.ShapeDtypeStruct((2, lens, PADW), F32),
        in_specs=[VMEM, VMEM],
        out_specs=VMEM,
        compiler_params=pltpu.CompilerParams(vmem_limit_bytes=16 << 20),
        name="sensor_turn",
    )(measured, background)


def upward():
    return lax.rem(lax.axis_index("band") + lax.axis_index("depth"), 2) == 0


def edge_kernel(own, other, *refs):
    sensor, out = (refs[0], refs[1]) if len(refs) == 2 else (None, refs[0])
    rows = own.shape[0]
    up = upward()
    outer = pl.multiple_of(jnp.where(up, rows - LX, 0), LX)
    inner = pl.multiple_of(jnp.where(up, rows - 2 * LX, LX), LX)
    for i, start in enumerate((outer, inner)):
        out[i] = (own[pl.ds(start, LX), :] + other[pl.ds(start, LX), :]).astype(BF)
    if sensor is not None:
        line = pl.multiple_of(inner - LX, LX)
        for i in range(2):
            out[2 + i] = sensor[i, pl.ds(line, LX), :].astype(BF)


def edge_call(own, other, *sensor):
    return pl.pallas_call(
        edge_kernel,
        out_shape=jax.ShapeDtypeStruct((2 + 2 * len(sensor), LX, PADW), BF),
        in_specs=[VMEM] * (2 + len(sensor)),
        out_specs=VMEM,
        compiler_params=pltpu.CompilerParams(vmem_limit_bytes=16 << 20),
        name="edge_rows",
    )(own, other, *sensor)


def ratio_planes(own, other, mine, theirs, sensor, halo, planes_ref, pix):
    rows = own.shape[0]
    lens = rows - 2 * LX
    band = lax.axis_index("band")
    up = upward()
    upper = [jnp.where(up, mine[i].astype(F32), theirs[i].astype(F32)) for i in range(2)]
    lower = [jnp.where(up, theirs[i].astype(F32), mine[i].astype(F32)) for i in range(2)]
    lane = lax.broadcasted_iota(jnp.int32, (1, PADW), 1) < pix

    def ratio(start, size, extra, measured, background, there):
        total = own[start : start + size, :] + other[start : start + size, :]
        if extra is not None:
            total = total + extra
        keep = lane if there is None else jnp.logical_and(lane, there)
        return jnp.where(keep, measured / (total + background), 0.0).astype(BF).astype(F32)

    parts = [
        ratio(0, LX, lower[1], halo[0], halo[1], band > 0),
        ratio(LX, LX, lower[0], sensor[0, 0:LX], sensor[1, 0:LX], None),
        ratio(2 * LX, lens - 2 * LX, None, sensor[0, LX : lens - LX], sensor[1, LX : lens - LX], None),
        ratio(lens, LX, upper[0], sensor[0, lens - LX : lens], sensor[1, lens - LX : lens], None),
        ratio(lens + LX, LX, upper[1], halo[2], halo[3], band < lax.axis_size("band") - 1),
    ]
    whole = jnp.concatenate(parts, axis=0)
    col = column_of(rows, PADW)
    planes_ref[1] = whole.astype(BF)
    planes_ref[2] = jnp.where(col > 0, pltpu.roll(whole, 1, 0), 0.0).astype(BF)
    planes_ref[0] = jnp.where(col < LX - 1, pltpu.roll(whole, rows - 1, 0), 0.0).astype(BF)
    planes_ref[3] = jnp.zeros((rows, PADW), BF)


def back_slab(ids, counts, plane, ratios, kp, acc, colsum):
    lens = acc.shape[0]
    acc[...] = jnp.zeros(acc.shape, F32)
    if colsum is not None:
        colsum[...] = jnp.zeros(colsum.shape, F32)
        row = lax.broadcasted_iota(jnp.int32, (16, 2 * MAIN + 2 * TAIL), 0)
        lane = lax.broadcasted_iota(jnp.int32, (16, 2 * MAIN + 2 * TAIL), 1)
        first = jnp.logical_or(lane < MAIN, jnp.logical_and(lane >= 2 * MAIN, lane < 2 * MAIN + TAIL))
        ones = jnp.where(row == jnp.where(first, 0, 1), 1.0, 0.0).astype(BF)

    def pair(p, carry):
        row_a, dx_a = place(ids, counts, plane, 2 * p)
        row_b, dx_b = place(ids, counts, plane, 2 * p + 1)
        a = ratios[dx_a, pl.ds(row_a, lens), :]
        b = ratios[dx_b, pl.ds(row_b, lens), :]
        left = jnp.concatenate([a[:, 0:MAIN], b[:, 0:MAIN], a[:, MAIN:], b[:, MAIN:]], axis=1)
        if colsum is not None:
            left = jnp.concatenate([left, ones], axis=0)
        out = dot(left, pair_blocks(kp, plane, 2 * p))
        acc[...] += out[0:lens]
        if colsum is not None:
            colsum[p] = out[lens : lens + 8]
        return carry

    lax.fori_loop(0, (counts[plane] + 1) // 2, pair, 0)


def sensitivity_slab(ids, counts, plane, lens, colsum):
    groups = colsum.shape[0] * 8
    sums = colsum[...].reshape(groups, colsum.shape[2])
    high = sums.astype(BF)
    rest = sums - high.astype(F32)
    mid = rest.astype(BF)
    low = (rest - mid.astype(F32)).astype(BF)
    right = jnp.concatenate([high.astype(F32), mid.astype(F32), low.astype(F32)], axis=0)
    right = jnp.concatenate([right, jnp.zeros((128 - 3 * groups, right.shape[1]), F32)], axis=0).astype(BF)
    lane = lax.broadcasted_iota(jnp.int32, (1, 128), 1)
    place_of = lax.rem(lane, groups)
    dy = jnp.full((1, 128), 2, jnp.int32)
    dx = jnp.full((1, 128), 2, jnp.int32)
    active = jnp.zeros((1, 128), jnp.int32)
    for s in range(ids.shape[1]):
        here = place_of == (s // 2) * 8 + s % 2
        ident = ids[plane, s]
        dy = jnp.where(here, ident // 3 - 1, dy)
        dx = jnp.where(here, ident % 3 - 1, dx)
        active = jnp.where(here, (s < counts[plane]).astype(jnp.int32), active)
    active = jnp.where(lane < 3 * groups, active, 0)
    l = lax.broadcasted_iota(jnp.int32, (lens, 128), 0)
    grid_rows = lens // LX * lax.axis_size("band")
    row = lax.axis_index("band") * (lens // LX) + l // LX - dy
    col = lax.rem(l, LX) - dx
    inside = (row >= 0) & (row < grid_rows) & (col >= 0) & (col < LX) & (active > 0)
    return dot(jnp.where(inside, 1.0, 0.0).astype(BF), right)


def middle_kernel(pix, ids, counts, own, other, mine, theirs, sensor, est, kp, part_out, vol_out, inv_out, halo_out, ratios, xs, back, colsum, acc):
    up = upward()
    for i in range(2):
        a = mine[2 + i].astype(F32)
        b = theirs[2 + i].astype(F32)
        halo_out[i] = jnp.where(up, b, a)
        halo_out[2 + i] = jnp.where(up, a, b)
    ratio_planes(own, other, mine, theirs, sensor, halo_out, ratios, pix)
    acc[0:3] = jnp.zeros((3,) + acc.shape[1:], F32)
    lens = est.shape[1]
    for z in range(est.shape[0]):
        back_slab(ids, counts, z, ratios, kp, back, colsum)
        inv = 1.0 / sensitivity_slab(ids, counts, z, lens, colsum)
        inv_out[z] = inv
        vol = est[z] * back[...] * inv
        vol_out[z] = vol
        xs[...] = vol.astype(BF)

        def pair(p, carry, z=z):
            project_pair(ids, counts, z, p, xs[...], kp, acc)
            return carry

        lax.fori_loop(0, (counts[z] + 1) // 2, pair, 0)
    part_out[...] = fold_dx(acc)


def middle_call(pix, ids, counts, own, other, mine, theirs, sensor, est, kp):
    planes, lens, vox = est.shape
    rows = own.shape[0]
    return pl.pallas_call(
        functools.partial(middle_kernel, pix),
        out_shape=(
            jax.ShapeDtypeStruct((rows, PADW), F32),
            jax.ShapeDtypeStruct((planes, lens, vox), F32),
            jax.ShapeDtypeStruct((planes, lens, vox), F32),
            jax.ShapeDtypeStruct((4, LX, PADW), F32),
        ),
        in_specs=[SMEM, SMEM] + [VMEM] * 7,
        out_specs=(VMEM,) * 4,
        scratch_shapes=[
            pltpu.VMEM((4, rows, PADW), BF),
            pltpu.VMEM((lens, vox), BF),
            pltpu.VMEM((lens, vox), F32),
            pltpu.VMEM((kp.shape[1] // 2, 8, vox), F32),
            pltpu.VMEM((4, rows, PADW), F32),
        ],
        compiler_params=pltpu.CompilerParams(vmem_limit_bytes=36 << 20),
        name="back_and_project",
    )(ids, counts, own, other, mine, theirs, sensor, est, kp)


def last_kernel(pix, ids, counts, own, other, mine, theirs, sensor, halo, vol, inv, kp, out, ratios, back):
    ratio_planes(own, other, mine, theirs, sensor, halo, ratios, pix)
    for z in range(vol.shape[0]):
        back_slab(ids, counts, z, ratios, kp, back, None)
        out[z] = (vol[z] * back[...] * inv[z]).T


def last_call(pix, ids, counts, own, other, mine, theirs, sensor, halo, vol, inv, kp):
    planes, lens, vox = vol.shape
    rows = own.shape[0]
    return pl.pallas_call(
        functools.partial(last_kernel, pix),
        out_shape=jax.ShapeDtypeStruct((planes, vox, lens), F32),
        in_specs=[SMEM, SMEM] + [VMEM] * 9,
        out_specs=VMEM,
        scratch_shapes=[
            pltpu.VMEM((4, rows, PADW), BF),
            pltpu.VMEM((lens, vox), F32),
        ],
        compiler_params=pltpu.CompilerParams(vmem_limit_bytes=36 << 20),
        name="back_last",
    )(ids, counts, own, other, mine, theirs, sensor, halo, vol, inv, kp)


def swap(x):
    return lax.ppermute(x, "depth", [(0, 1), (1, 0)])


def edge_exchange(x):
    bands = lax.axis_size("band")
    pairs = []
    for b in range(bands - 1):
        d = b % 2
        pairs += [(2 * b + d, 2 * b + 2 + d), (2 * b + 2 + d, 2 * b + d)]
    return lax.ppermute(x, ("band", "depth"), pairs)


def per_device(estimate, psf_blocks, offset_ids, block_counts, measured, background):
    pix = measured.shape[0]
    part, est, kp = first_call(estimate, psf_blocks, offset_ids, block_counts)
    other = swap(part)
    sensor = sensor_call(measured, background)
    mine = edge_exchange(edge_call(part, other, sensor))
    theirs = swap(mine)
    part, vol, inv, halo = middle_call(pix, offset_ids, block_counts, part, other, mine, theirs, sensor, est, kp)
    other = swap(part)
    mine = edge_exchange(edge_call(part, other))
    theirs = swap(mine)
    return last_call(pix, offset_ids, block_counts, part, other, mine, theirs, sensor, halo, vol, inv, kp)


def solution(mesh):
    in_specs = (
        P("depth", "parts", "band"),
        P("depth", None, None, None),
        P("depth", None),
        P("depth"),
        P("parts", "band"),
        P("parts", "band"),
    )
    return jax.shard_map(
        per_device, mesh=mesh, in_specs=in_specs, out_specs=P("depth", "parts", "band"), check_vma=False
    )
```

profile of v0, /device:TPU:0, one launch (start us, length us, event | category | flops | bytes accessed | tf_op | source)
XLA Modules:
  0.0 61.7 jit_solution(14621606821782057690)
XLA Ops:
  0.0 0.0 copy-start
  0.0 2.9 %copy-done = bf16[2,9,361,512]{3,0,2,1:T(2,128)(2,1)S(1)} copy-done((bf16[2,9,361,512]{3,0,2,1:T(2,128)(2,1)S(1)}, bf16[2,9,361,512]{3,0,2,1:T(2,128)(2,1)}, u32[]{:S(2)}) %copy-start) | copy-done | bytes 6653976
  2.9 0.0 copy-start.1
  2.9 1.4 %copy-done.1 = f32[2,512,384]{2,1,0:T(8,128)S(1)} copy-done((f32[2,512,384]{2,1,0:T(8,128)S(1)}, f32[2,512,384]{2,1,0:T(8,128)}, u32[]{:S(2)}) %copy-start.1) | copy-done | bytes 1572888
  4.3 0.0 copy-start.4
  4.3 0.7 %copy-done.4 = s32[2,9]{1,0:T(2,128)S(1)} copy-done((s32[2,9]{1,0:T(2,128)S(1)}, s32[2,9]{1,0:T(2,128)}, u32[]{:S(2)}) %copy-start.4) | copy-done | bytes 96
  5.0 0.0 copy-start.5
  5.0 0.7 %copy-done.5 = s32[2]{0:T(128)S(1)} copy-done((s32[2]{0:T(128)S(1)}, s32[2]{0:T(128)}, u32[]{:S(2)}) %copy-start.5) | copy-done | bytes 32
  5.6 0.0 copy-start.2
  5.6 0.0 copy-start.3
  5.6 10.9 %project_first.1 = (f32[576,384]{1,0:T(8,128)S(1)}, f32[2,384,512]{2,1,0:T(8,128)S(1)}, bf16[2,10,384,512]{3,2,1,0:T(8,128)(2,1)S(1)}) custom-call(s32[2,9]{1,0:T(2,128)S(1)} %copy-done.4, s32[2]{0:T(128)S(1)} %copy-done.5, f32[2,512,384]{2,1,0:T(8,128)S(1)} %copy-done.1, bf16[9,361,2,512]{3,2,1,0:T(2,128)(2,1)S(1)} %bitcast.1), custom_call_target="tpu_custom_call" | custom-call | tf_op jit(solution)/shard_map/project_first/pallas_call | solution.py:111
  16.6 0.5 collective-permute-start
  17.1 0.0 copy-done.2
  17.1 0.0 copy-done.3
  17.1 0.4 sensor_turn.1.refs_0_.sensor
  17.5 1.7 %collective-permute-done.other = f32[576,384]{1,0:T(8,128)S(1)} collective-permute-done((f32[576,384]{1,0:T(8,128)S(1)}, f32[576,384]{1,0:T(8,128)S(1)}, u32[]{:S(2)}, u32[]{:S(2)}) %collective-permute-start) | collective-permute-done | bytes 884768 | tf_op jit(solution)/shard_map/ppermute | solution.py:344
  19.2 4.8 %collective-permute-start.1 = (bf16[4,96,384]{2,1,0:T(8,128)(2,1)S(1)}, bf16[4,96,384]{2,1,0:T(8,128)(2,1)S(1)}, u32[]{:S(2)}, u32[]{:S(2)}) collective-permute-start(bf16[4,96,384]{2,1,0:T(8,128)(2,1)S(1)} %edge_rows.2), channel_id=1, source_target_pairs={{0,2},{2,0},{3,5},{5,3},{4,6},{6,4},{7,9},{9,7},{8,10},{10,8},{11,... | collective-permute-start | bytes 884744 | tf_op jit(solution)/shard_map/ppermute | solution.py:353
  24.0 7.4 %collective-permute-done.1.mine = bf16[4,96,384]{2,1,0:T(8,128)(2,1)S(1)} collective-permute-done((bf16[4,96,384]{2,1,0:T(8,128)(2,1)S(1)}, bf16[4,96,384]{2,1,0:T(8,128)(2,1)S(1)}, u32[]{:S(2)}, u32[]{:S(2)}) %collective-permute-start.1) | collective-permute-done | bytes 294944 | tf_op jit(solution)/shard_map/ppermute | solution.py:353
  31.4 0.0 collective-permute-start.2
  31.4 1.6 %collective-permute-done.2.theirs = bf16[4,96,384]{2,1,0:T(8,128)(2,1)S(1)} collective-permute-done((bf16[4,96,384]{2,1,0:T(8,128)(2,1)S(1)}, bf16[4,96,384]{2,1,0:T(8,128)(2,1)S(1)}, u32[]{:S(2)}, u32[]{:S(2)}) %collective-permute-start.2) | collective-permute-done | bytes 294944 | tf_op jit(solution)/shard_map/ppermute | solution.py:344
  33.0 10.0 %back_and_project.1 = (f32[576,384]{1,0:T(8,128)S(1)}, f32[2,384,512]{2,1,0:T(8,128)S(1)}, f32[2,384,512]{2,1,0:T(8,128)S(1)}, f32[4,96,384]{2,1,0:T(8,128)S(1)}) custom-call(s32[2,9]{1,0:T(2,128)S(1)} %copy-done.4, s32[2]{0:T(128)S(1)} %copy-done.5, f32[576,384]{1,0:T(8,128)S(1)} %get-tuple-element.12.own, f32[576,384]{1,0:T(8,128)S(1)} %collective-permute-done.other, ...), custom_call_target="tpu_custom_call" | custom-call | tf_op jit(solution)/shard_map/back_and_project/pallas_call | solution.py:297
  43.0 0.1 collective-permute-start.3
  43.1 2.4 %collective-permute-done.3.other = f32[576,384]{1,0:T(8,128)S(1)} collective-permute-done((f32[576,384]{1,0:T(8,128)S(1)}, f32[576,384]{1,0:T(8,128)S(1)}, u32[]{:S(2)}, u32[]{:S(2)}) %collective-permute-start.3) | collective-permute-done | bytes 884768 | tf_op jit(solution)/shard_map/ppermute | solution.py:344
  45.5 4.4 %collective-permute-start.4 = (bf16[2,96,384]{2,1,0:T(8,128)(2,1)S(1)}, bf16[2,96,384]{2,1,0:T(8,128)(2,1)S(1)}, u32[]{:S(2)}, u32[]{:S(2)}) collective-permute-start(bf16[2,96,384]{2,1,0:T(8,128)(2,1)S(1)} %edge_rows.3), channel_id=1, source_target_pairs={{0,2},{2,0},{3,5},{5,3},{4,6},{6,4},{7,9},{9,7},{8,10},{10,8},{11,... | collective-permute-start | bytes 442376 | tf_op jit(solution)/shard_map/ppermute | solution.py:353
  49.9 4.2 %collective-permute-done.4.mine = bf16[2,96,384]{2,1,0:T(8,128)(2,1)S(1)} collective-permute-done((bf16[2,96,384]{2,1,0:T(8,128)(2,1)S(1)}, bf16[2,96,384]{2,1,0:T(8,128)(2,1)S(1)}, u32[]{:S(2)}, u32[]{:S(2)}) %collective-permute-start.4) | collective-permute-done | bytes 147488 | tf_op jit(solution)/shard_map/ppermute | solution.py:353
  54.1 0.0 collective-permute-start.5
  54.1 1.4 %collective-permute-done.5.theirs = bf16[2,96,384]{2,1,0:T(8,128)(2,1)S(1)} collective-permute-done((bf16[2,96,384]{2,1,0:T(8,128)(2,1)S(1)}, bf16[2,96,384]{2,1,0:T(8,128)(2,1)S(1)}, u32[]{:S(2)}, u32[]{:S(2)}) %collective-permute-start.5) | collective-permute-done | bytes 147488 | tf_op jit(solution)/shard_map/ppermute | solution.py:344
  55.5 6.2 %back_last.1 = f32[2,512,384]{2,1,0:T(8,128)} custom-call(s32[2,9]{1,0:T(2,128)S(1)} %copy-done.4, s32[2]{0:T(128)S(1)} %copy-done.5, f32[576,384]{1,0:T(8,128)S(1)} %get-tuple-element.15.own, f32[576,384]{1,0:T(8,128)S(1)} %collective-permute-done.3.other, bf16[2,96,384]{2,1,0:T(8,128)(2,1)S(1)} %collective-permute-done.4.mine, ...), custom_call_target="tpu_custom_call" | custom-call | tf_op jit(solution)/shard_map/back_last/pallas_call | solution.py:329
  (2 shorter events, 0.1 us)
Async XLA Ops:
  0.0 2.9 %copy-start = (bf16[2,9,361,512]{3,0,2,1:T(2,128)(2,1)S(1)}, bf16[2,9,361,512]{3,0,2,1:T(2,128)(2,1)}, u32[]{:S(2)}) copy-start(bf16[2,9,361,512]{3,0,2,1:T(2,128)(2,1)} %param.7) | copy-start | bytes 19961860
  2.9 1.4 %copy-start.1 = (f32[2,512,384]{2,1,0:T(8,128)S(1)}, f32[2,512,384]{2,1,0:T(8,128)}, u32[]{:S(2)}) copy-start(f32[2,512,384]{2,1,0:T(8,128)} %est.1) | copy-start | bytes 4718596
  4.3 0.7 %copy-start.4 = (s32[2,9]{1,0:T(2,128)S(1)}, s32[2,9]{1,0:T(2,128)}, u32[]{:S(2)}) copy-start(s32[2,9]{1,0:T(2,128)} %ids.5) | copy-start | bytes 220
  5.0 0.7 %copy-start.5 = (s32[2]{0:T(128)S(1)}, s32[2]{0:T(128)}, u32[]{:S(2)}) copy-start(s32[2]{0:T(128)} %counts.5) | copy-start | bytes 28
  5.6 11.5 %copy-start.2 = (f32[361,384]{1,0:T(8,128)S(1)}, f32[361,384]{1,0:T(8,128)}, u32[]{:S(2)}) copy-start(f32[361,384]{1,0:T(8,128)} %meas.1) | copy-start | bytes 1663492
  5.6 11.5 %copy-start.3 = (f32[361,384]{1,0:T(8,128)S(1)}, f32[361,384]{1,0:T(8,128)}, u32[]{:S(2)}) copy-start(f32[361,384]{1,0:T(8,128)} %bg.1) | copy-start | bytes 1663492
  16.6 2.6 %collective-permute-start = (f32[576,384]{1,0:T(8,128)S(1)}, f32[576,384]{1,0:T(8,128)S(1)}, u32[]{:S(2)}, u32[]{:S(2)}) collective-permute-start(f32[576,384]{1,0:T(8,128)S(1)} %get-tuple-element.12.own), channel_id=1, source_target_pairs={{0,1},{1,0},{2,3},{3,2},{4,5},{5,4},{6,7},{7,6},{8,9},{9,8},{10,11... | collective-permute-start | bytes 2654216 | tf_op jit(solution)/shard_map/ppermute | solution.py:344
  19.2 12.2 %collective-permute-start.1 = (bf16[4,96,384]{2,1,0:T(8,128)(2,1)S(1)}, bf16[4,96,384]{2,1,0:T(8,128)(2,1)S(1)}, u32[]{:S(2)}, u32[]{:S(2)}) collective-permute-start(bf16[4,96,384]{2,1,0:T(8,128)(2,1)S(1)} %edge_rows.2), channel_id=1, source_target_pairs={{0,2},{2,0},{3,5},{5,3},{4,6},{6,4},{7,9},{9,7},{8,10},{10,8},{11,... | collective-permute-start | bytes 884744 | tf_op jit(solution)/shard_map/ppermute | solution.py:353
  31.4 1.6 %collective-permute-start.2 = (bf16[4,96,384]{2,1,0:T(8,128)(2,1)S(1)}, bf16[4,96,384]{2,1,0:T(8,128)(2,1)S(1)}, u32[]{:S(2)}, u32[]{:S(2)}) collective-permute-start(bf16[4,96,384]{2,1,0:T(8,128)(2,1)S(1)} %collective-permute-done.1.mine), channel_id=1, source_target_pairs={{0,1},{1,0},{2,3},{3,2},{4,5},{5,4},{6,7},{7,6},{8,9},{9,8},{10,11... | collective-permute-start | bytes 884744 | tf_op jit(solution)/shard_map/ppermute | solution.py:344
  43.0 2.5 %collective-permute-start.3 = (f32[576,384]{1,0:T(8,128)S(1)}, f32[576,384]{1,0:T(8,128)S(1)}, u32[]{:S(2)}, u32[]{:S(2)}) collective-permute-start(f32[576,384]{1,0:T(8,128)S(1)} %get-tuple-element.15.own), channel_id=1, source_target_pairs={{0,1},{1,0},{2,3},{3,2},{4,5},{5,4},{6,7},{7,6},{8,9},{9,8},{10,11... | collective-permute-start | bytes 2654216 | tf_op jit(solution)/shard_map/ppermute | solution.py:344
  45.5 8.6 %collective-permute-start.4 = (bf16[2,96,384]{2,1,0:T(8,128)(2,1)S(1)}, bf16[2,96,384]{2,1,0:T(8,128)(2,1)S(1)}, u32[]{:S(2)}, u32[]{:S(2)}) collective-permute-start(bf16[2,96,384]{2,1,0:T(8,128)(2,1)S(1)} %edge_rows.3), channel_id=1, source_target_pairs={{0,2},{2,0},{3,5},{5,3},{4,6},{6,4},{7,9},{9,7},{8,10},{10,8},{11,... | collective-permute-start | bytes 442376 | tf_op jit(solution)/shard_map/ppermute | solution.py:353
  54.1 1.4 %collective-permute-start.5 = (bf16[2,96,384]{2,1,0:T(8,128)(2,1)S(1)}, bf16[2,96,384]{2,1,0:T(8,128)(2,1)S(1)}, u32[]{:S(2)}, u32[]{:S(2)}) collective-permute-start(bf16[2,96,384]{2,1,0:T(8,128)(2,1)S(1)} %collective-permute-done.4.mine), channel_id=1, source_target_pairs={{0,1},{1,0},{2,3},{3,2},{4,5},{5,4},{6,7},{7,6},{8,9},{9,8},{10,11... | collective-permute-start | bytes 442376 | tf_op jit(solution)/shard_map/ppermute | solution.py:344
where the time goes:
time: 62.5 us; the launch traced here: 61.7 us
  Pallas kernels  27.6 us (44%)
  waiting for transfers between devices  18.6 us (30%)
  starting transfers between devices  9.78 us (16%)
  local copies, waits for them, and re-layouts  5.64 us (9%)
    ppermute x2, waiting for transfers between devices, edge_exchange(): return lax.ppermute(x, ('band', 'depth'), pairs)  11.6 us
    pallas_call x1, Pallas kernels, first_call(): pl.pallas_call(first_kernel, out_shape=(jax.ShapeDtypeStruct((rows, PADW)...  10.9 us
    pallas_call x1, Pallas kernels, middle_call(): pl.pallas_call(functools.partial(middle_kernel, pix), out_shape=(jax.Shap...  10 us
    ppermute x2, starting transfers between devices, edge_exchange(): return lax.ppermute(x, ('band', 'depth'), pairs)  9.19 us
    ppermute x4, waiting for transfers between devices, swap(): return lax.ppermute(x, 'depth', [(0, 1), (1, 0)])  7.04 us
    pallas_call x1, Pallas kernels, last_call(): pl.pallas_call(functools.partial(last_kernel, pix), out_shape=jax.ShapeDt...  6.21 us
    unnamed x12, local copies, waits for them, and re-layouts  5.64 us
  transfers between devices with their start and end apart: 6, of which 6 were waited for; matrix products, arithmetic and copies ran while one was open for 0% of the time, Pallas kernels for 1%

commit v1 on v0

v1 whole, which is shorter than its diff:
```python
import functools
import jax
import jax.numpy as jnp
from jax import lax
from jax.experimental import pallas as pl
from jax.experimental.pallas import tpu as pltpu
from jax.sharding import PartitionSpec as P

LX = 96
BF = jnp.bfloat16
F32 = jnp.float32
PADW = 384
SPLIT_VMEM = 24 << 20

SMEM = pl.BlockSpec(memory_space=pltpu.SMEM)
VMEM = pl.BlockSpec(memory_space=pltpu.VMEM)
ANY = pl.BlockSpec(memory_space=pl.ANY)


def dot(a, b):
    return lax.dot_general(a, b, (((1,), (0,)), ((), ())), preferred_element_type=F32)


def dot_t(a, b):
    return lax.dot_general(a, b, (((1,), (1,)), ((), ())), preferred_element_type=F32)


def count_of(info, plane):
    return info[1][plane]


def place(info, plane, slot):
    ident = info[0][plane, min(slot, info[0].shape[1] - 1)]
    start = pl.multiple_of((2 - ident // 3) * LX, LX)
    return start, jnp.where(slot < count_of(info, plane), ident % 3, 3)


def by_pairs(info, plane, slots, body):
    pairs = (count_of(info, plane) + 1) // 2
    for k in range(1, slots // 2 + 1):
        pl.when(pairs == k)(functools.partial(body, 2 * k))


def project_slab(info, plane, x, kp, acc):
    rows, vox = x.shape

    def body(used):
        out = dot_t(x[...], kp[plane, 0:used].reshape(used * PADW, vox))
        for s in range(used):
            row, dx = place(info, plane, s)
            acc[dx, pl.ds(row, rows), :] += out[:, s * PADW : (s + 1) * PADW]

    by_pairs(info, plane, kp.shape[1], body)


def back_slab(info, plane, ratios, kp, acc):
    lens, vox = acc.shape

    def body(used):
        left = []
        for s in range(used):
            row, dx = place(info, plane, s)
            left.append(ratios[dx, pl.ds(row, lens), :])
        acc[...] = dot(jnp.concatenate(left, axis=1), kp[plane, 0:used].reshape(used * PADW, vox))

    by_pairs(info, plane, kp.shape[1], body)


def each_plane(planes, body):
    lax.fori_loop(0, planes, lambda z, carry: (body(z), carry)[1], 0)


def column_of(rows, width):
    return lax.rem(lax.broadcasted_iota(jnp.int32, (rows, width), 0), LX)


def fold_dx(acc):
    rows = acc.shape[1]
    col = column_of(rows, PADW)
    left = jnp.where(col > 0, pltpu.roll(acc[0], 1, 0), 0.0)
    right = jnp.where(col < LX - 1, pltpu.roll(acc[2], rows - 1, 0), 0.0)
    return acc[1] + left + right


def split_kernel(psf, kp):
    slots, pix, planes, vox = psf.shape
    even = kp.shape[1]
    full = pix // 16 * 16
    kp[:, :, full:PADW, :] = jnp.zeros((planes, even, PADW - full, vox), BF)
    if slots < even:
        kp[:, slots, 0:full, :] = jnp.zeros((planes, full, vox), BF)
    for s in range(slots):
        both = jnp.swapaxes(psf[s], 0, 1)
        for z in range(planes):
            kp[z, s, 0:pix, :] = both[z]


def split_call(psf):
    planes, slots, pix, vox = psf.shape
    return pl.pallas_call(
        split_kernel,
        out_shape=jax.ShapeDtypeStruct((planes, slots + slots % 2, PADW, vox), BF),
        in_specs=[VMEM],
        out_specs=VMEM,
        compiler_params=pltpu.CompilerParams(vmem_limit_bytes=SPLIT_VMEM),
        cost_estimate=cost(5),
        name="split_planes",
    )(jnp.transpose(psf, (1, 2, 0, 3)))


def first_kernel(ids, counts, est, kp, part_out, est_out, xs, acc):
    acc[0:3] = jnp.zeros((3,) + acc.shape[1:], F32)

    def body(z):
        t = est[z].T
        est_out[z] = t
        xs[...] = t.astype(BF)
        project_slab((ids, counts), z, xs, kp, acc)

    each_plane(est.shape[0], body)
    part_out[...] = fold_dx(acc)


def first_call(estimate, kp, ids, counts):
    planes, vox, lens = estimate.shape
    rows = lens + 2 * LX
    return pl.pallas_call(
        first_kernel,
        out_shape=(
            jax.ShapeDtypeStruct((rows, PADW), F32),
            jax.ShapeDtypeStruct((planes, lens, vox), F32),
        ),
        in_specs=[SMEM, SMEM, VMEM, VMEM],
        out_specs=(VMEM, VMEM),
        scratch_shapes=[
            pltpu.VMEM((lens, vox), BF),
            pltpu.VMEM((4, rows, PADW), F32),
        ],
        compiler_params=pltpu.CompilerParams(vmem_limit_bytes=36 << 20),
        cost_estimate=cost(5),
        name="project_first",
    )(ids, counts, estimate, kp)


def cost(us):
    return pl.CostEstimate(flops=int(us * 1e9), bytes_accessed=int(us * 3e6), transcendentals=0)


def sensor_kernel(meas, bg, out):
    pix = meas.shape[0]
    out[...] = jnp.zeros(out.shape, F32)
    out[0, :, 0:pix] = meas[...].T
    out[1, :, 0:pix] = bg[...].T


def sensor_call(measured, background):
    lens = measured.shape[1]
    return pl.pallas_call(
        sensor_kernel,
        out_shape=jax.ShapeDtypeStruct((2, lens, PADW), F32),
        in_specs=[VMEM, VMEM],
        out_specs=VMEM,
        compiler_params=pltpu.CompilerParams(vmem_limit_bytes=16 << 20),
        cost_estimate=cost(1),
        name="sensor_turn",
    )(measured, background)


def upward():
    return lax.rem(lax.axis_index("band") + lax.axis_index("depth"), 2) == 0


def edge_kernel(own, other, *refs):
    sensor, out = (refs[0], refs[1]) if len(refs) == 2 else (None, refs[0])
    rows = own.shape[0]
    up = upward()
    outer = pl.multiple_of(jnp.where(up, rows - LX, 0), LX)
    inner = pl.multiple_of(jnp.where(up, rows - 2 * LX, LX), LX)
    for i, start in enumerate((outer, inner)):
        out[i] = (own[pl.ds(start, LX), :] + other[pl.ds(start, LX), :]).astype(BF)
    if sensor is not None:
        line = pl.multiple_of(inner - LX, LX)
        for i in range(2):
            out[2 + i] = sensor[i, pl.ds(line, LX), :].astype(BF)


def edge_call(own, other, *sensor):
    return pl.pallas_call(
        edge_kernel,
        out_shape=jax.ShapeDtypeStruct((2 + 2 * len(sensor), LX, PADW), BF),
        in_specs=[VMEM] * (2 + len(sensor)),
        out_specs=VMEM,
        compiler_params=pltpu.CompilerParams(vmem_limit_bytes=16 << 20),
        name="edge_rows",
    )(own, other, *sensor)


def ratio_planes(own, other, mine, theirs, sensor, halo, planes_ref, pix):
    rows = own.shape[0]
    lens = rows - 2 * LX
    band = lax.axis_index("band")
    up = upward()
    upper = [jnp.where(up, mine[i].astype(F32), theirs[i].astype(F32)) for i in range(2)]
    lower = [jnp.where(up, theirs[i].astype(F32), mine[i].astype(F32)) for i in range(2)]
    lane = lax.broadcasted_iota(jnp.int32, (1, PADW), 1) < pix

    def ratio(start, size, extra, measured, background, there):
        total = own[start : start + size, :] + other[start : start + size, :]
        if extra is not None:
            total = total + extra
        keep = lane if there is None else jnp.logical_and(lane, there)
        return jnp.where(keep, measured / (total + background), 0.0).astype(BF).astype(F32)

    parts = [
        ratio(0, LX, lower[1], halo[0], halo[1], band > 0),
        ratio(LX, LX, lower[0], sensor[0, 0:LX], sensor[1, 0:LX], None),
        ratio(2 * LX, lens - 2 * LX, None, sensor[0, LX : lens - LX], sensor[1, LX : lens - LX], None),
        ratio(lens, LX, upper[0], sensor[0, lens - LX : lens], sensor[1, lens - LX : lens], None),
        ratio(lens + LX, LX, upper[1], halo[2], halo[3], band < lax.axis_size("band") - 1),
    ]
    whole = jnp.concatenate(parts, axis=0)
    col = column_of(rows, PADW)
    planes_ref[1] = whole.astype(BF)
    planes_ref[2] = jnp.where(col > 0, pltpu.roll(whole, 1, 0), 0.0).astype(BF)
    planes_ref[0] = jnp.where(col < LX - 1, pltpu.roll(whole, rows - 1, 0), 0.0).astype(BF)
    planes_ref[3] = jnp.zeros((rows, PADW), BF)


def sensitivity_kernel(ids, counts, kp, after, inv_out):
    planes, even, _, vox = kp.shape
    lens = inv_out.shape[1]
    width = even * PADW
    lane = lax.broadcasted_iota(jnp.int32, (16, width), 1)
    slot = lax.broadcasted_iota(jnp.int32, (16, width), 0)
    ones = jnp.where(lane // PADW == slot, 1.0, 0.0).astype(BF)
    lane = lax.broadcasted_iota(jnp.int32, (1, 128), 1)
    slot = lax.rem(lane, 16)
    l = lax.broadcasted_iota(jnp.int32, (lens, 128), 0)
    grid_rows = lens // LX * lax.axis_size("band")
    row = lax.axis_index("band") * (lens // LX) + l // LX
    col = lax.rem(l, LX)

    def body(z):
        sums = dot(ones, kp[z].reshape(width, vox))
        high = sums.astype(BF).astype(F32)
        mid = (sums - high).astype(BF).astype(F32)
        low = sums - high - mid
        right = jnp.concatenate([high, mid, low, jnp.zeros((80, vox), F32)], axis=0).astype(BF)
        dy = jnp.zeros((1, 128), jnp.int32)
        dx = jnp.zeros((1, 128), jnp.int32)
        for s in range(ids.shape[1]):
            dy = jnp.where(slot == s, ids[z, s] // 3 - 1, dy)
            dx = jnp.where(slot == s, ids[z, s] % 3 - 1, dx)
        active = (slot < counts[z]) & (lane < 48)
        r = row - dy
        c = col - dx
        inside = (r >= 0) & (r < grid_rows) & (c >= 0) & (c < LX) & active
        inv_out[z] = 1.0 / dot(jnp.where(inside, 1.0, 0.0).astype(BF), right)

    each_plane(planes, body)


def sensitivity_call(ids, counts, kp, lens, after):
    planes, _, _, vox = kp.shape
    return pl.pallas_call(
        sensitivity_kernel,
        out_shape=jax.ShapeDtypeStruct((planes, lens, vox), F32),
        in_specs=[SMEM, SMEM, VMEM, ANY],
        out_specs=VMEM,
        compiler_params=pltpu.CompilerParams(vmem_limit_bytes=16 << 20),
        cost_estimate=cost(3),
        name="sensitivity",
    )(ids, counts, kp, after)


def middle_kernel(pix, ids, counts, own, other, mine, theirs, sensor, est, inv, kp, part_out, vol_out, halo_out, ratios, xs, back, acc):
    up = upward()
    for i in range(2):
        a = mine[2 + i].astype(F32)
        b = theirs[2 + i].astype(F32)
        halo_out[i] = jnp.where(up, b, a)
        halo_out[2 + i] = jnp.where(up, a, b)
    ratio_planes(own, other, mine, theirs, sensor, halo_out, ratios, pix)
    acc[0:3] = jnp.zeros((3,) + acc.shape[1:], F32)

    def body(z):
        back_slab((ids, counts), z, ratios, kp, back)
        vol = est[z] * back[...] * inv[z]
        vol_out[z] = vol
        xs[...] = vol.astype(BF)
        project_slab((ids, counts), z, xs, kp, acc)

    each_plane(est.shape[0], body)
    part_out[...] = fold_dx(acc)


def middle_call(pix, ids, counts, own, other, mine, theirs, sensor, est, inv, kp):
    planes, lens, vox = est.shape
    rows = own.shape[0]
    return pl.pallas_call(
        functools.partial(middle_kernel, pix),
        out_shape=(
            jax.ShapeDtypeStruct((rows, PADW), F32),
            jax.ShapeDtypeStruct((planes, lens, vox), F32),
            jax.ShapeDtypeStruct((4, LX, PADW), F32),
        ),
        in_specs=[SMEM, SMEM] + [VMEM] * 8,
        out_specs=(VMEM,) * 3,
        scratch_shapes=[
            pltpu.VMEM((4, rows, PADW), BF),
            pltpu.VMEM((lens, vox), BF),
            pltpu.VMEM((lens, vox), F32),
            pltpu.VMEM((4, rows, PADW), F32),
        ],
        compiler_params=pltpu.CompilerParams(vmem_limit_bytes=36 << 20),
        cost_estimate=cost(10),
        name="back_and_project",
    )(ids, counts, own, other, mine, theirs, sensor, est, inv, kp)


def last_kernel(pix, ids, counts, own, other, mine, theirs, sensor, halo, vol, inv, kp, out, ratios, back):
    ratio_planes(own, other, mine, theirs, sensor, halo, ratios, pix)

    def body(z):
        back_slab((ids, counts), z, ratios, kp, back)
        out[z] = (vol[z] * back[...] * inv[z]).T

    each_plane(vol.shape[0], body)


def last_call(pix, ids, counts, own, other, mine, theirs, sensor, halo, vol, inv, kp):
    planes, lens, vox = vol.shape
    rows = own.shape[0]
    return pl.pallas_call(
        functools.partial(last_kernel, pix),
        out_shape=jax.ShapeDtypeStruct((planes, vox, lens), F32),
        in_specs=[SMEM, SMEM] + [VMEM] * 9,
        out_specs=VMEM,
        scratch_shapes=[
            pltpu.VMEM((4, rows, PADW), BF),
            pltpu.VMEM((lens, vox), F32),
        ],
        compiler_params=pltpu.CompilerParams(vmem_limit_bytes=36 << 20),
        cost_estimate=cost(6),
        name="back_last",
    )(ids, counts, own, other, mine, theirs, sensor, halo, vol, inv, kp)


def swap(x):
    return lax.ppermute(x, "depth", [(0, 1), (1, 0)])


def edge_exchange(x):
    bands = lax.axis_size("band")
    pairs = []
    for b in range(bands - 1):
        d = b % 2
        pairs += [(2 * b + d, 2 * b + 2 + d), (2 * b + 2 + d, 2 * b + d)]
    return lax.ppermute(x, ("band", "depth"), pairs)


def per_device(estimate, psf_blocks, offset_ids, block_counts, measured, background):
    pix, lens = measured.shape
    kp = split_call(psf_blocks)
    part, est = first_call(estimate, kp, offset_ids, block_counts)
    other = swap(part)
    sensor = sensor_call(measured, background)
    edges = edge_call(part, other, sensor)
    mine = edge_exchange(edges)
    inv = sensitivity_call(offset_ids, block_counts, kp, lens, edges)
    mine, inv = lax.optimization_barrier((mine, inv))
    theirs = swap(mine)
    part, vol, halo = middle_call(pix, offset_ids, block_counts, part, other, mine, theirs, sensor, est, inv, kp)
    other = swap(part)
    mine = edge_exchange(edge_call(part, other))
    theirs = swap(mine)
    return last_call(pix, offset_ids, block_counts, part, other, mine, theirs, sensor, halo, vol, inv, kp)


def solution(mesh):
    in_specs = (
        P("depth", "parts", "band"),
        P("depth", None, None, None),
        P("depth", None),
        P("depth"),
        P("parts", "band"),
        P("parts", "band"),
    )
    return jax.shard_map(
        per_device, mesh=mesh, in_specs=in_specs, out_specs=P("depth", "parts", "band"), check_vma=False
    )
```

time: 62.5 us -> 51.6 us (0.83)
  the two profiles are of different devices: /device:TPU:0 before, /device:TPU:25 now
where the time goes in v1:
time: 51.6 us; the launch traced here: 50.8 us
  Pallas kernels  22.7 us (44%)
  waiting for transfers between devices  13.1 us (25%)
  starting transfers between devices  11.9 us (23%)
  local copies, waits for them, and re-layouts  2.91 us (6%)
    pallas_call x1, Pallas kernels, middle_call(): pl.pallas_call(functools.partial(middle_kernel, pix), out_shape=(jax.Shap...  7.69 us
    ppermute x4, waiting for transfers between devices, swap(): return lax.ppermute(x, 'depth', [(0, 1), (1, 0)])  6.65 us
    ppermute x2, starting transfers between devices, edge_exchange(): return lax.ppermute(x, ('band', 'depth'), pairs)  6.47 us
    ppermute x2, waiting for transfers between devices, edge_exchange(): return lax.ppermute(x, ('band', 'depth'), pairs)  6.46 us
    ppermute x4, starting transfers between devices, swap(): return lax.ppermute(x, 'depth', [(0, 1), (1, 0)])  5.44 us
    pallas_call x1, Pallas kernels, last_call(): pl.pallas_call(functools.partial(last_kernel, pix), out_shape=jax.ShapeDt...  5.36 us
    pallas_call x1, Pallas kernels, first_call(): pl.pallas_call(first_kernel, out_shape=(jax.ShapeDtypeStruct((rows, PADW)...  4.38 us
    unnamed x12, local copies, waits for them, and re-layouts  2.91 us
  transfers between devices with their start and end apart: 6, of which 6 were waited for; matrix products, arithmetic and copies ran while one was open for 0% of the time, Pallas kernels for 5%

profile of v1, /device:TPU:25, one launch (start us, length us, event | category | flops | bytes accessed | tf_op | source)
XLA Modules:
  0.0 50.8 jit_solution(12186111258588604922)
XLA Ops:
  0.0 0.0 copy-start
  0.0 2.9 %copy-done = bf16[2,9,361,512]{3,0,2,1:T(2,128)(2,1)S(1)} copy-done((bf16[2,9,361,512]{3,0,2,1:T(2,128)(2,1)S(1)}, bf16[2,9,361,512]{3,0,2,1:T(2,128)(2,1)}, u32[]{:S(2)}) %copy-start) | copy-done | bytes 6653976
  2.9 0.0 copy-start.1
  2.9 0.0 copy-start.4
  2.9 0.0 copy-start.5
  2.9 2.4 %split_planes.1.kp = bf16[2,10,384,512]{3,2,1,0:T(8,128)(2,1)S(1)} custom-call(bf16[9,361,2,512]{3,2,1,0:T(2,128)(2,1)S(1)} %bitcast.1), custom_call_target="tpu_custom_call" | custom-call | flops 5000000000 | bytes 15000000 | tf_op jit(solution)/shard_map/split_planes/pallas_call | solution.py:100
  5.3 0.0 copy-done.1
  5.3 0.0 copy-done.4
  5.3 0.0 copy-done.5
  5.3 0.0 copy-start.2
  5.4 0.0 copy-start.3
  5.4 4.4 %project_first.1 = (f32[576,384]{1,0:T(8,128)S(1)}, f32[2,384,512]{2,1,0:T(8,128)S(1)}) custom-call(s32[2,9]{1,0:T(2,128)S(1)} %copy-done.4, s32[2]{0:T(128)S(1)} %copy-done.5, f32[2,512,384]{2,1,0:T(8,128)S(1)} %copy-done.1, bf16[2,10,384,512]{3,2,1,0:T(8,128)(2,1)S(1)} %split_planes.1.kp), custom_call_target="tpu_custom_call" | custom-call | flops 5000000000 | bytes 15000000 | tf_op jit(solution)/shard_map/project_first/pallas_call | solution.py:127
  9.8 0.1 collective-permute-start
  9.8 0.0 copy-done.2
  9.8 0.0 copy-done.3
  9.9 0.4 sensor_turn.1.refs_0_.sensor
  10.2 2.0 %collective-permute-done.other = f32[576,384]{1,0:T(8,128)S(1)} collective-permute-done((f32[576,384]{1,0:T(8,128)S(1)}, f32[576,384]{1,0:T(8,128)S(1)}, u32[]{:S(2)}, u32[]{:S(2)}) %collective-permute-start) | collective-permute-done | bytes 884768 | tf_op jit(solution)/shard_map/ppermute | solution.py:350
  12.3 3.2 %collective-permute-start.1 = (bf16[4,96,384]{2,1,0:T(8,128)(2,1)S(1)}, bf16[4,96,384]{2,1,0:T(8,128)(2,1)S(1)}, u32[]{:S(2)}, u32[]{:S(2)}) collective-permute-start(bf16[4,96,384]{2,1,0:T(8,128)(2,1)S(1)} %edge_rows.2.after), channel_id=1, source_target_pairs={{0,2},{2,0},{3,5},{5,3},{4,6},{6,4},{7,9},{9,7},{8,10},{10,8},{11,... | collective-permute-start | bytes 884744 | tf_op jit(solution)/shard_map/ppermute | solution.py:359
  15.5 2.4 %sensitivity.1.inv = f32[2,384,512]{2,1,0:T(8,128)S(1)} custom-call(s32[2,9]{1,0:T(2,128)S(1)} %copy-done.4, s32[2]{0:T(128)S(1)} %copy-done.5, bf16[2,10,384,512]{3,2,1,0:T(8,128)(2,1)S(1)} %split_planes.1.kp, bf16[4,96,384]{2,1,0:T(8,128)(2,1)S(1)} %edge_rows.2.after), custom_call_target="tpu_custom_call" | custom-call | flops 3000000000 | bytes 9000000 | tf_op jit(solution)/shard_map/sensitivity/pallas_call | solution.py:265
  17.9 2.8 %collective-permute-done.1.mine = bf16[4,96,384]{2,1,0:T(8,128)(2,1)S(1)} collective-permute-done((bf16[4,96,384]{2,1,0:T(8,128)(2,1)S(1)}, bf16[4,96,384]{2,1,0:T(8,128)(2,1)S(1)}, u32[]{:S(2)}, u32[]{:S(2)}) %collective-permute-start.1) | collective-permute-done | bytes 294944 | tf_op jit(solution)/shard_map/ppermute | solution.py:359
  20.8 3.4 %collective-permute-start.2 = (bf16[4,96,384]{2,1,0:T(8,128)(2,1)S(1)}, bf16[4,96,384]{2,1,0:T(8,128)(2,1)S(1)}, u32[]{:S(2)}, u32[]{:S(2)}) collective-permute-start(bf16[4,96,384]{2,1,0:T(8,128)(2,1)S(1)} %collective-permute-done.1.mine), channel_id=1, source_target_pairs={{0,1},{1,0},{2,3},{3,2},{4,5},{5,4},{6,7},{7,6},{8,9},{9,8},{10,11... | collective-permute-start | bytes 884744 | tf_op jit(solution)/shard_map/ppermute | solution.py:350
  24.2 1.2 %collective-permute-done.2.theirs = bf16[4,96,384]{2,1,0:T(8,128)(2,1)S(1)} collective-permute-done((bf16[4,96,384]{2,1,0:T(8,128)(2,1)S(1)}, bf16[4,96,384]{2,1,0:T(8,128)(2,1)S(1)}, u32[]{:S(2)}, u32[]{:S(2)}) %collective-permute-start.2) | collective-permute-done | bytes 294944 | tf_op jit(solution)/shard_map/ppermute | solution.py:350
  25.4 7.7 %back_and_project.1 = (f32[576,384]{1,0:T(8,128)S(1)}, f32[2,384,512]{2,1,0:T(8,128)S(1)}, f32[4,96,384]{2,1,0:T(8,128)S(1)}) custom-call(s32[2,9]{1,0:T(2,128)S(1)} %copy-done.4, s32[2]{0:T(128)S(1)} %copy-done.5, f32[576,384]{1,0:T(8,128)S(1)} %get-tuple-element.12.own, f32[576,384]{1,0:T(8,128)S(1)} %collective-permute-done.other, ...), custom_call_target="tpu_custom_call" | custom-call | flops 10000000000 | bytes 30000000 | tf_op jit(solution)/shard_map/back_and_project/pallas_call | solution.py:300
  33.1 0.1 collective-permute-start.3
  33.2 2.4 %collective-permute-done.3.other = f32[576,384]{1,0:T(8,128)S(1)} collective-permute-done((f32[576,384]{1,0:T(8,128)S(1)}, f32[576,384]{1,0:T(8,128)S(1)}, u32[]{:S(2)}, u32[]{:S(2)}) %collective-permute-start.3) | collective-permute-done | bytes 884768 | tf_op jit(solution)/shard_map/ppermute | solution.py:350
  35.6 3.3 %collective-permute-start.4 = (bf16[2,96,384]{2,1,0:T(8,128)(2,1)S(1)}, bf16[2,96,384]{2,1,0:T(8,128)(2,1)S(1)}, u32[]{:S(2)}, u32[]{:S(2)}) collective-permute-start(bf16[2,96,384]{2,1,0:T(8,128)(2,1)S(1)} %edge_rows.3), channel_id=1, source_target_pairs={{0,2},{2,0},{3,5},{5,3},{4,6},{6,4},{7,9},{9,7},{8,10},{10,8},{11,... | collective-permute-start | bytes 442376 | tf_op jit(solution)/shard_map/ppermute | solution.py:359
  38.9 3.6 %collective-permute-done.4.mine = bf16[2,96,384]{2,1,0:T(8,128)(2,1)S(1)} collective-permute-done((bf16[2,96,384]{2,1,0:T(8,128)(2,1)S(1)}, bf16[2,96,384]{2,1,0:T(8,128)(2,1)S(1)}, u32[]{:S(2)}, u32[]{:S(2)}) %collective-permute-start.4) | collective-permute-done | bytes 147488 | tf_op jit(solution)/shard_map/ppermute | solution.py:359
  42.5 1.9 %collective-permute-start.5 = (bf16[2,96,384]{2,1,0:T(8,128)(2,1)S(1)}, bf16[2,96,384]{2,1,0:T(8,128)(2,1)S(1)}, u32[]{:S(2)}, u32[]{:S(2)}) collective-permute-start(bf16[2,96,384]{2,1,0:T(8,128)(2,1)S(1)} %collective-permute-done.4.mine), channel_id=1, source_target_pairs={{0,1},{1,0},{2,3},{3,2},{4,5},{5,4},{6,7},{7,6},{8,9},{9,8},{10,11... | collective-permute-start | bytes 442376 | tf_op jit(solution)/shard_map/ppermute | solution.py:350
  44.4 1.0 %collective-permute-done.5.theirs = bf16[2,96,384]{2,1,0:T(8,128)(2,1)S(1)} collective-permute-done((bf16[2,96,384]{2,1,0:T(8,128)(2,1)S(1)}, bf16[2,96,384]{2,1,0:T(8,128)(2,1)S(1)}, u32[]{:S(2)}, u32[]{:S(2)}) %collective-permute-start.5) | collective-permute-done | bytes 147488 | tf_op jit(solution)/shard_map/ppermute | solution.py:350
  45.4 5.4 %back_last.1 = f32[2,512,384]{2,1,0:T(8,128)} custom-call(s32[2,9]{1,0:T(2,128)S(1)} %copy-done.4, s32[2]{0:T(128)S(1)} %copy-done.5, f32[576,384]{1,0:T(8,128)S(1)} %get-tuple-element.16.own, f32[576,384]{1,0:T(8,128)S(1)} %collective-permute-done.3.other, bf16[2,96,384]{2,1,0:T(8,128)(2,1)S(1)} %collective-permute-done.4.mine, ...), custom_call_target="tpu_custom_call" | custom-call | flops 6000000000 | bytes 18000000 | tf_op jit(solution)/shard_map/back_last/pallas_call | solution.py:334
  (2 shorter events, 0.1 us)
Async XLA Ops:
  0.0 2.9 %copy-start = (bf16[2,9,361,512]{3,0,2,1:T(2,128)(2,1)S(1)}, bf16[2,9,361,512]{3,0,2,1:T(2,128)(2,1)}, u32[]{:S(2)}) copy-start(bf16[2,9,361,512]{3,0,2,1:T(2,128)(2,1)} %param.7) | copy-start | bytes 19961860
  2.9 2.4 %copy-start.1 = (f32[2,512,384]{2,1,0:T(8,128)S(1)}, f32[2,512,384]{2,1,0:T(8,128)}, u32[]{:S(2)}) copy-start(f32[2,512,384]{2,1,0:T(8,128)} %est.1) | copy-start | bytes 4718596
  2.9 2.4 %copy-start.4 = (s32[2,9]{1,0:T(2,128)S(1)}, s32[2,9]{1,0:T(2,128)}, u32[]{:S(2)}) copy-start(s32[2,9]{1,0:T(2,128)} %ids.7) | copy-start | bytes 220
  2.9 2.4 %copy-start.5 = (s32[2]{0:T(128)S(1)}, s32[2]{0:T(128)}, u32[]{:S(2)}) copy-start(s32[2]{0:T(128)} %counts.7) | copy-start | bytes 28
  5.3 4.5 %copy-start.2 = (f32[361,384]{1,0:T(8,128)S(1)}, f32[361,384]{1,0:T(8,128)}, u32[]{:S(2)}) copy-start(f32[361,384]{1,0:T(8,128)} %meas.1) | copy-start | bytes 1663492
  5.4 4.5 %copy-start.3 = (f32[361,384]{1,0:T(8,128)S(1)}, f32[361,384]{1,0:T(8,128)}, u32[]{:S(2)}) copy-start(f32[361,384]{1,0:T(8,128)} %bg.1) | copy-start | bytes 1663492
  9.8 2.5 %collective-permute-start = (f32[576,384]{1,0:T(8,128)S(1)}, f32[576,384]{1,0:T(8,128)S(1)}, u32[]{:S(2)}, u32[]{:S(2)}) collective-permute-start(f32[576,384]{1,0:T(8,128)S(1)} %get-tuple-element.12.own), channel_id=1, source_target_pairs={{0,1},{1,0},{2,3},{3,2},{4,5},{5,4},{6,7},{7,6},{8,9},{9,8},{10,11... | collective-permute-start | bytes 2654216 | tf_op jit(solution)/shard_map/ppermute | solution.py:350
  12.3 8.5 %collective-permute-start.1 = (bf16[4,96,384]{2,1,0:T(8,128)(2,1)S(1)}, bf16[4,96,384]{2,1,0:T(8,128)(2,1)S(1)}, u32[]{:S(2)}, u32[]{:S(2)}) collective-permute-start(bf16[4,96,384]{2,1,0:T(8,128)(2,1)S(1)} %edge_rows.2.after), channel_id=1, source_target_pairs={{0,2},{2,0},{3,5},{5,3},{4,6},{6,4},{7,9},{9,7},{8,10},{10,8},{11,... | collective-permute-start | bytes 884744 | tf_op jit(solution)/shard_map/ppermute | solution.py:359
  20.8 4.6 %collective-permute-start.2 = (bf16[4,96,384]{2,1,0:T(8,128)(2,1)S(1)}, bf16[4,96,384]{2,1,0:T(8,128)(2,1)S(1)}, u32[]{:S(2)}, u32[]{:S(2)}) collective-permute-start(bf16[4,96,384]{2,1,0:T(8,128)(2,1)S(1)} %collective-permute-done.1.mine), channel_id=1, source_target_pairs={{0,1},{1,0},{2,3},{3,2},{4,5},{5,4},{6,7},{7,6},{8,9},{9,8},{10,11... | collective-permute-start | bytes 884744 | tf_op jit(solution)/shard_map/ppermute | solution.py:350
  33.1 2.5 %collective-permute-start.3 = (f32[576,384]{1,0:T(8,128)S(1)}, f32[576,384]{1,0:T(8,128)S(1)}, u32[]{:S(2)}, u32[]{:S(2)}) collective-permute-start(f32[576,384]{1,0:T(8,128)S(1)} %get-tuple-element.16.own), channel_id=1, source_target_pairs={{0,1},{1,0},{2,3},{3,2},{4,5},{5,4},{6,7},{7,6},{8,9},{9,8},{10,11... | collective-permute-start | bytes 2654216 | tf_op jit(solution)/shard_map/ppermute | solution.py:350
  35.6 6.9 %collective-permute-start.4 = (bf16[2,96,384]{2,1,0:T(8,128)(2,1)S(1)}, bf16[2,96,384]{2,1,0:T(8,128)(2,1)S(1)}, u32[]{:S(2)}, u32[]{:S(2)}) collective-permute-start(bf16[2,96,384]{2,1,0:T(8,128)(2,1)S(1)} %edge_rows.3), channel_id=1, source_target_pairs={{0,2},{2,0},{3,5},{5,3},{4,6},{6,4},{7,9},{9,7},{8,10},{10,8},{11,... | collective-permute-start | bytes 442376 | tf_op jit(solution)/shard_map/ppermute | solution.py:359
  42.5 2.9 %collective-permute-start.5 = (bf16[2,96,384]{2,1,0:T(8,128)(2,1)S(1)}, bf16[2,96,384]{2,1,0:T(8,128)(2,1)S(1)}, u32[]{:S(2)}, u32[]{:S(2)}) collective-permute-start(bf16[2,96,384]{2,1,0:T(8,128)(2,1)S(1)} %collective-permute-done.4.mine), channel_id=1, source_target_pairs={{0,1},{1,0},{2,3},{3,2},{4,5},{5,4},{6,7},{7,6},{8,9},{9,8},{10,11... | collective-permute-start | bytes 442376 | tf_op jit(solution)/shard_map/ppermute | solution.py:350

commit v2 on v1

--- a/solution.py
+++ b/solution.py
@@ -202,6 +202,8 @@
     up = upward()
     upper = [jnp.where(up, mine[i].astype(F32), theirs[i].astype(F32)) for i in range(2)]
     lower = [jnp.where(up, theirs[i].astype(F32), mine[i].astype(F32)) for i in range(2)]
+    below = band > 0
+    above = band < lax.axis_size("band") - 1
     lane = lax.broadcasted_iota(jnp.int32, (1, PADW), 1) < pix
 
     def ratio(start, size, extra, measured, background, there):
@@ -212,11 +214,11 @@
         return jnp.where(keep, measured / (total + background), 0.0).astype(BF).astype(F32)
 
     parts = [
-        ratio(0, LX, lower[1], halo[0], halo[1], band > 0),
-        ratio(LX, LX, lower[0], sensor[0, 0:LX], sensor[1, 0:LX], None),
+        ratio(0, LX, lower[1], halo[0], halo[1], below),
+        ratio(LX, LX, jnp.where(below, lower[0], 0.0), sensor[0, 0:LX], sensor[1, 0:LX], None),
         ratio(2 * LX, lens - 2 * LX, None, sensor[0, LX : lens - LX], sensor[1, LX : lens - LX], None),
-        ratio(lens, LX, upper[0], sensor[0, lens - LX : lens], sensor[1, lens - LX : lens], None),
-        ratio(lens + LX, LX, upper[1], halo[2], halo[3], band < lax.axis_size("band") - 1),
+        ratio(lens, LX, jnp.where(above, upper[0], 0.0), sensor[0, lens - LX : lens], sensor[1, lens - LX : lens], None),
+        ratio(lens + LX, LX, upper[1], halo[2], halo[3], above),
     ]
     whole = jnp.concatenate(parts, axis=0)
     col = column_of(rows, PADW)
@@ -351,12 +353,16 @@
 
 
 def edge_exchange(x):
-    bands = lax.axis_size("band")
+    parts, bands, depth = (lax.axis_size(a) for a in ("parts", "band", "depth"))
     pairs = []
-    for b in range(bands - 1):
-        d = b % 2
-        pairs += [(2 * b + d, 2 * b + 2 + d), (2 * b + 2 + d, 2 * b + d)]
-    return lax.ppermute(x, ("band", "depth"), pairs)
+    for p in range(parts):
+        for b in range(bands):
+            for d in range(depth):
+                q, c = p, b + (1 if (b + d) % 2 == 0 else -1)
+                if c < 0 or c == bands:
+                    q, c = min(p ^ 1, parts - 1), b
+                pairs.append(((p * bands + b) * depth + d, (q * bands + c) * depth + d))
+    return lax.ppermute(x, ("parts", "band", "depth"), pairs)
 
 
 def per_device(estimate, psf_blocks, offset_ids, block_counts, measured, background):

time: 51.6 us -> 48.7 us (0.944); the launches traced: 50.8 us -> 48.6 us
  starting transfers between devices: 11.9 us -> 7.79 us
  Pallas kernels: 22.7 us -> 24.2 us
    ppermute x2, starting transfers between devices: 6.47 us -> 2.35 us  [edge_exchange(): return lax.ppermute(x, ('parts', 'band', 'depth'), pairs)]
    pallas_call x1, Pallas kernels: 7.69 us -> 8.49 us  [middle_call(): pl.pallas_call(functools.partial(middle_kernel, pix), out_shape=(jax.Shap...]
  transfers between devices with their start and end apart: 6 -> 6, of which waited for: 6 -> 6; matrix products, arithmetic and copies ran while one was open for 0% -> 0% of each run, Pallas kernels for 5% -> 6%
where the time goes in v2:
time: 48.7 us; the launch traced here: 48.6 us
  Pallas kernels  24.2 us (50%)
  waiting for transfers between devices  13.6 us (28%)
  starting transfers between devices  7.79 us (16%)
  local copies, waits for them, and re-layouts  2.91 us (6%)
    pallas_call x1, Pallas kernels, middle_call(): pl.pallas_call(functools.partial(middle_kernel, pix), out_shape=(jax.Shap...  8.49 us
    ppermute x2, waiting for transfers between devices, edge_exchange(): return lax.ppermute(x, ('parts', 'band', 'depth'), pairs)  6.94 us
    ppermute x4, waiting for transfers between devices, swap(): return lax.ppermute(x, 'depth', [(0, 1), (1, 0)])  6.65 us
    pallas_call x1, Pallas kernels, last_call(): pl.pallas_call(functools.partial(last_kernel, pix), out_shape=jax.ShapeDt...  5.67 us
    ppermute x4, starting transfers between devices, swap(): return lax.ppermute(x, 'depth', [(0, 1), (1, 0)])  5.44 us
    pallas_call x1, Pallas kernels, first_call(): pl.pallas_call(first_kernel, out_shape=(jax.ShapeDtypeStruct((rows, PADW)...  4.73 us
    unnamed x12, local copies, waits for them, and re-layouts  2.91 us
    pallas_call x1, Pallas kernels, sensitivity_call(): pl.pallas_call(sensitivity_kernel, out_shape=jax.ShapeDtypeStruct((planes...  2.41 us
  transfers between devices with their start and end apart: 6, of which 6 were waited for; matrix products, arithmetic and copies ran while one was open for 0% of the time, Pallas kernels for 6%

profile of v2, /device:TPU:25, one launch (start us, length us, event | category | flops | bytes accessed | tf_op | source)
XLA Modules:
  0.0 48.6 jit_solution(10068569929950197875)
XLA Ops:
  0.0 0.0 copy-start
  0.0 2.9 %copy-done = bf16[2,9,361,512]{3,0,2,1:T(2,128)(2,1)S(1)} copy-done((bf16[2,9,361,512]{3,0,2,1:T(2,128)(2,1)S(1)}, bf16[2,9,361,512]{3,0,2,1:T(2,128)(2,1)}, u32[]{:S(2)}) %copy-start) | copy-done | bytes 6653976
  2.9 0.0 copy-start.1
  2.9 0.0 copy-start.4
  2.9 0.0 copy-start.5
  2.9 2.4 %split_planes.1.kp = bf16[2,10,384,512]{3,2,1,0:T(8,128)(2,1)S(1)} custom-call(bf16[9,361,2,512]{3,2,1,0:T(2,128)(2,1)S(1)} %bitcast.1), custom_call_target="tpu_custom_call" | custom-call | flops 5000000000 | bytes 15000000 | tf_op jit(solution)/shard_map/split_planes/pallas_call | solution.py:100
  5.3 0.0 copy-done.1
  5.3 0.0 copy-done.4
  5.3 0.0 copy-done.5
  5.3 0.0 copy-start.2
  5.4 0.0 copy-start.3
  5.4 4.7 %project_first.1 = (f32[576,384]{1,0:T(8,128)S(1)}, f32[2,384,512]{2,1,0:T(8,128)S(1)}) custom-call(s32[2,9]{1,0:T(2,128)S(1)} %copy-done.4, s32[2]{0:T(128)S(1)} %copy-done.5, f32[2,512,384]{2,1,0:T(8,128)S(1)} %copy-done.1, bf16[2,10,384,512]{3,2,1,0:T(8,128)(2,1)S(1)} %split_planes.1.kp), custom_call_target="tpu_custom_call" | custom-call | flops 5000000000 | bytes 15000000 | tf_op jit(solution)/shard_map/project_first/pallas_call | solution.py:127
  10.1 0.1 collective-permute-start
  10.2 0.0 copy-done.2
  10.2 0.0 copy-done.3
  10.2 0.4 sensor_turn.1.refs_0_.sensor
  10.6 2.0 %collective-permute-done.other = f32[576,384]{1,0:T(8,128)S(1)} collective-permute-done((f32[576,384]{1,0:T(8,128)S(1)}, f32[576,384]{1,0:T(8,128)S(1)}, u32[]{:S(2)}, u32[]{:S(2)}) %collective-permute-start) | collective-permute-done | bytes 884768 | tf_op jit(solution)/shard_map/ppermute | solution.py:352
  12.6 1.2 %collective-permute-start.1 = (bf16[4,96,384]{2,1,0:T(8,128)(2,1)S(1)}, bf16[4,96,384]{2,1,0:T(8,128)(2,1)S(1)}, u32[]{:S(2)}, u32[]{:S(2)}) collective-permute-start(bf16[4,96,384]{2,1,0:T(8,128)(2,1)S(1)} %edge_rows.2.after), channel_id=1, source_target_pairs={{0,2},{1,17},{2,0},{3,5},{4,6},{5,3},{6,4},{7,9},{8,10},{9,7},{10,... | collective-permute-start | bytes 884744 | tf_op jit(solution)/shard_map/ppermute | solution.py:365
  13.8 2.4 %sensitivity.1.inv = f32[2,384,512]{2,1,0:T(8,128)S(1)} custom-call(s32[2,9]{1,0:T(2,128)S(1)} %copy-done.4, s32[2]{0:T(128)S(1)} %copy-done.5, bf16[2,10,384,512]{3,2,1,0:T(8,128)(2,1)S(1)} %split_planes.1.kp, bf16[4,96,384]{2,1,0:T(8,128)(2,1)S(1)} %edge_rows.2.after), custom_call_target="tpu_custom_call" | custom-call | flops 3000000000 | bytes 9000000 | tf_op jit(solution)/shard_map/sensitivity/pallas_call | solution.py:267
  16.2 3.0 %collective-permute-done.1.mine = bf16[4,96,384]{2,1,0:T(8,128)(2,1)S(1)} collective-permute-done((bf16[4,96,384]{2,1,0:T(8,128)(2,1)S(1)}, bf16[4,96,384]{2,1,0:T(8,128)(2,1)S(1)}, u32[]{:S(2)}, u32[]{:S(2)}) %collective-permute-start.1) | collective-permute-done | bytes 294944 | tf_op jit(solution)/shard_map/ppermute | solution.py:365
  19.3 3.4 %collective-permute-start.2 = (bf16[4,96,384]{2,1,0:T(8,128)(2,1)S(1)}, bf16[4,96,384]{2,1,0:T(8,128)(2,1)S(1)}, u32[]{:S(2)}, u32[]{:S(2)}) collective-permute-start(bf16[4,96,384]{2,1,0:T(8,128)(2,1)S(1)} %collective-permute-done.1.mine), channel_id=1, source_target_pairs={{0,1},{1,0},{2,3},{3,2},{4,5},{5,4},{6,7},{7,6},{8,9},{9,8},{10,11... | collective-permute-start | bytes 884744 | tf_op jit(solution)/shard_map/ppermute | solution.py:352
  22.7 1.2 %collective-permute-done.2.theirs = bf16[4,96,384]{2,1,0:T(8,128)(2,1)S(1)} collective-permute-done((bf16[4,96,384]{2,1,0:T(8,128)(2,1)S(1)}, bf16[4,96,384]{2,1,0:T(8,128)(2,1)S(1)}, u32[]{:S(2)}, u32[]{:S(2)}) %collective-permute-start.2) | collective-permute-done | bytes 294944 | tf_op jit(solution)/shard_map/ppermute | solution.py:352
  23.9 8.5 %back_and_project.1 = (f32[576,384]{1,0:T(8,128)S(1)}, f32[2,384,512]{2,1,0:T(8,128)S(1)}, f32[4,96,384]{2,1,0:T(8,128)S(1)}) custom-call(s32[2,9]{1,0:T(2,128)S(1)} %copy-done.4, s32[2]{0:T(128)S(1)} %copy-done.5, f32[576,384]{1,0:T(8,128)S(1)} %get-tuple-element.12.own, f32[576,384]{1,0:T(8,128)S(1)} %collective-permute-done.other, ...), custom_call_target="tpu_custom_call" | custom-call | flops 10000000000 | bytes 30000000 | tf_op jit(solution)/shard_map/back_and_project/pallas_call | solution.py:302
  32.4 0.1 collective-permute-start.3
  32.5 2.4 %collective-permute-done.3.other = f32[576,384]{1,0:T(8,128)S(1)} collective-permute-done((f32[576,384]{1,0:T(8,128)S(1)}, f32[576,384]{1,0:T(8,128)S(1)}, u32[]{:S(2)}, u32[]{:S(2)}) %collective-permute-start.3) | collective-permute-done | bytes 884768 | tf_op jit(solution)/shard_map/ppermute | solution.py:352
  35.0 1.2 %collective-permute-start.4 = (bf16[2,96,384]{2,1,0:T(8,128)(2,1)S(1)}, bf16[2,96,384]{2,1,0:T(8,128)(2,1)S(1)}, u32[]{:S(2)}, u32[]{:S(2)}) collective-permute-start(bf16[2,96,384]{2,1,0:T(8,128)(2,1)S(1)} %edge_rows.3), channel_id=1, source_target_pairs={{0,2},{1,17},{2,0},{3,5},{4,6},{5,3},{6,4},{7,9},{8,10},{9,7},{10,... | collective-permute-start | bytes 442376 | tf_op jit(solution)/shard_map/ppermute | solution.py:365
  36.1 3.9 %collective-permute-done.4.mine = bf16[2,96,384]{2,1,0:T(8,128)(2,1)S(1)} collective-permute-done((bf16[2,96,384]{2,1,0:T(8,128)(2,1)S(1)}, bf16[2,96,384]{2,1,0:T(8,128)(2,1)S(1)}, u32[]{:S(2)}, u32[]{:S(2)}) %collective-permute-start.4) | collective-permute-done | bytes 147488 | tf_op jit(solution)/shard_map/ppermute | solution.py:365
  40.0 1.9 %collective-permute-start.5 = (bf16[2,96,384]{2,1,0:T(8,128)(2,1)S(1)}, bf16[2,96,384]{2,1,0:T(8,128)(2,1)S(1)}, u32[]{:S(2)}, u32[]{:S(2)}) collective-permute-start(bf16[2,96,384]{2,1,0:T(8,128)(2,1)S(1)} %collective-permute-done.4.mine), channel_id=1, source_target_pairs={{0,1},{1,0},{2,3},{3,2},{4,5},{5,4},{6,7},{7,6},{8,9},{9,8},{10,11... | collective-permute-start | bytes 442376 | tf_op jit(solution)/shard_map/ppermute | solution.py:352
  41.9 1.0 %collective-permute-done.5.theirs = bf16[2,96,384]{2,1,0:T(8,128)(2,1)S(1)} collective-permute-done((bf16[2,96,384]{2,1,0:T(8,128)(2,1)S(1)}, bf16[2,96,384]{2,1,0:T(8,128)(2,1)S(1)}, u32[]{:S(2)}, u32[]{:S(2)}) %collective-permute-start.5) | collective-permute-done | bytes 147488 | tf_op jit(solution)/shard_map/ppermute | solution.py:352
  42.9 5.7 %back_last.1 = f32[2,512,384]{2,1,0:T(8,128)} custom-call(s32[2,9]{1,0:T(2,128)S(1)} %copy-done.4, s32[2]{0:T(128)S(1)} %copy-done.5, f32[576,384]{1,0:T(8,128)S(1)} %get-tuple-element.16.own, f32[576,384]{1,0:T(8,128)S(1)} %collective-permute-done.3.other, bf16[2,96,384]{2,1,0:T(8,128)(2,1)S(1)} %collective-permute-done.4.mine, ...), custom_call_target="tpu_custom_call" | custom-call | flops 6000000000 | bytes 18000000 | tf_op jit(solution)/shard_map/back_last/pallas_call | solution.py:336
  (2 shorter events, 0.1 us)
Async XLA Ops:
  0.0 2.9 %copy-start = (bf16[2,9,361,512]{3,0,2,1:T(2,128)(2,1)S(1)}, bf16[2,9,361,512]{3,0,2,1:T(2,128)(2,1)}, u32[]{:S(2)}) copy-start(bf16[2,9,361,512]{3,0,2,1:T(2,128)(2,1)} %param.7) | copy-start | bytes 19961860
  2.9 2.4 %copy-start.1 = (f32[2,512,384]{2,1,0:T(8,128)S(1)}, f32[2,512,384]{2,1,0:T(8,128)}, u32[]{:S(2)}) copy-start(f32[2,512,384]{2,1,0:T(8,128)} %est.1) | copy-start | bytes 4718596
  2.9 2.4 %copy-start.4 = (s32[2,9]{1,0:T(2,128)S(1)}, s32[2,9]{1,0:T(2,128)}, u32[]{:S(2)}) copy-start(s32[2,9]{1,0:T(2,128)} %ids.7) | copy-start | bytes 220
  2.9 2.4 %copy-start.5 = (s32[2]{0:T(128)S(1)}, s32[2]{0:T(128)}, u32[]{:S(2)}) copy-start(s32[2]{0:T(128)} %counts.7) | copy-start | bytes 28
  5.3 4.8 %copy-start.2 = (f32[361,384]{1,0:T(8,128)S(1)}, f32[361,384]{1,0:T(8,128)}, u32[]{:S(2)}) copy-start(f32[361,384]{1,0:T(8,128)} %meas.1) | copy-start | bytes 1663492
  5.4 4.8 %copy-start.3 = (f32[361,384]{1,0:T(8,128)S(1)}, f32[361,384]{1,0:T(8,128)}, u32[]{:S(2)}) copy-start(f32[361,384]{1,0:T(8,128)} %bg.1) | copy-start | bytes 1663492
  10.1 2.5 %collective-permute-start = (f32[576,384]{1,0:T(8,128)S(1)}, f32[576,384]{1,0:T(8,128)S(1)}, u32[]{:S(2)}, u32[]{:S(2)}) collective-permute-start(f32[576,384]{1,0:T(8,128)S(1)} %get-tuple-element.12.own), channel_id=1, source_target_pairs={{0,1},{1,0},{2,3},{3,2},{4,5},{5,4},{6,7},{7,6},{8,9},{9,8},{10,11... | collective-permute-start | bytes 2654216 | tf_op jit(solution)/shard_map/ppermute | solution.py:352
  12.6 6.6 %collective-permute-start.1 = (bf16[4,96,384]{2,1,0:T(8,128)(2,1)S(1)}, bf16[4,96,384]{2,1,0:T(8,128)(2,1)S(1)}, u32[]{:S(2)}, u32[]{:S(2)}) collective-permute-start(bf16[4,96,384]{2,1,0:T(8,128)(2,1)S(1)} %edge_rows.2.after), channel_id=1, source_target_pairs={{0,2},{1,17},{2,0},{3,5},{4,6},{5,3},{6,4},{7,9},{8,10},{9,7},{10,... | collective-permute-start | bytes 884744 | tf_op jit(solution)/shard_map/ppermute | solution.py:365
  19.3 4.6 %collective-permute-start.2 = (bf16[4,96,384]{2,1,0:T(8,128)(2,1)S(1)}, bf16[4,96,384]{2,1,0:T(8,128)(2,1)S(1)}, u32[]{:S(2)}, u32[]{:S(2)}) collective-permute-start(bf16[4,96,384]{2,1,0:T(8,128)(2,1)S(1)} %collective-permute-done.1.mine), channel_id=1, source_target_pairs={{0,1},{1,0},{2,3},{3,2},{4,5},{5,4},{6,7},{7,6},{8,9},{9,8},{10,11... | collective-permute-start | bytes 884744 | tf_op jit(solution)/shard_map/ppermute | solution.py:352
  32.4 2.5 %collective-permute-start.3 = (f32[576,384]{1,0:T(8,128)S(1)}, f32[576,384]{1,0:T(8,128)S(1)}, u32[]{:S(2)}, u32[]{:S(2)}) collective-permute-start(f32[576,384]{1,0:T(8,128)S(1)} %get-tuple-element.16.own), channel_id=1, source_target_pairs={{0,1},{1,0},{2,3},{3,2},{4,5},{5,4},{6,7},{7,6},{8,9},{9,8},{10,11... | collective-permute-start | bytes 2654216 | tf_op jit(solution)/shard_map/ppermute | solution.py:352
  35.0 5.1 %collective-permute-start.4 = (bf16[2,96,384]{2,1,0:T(8,128)(2,1)S(1)}, bf16[2,96,384]{2,1,0:T(8,128)(2,1)S(1)}, u32[]{:S(2)}, u32[]{:S(2)}) collective-permute-start(bf16[2,96,384]{2,1,0:T(8,128)(2,1)S(1)} %edge_rows.3), channel_id=1, source_target_pairs={{0,2},{1,17},{2,0},{3,5},{4,6},{5,3},{6,4},{7,9},{8,10},{9,7},{10,... | collective-permute-start | bytes 442376 | tf_op jit(solution)/shard_map/ppermute | solution.py:365
  40.0 2.9 %collective-permute-start.5 = (bf16[2,96,384]{2,1,0:T(8,128)(2,1)S(1)}, bf16[2,96,384]{2,1,0:T(8,128)(2,1)S(1)}, u32[]{:S(2)}, u32[]{:S(2)}) collective-permute-start(bf16[2,96,384]{2,1,0:T(8,128)(2,1)S(1)} %collective-permute-done.4.mine), channel_id=1, source_target_pairs={{0,1},{1,0},{2,3},{3,2},{4,5},{5,4},{6,7},{7,6},{8,9},{9,8},{10,11... | collective-permute-start | bytes 442376 | tf_op jit(solution)/shard_map/ppermute | solution.py:352

commit v3 on v2

--- a/solution.py
+++ b/solution.py
@@ -30,15 +30,15 @@
 
 
 def place(info, plane, slot):
-    ident = info[0][plane, min(slot, info[0].shape[1] - 1)]
+    ident = info[0][plane, slot]
     start = pl.multiple_of((2 - ident // 3) * LX, LX)
     return start, jnp.where(slot < count_of(info, plane), ident % 3, 3)
 
 
 def by_pairs(info, plane, slots, body):
     pairs = (count_of(info, plane) + 1) // 2
-    for k in range(1, slots // 2 + 1):
-        pl.when(pairs == k)(functools.partial(body, 2 * k))
+    for k in range(1, (slots + 1) // 2 + 1):
+        pl.when(pairs == k)(functools.partial(body, min(2 * k, slots)))
 
 
 def project_slab(info, plane, x, kp, acc):
@@ -84,11 +84,8 @@
 
 def split_kernel(psf, kp):
     slots, pix, planes, vox = psf.shape
-    even = kp.shape[1]
     full = pix // 16 * 16
-    kp[:, :, full:PADW, :] = jnp.zeros((planes, even, PADW - full, vox), BF)
-    if slots < even:
-        kp[:, slots, 0:full, :] = jnp.zeros((planes, full, vox), BF)
+    kp[:, :, full:PADW, :] = jnp.zeros((planes, slots, PADW - full, vox), BF)
     for s in range(slots):
         both = jnp.swapaxes(psf[s], 0, 1)
         for z in range(planes):
@@ -99,7 +96,7 @@
     planes, slots, pix, vox = psf.shape
     return pl.pallas_call(
         split_kernel,
-        out_shape=jax.ShapeDtypeStruct((planes, slots + slots % 2, PADW, vox), BF),
+        out_shape=jax.ShapeDtypeStruct((planes, slots, PADW, vox), BF),
         in_specs=[VMEM],
         out_specs=VMEM,
         compiler_params=pltpu.CompilerParams(vmem_limit_bytes=SPLIT_VMEM),
@@ -108,7 +105,7 @@
     )(jnp.transpose(psf, (1, 2, 0, 3)))
 
 
-def first_kernel(ids, counts, est, kp, part_out, est_out, xs, acc):
+def first_kernel(ids, counts, est, kp, part_out, send_out, est_out, xs, acc):
     acc[0:3] = jnp.zeros((3,) + acc.shape[1:], F32)
 
     def body(z):
@@ -118,7 +115,7 @@
         project_slab((ids, counts), z, xs, kp, acc)
 
     each_plane(est.shape[0], body)
-    part_out[...] = fold_dx(acc)
+    keep_part(fold_dx(acc), part_out, send_out)
 
 
 def first_call(estimate, kp, ids, counts):
@@ -128,10 +125,11 @@
         first_kernel,
         out_shape=(
             jax.ShapeDtypeStruct((rows, PADW), F32),
+            jax.ShapeDtypeStruct((2 * LX, PADW), F32),
             jax.ShapeDtypeStruct((planes, lens, vox), F32),
         ),
         in_specs=[SMEM, SMEM, VMEM, VMEM],
-        out_specs=(VMEM, VMEM),
+        out_specs=(VMEM, VMEM, VMEM),
         scratch_shapes=[
             pltpu.VMEM((lens, vox), BF),
             pltpu.VMEM((4, rows, PADW), F32),
@@ -146,6 +144,10 @@
     return pl.CostEstimate(flops=int(us * 1e9), bytes_accessed=int(us * 3e6), transcendentals=0)
 
 
+def upward():
+    return lax.rem(lax.axis_index("band") + lax.axis_index("depth"), 2) == 1
+
+
 def sensor_kernel(meas, bg, out):
     pix = meas.shape[0]
     out[...] = jnp.zeros(out.shape, F32)
@@ -166,20 +168,23 @@
     )(measured, background)
 
 
-def upward():
-    return lax.rem(lax.axis_index("band") + lax.axis_index("depth"), 2) == 0
+def keep_part(total, part_out, send_out):
+    part_out[...] = total
+    rows = part_out.shape[0]
+    start = pl.multiple_of(jnp.where(upward(), 0, rows - 2 * LX), LX)
+    send_out[...] = part_out[pl.ds(start, 2 * LX), :]
 
 
 def edge_kernel(own, other, *refs):
-    sensor, out = (refs[0], refs[1]) if len(refs) == 2 else (None, refs[0])
+    out = refs[-1]
     rows = own.shape[0]
     up = upward()
-    outer = pl.multiple_of(jnp.where(up, rows - LX, 0), LX)
-    inner = pl.multiple_of(jnp.where(up, rows - 2 * LX, LX), LX)
-    for i, start in enumerate((outer, inner)):
-        out[i] = (own[pl.ds(start, LX), :] + other[pl.ds(start, LX), :]).astype(BF)
-    if sensor is not None:
-        line = pl.multiple_of(inner - LX, LX)
+    base = pl.multiple_of(jnp.where(up, rows - 2 * LX, 0), LX)
+    for i in range(2):
+        line = pl.multiple_of(jnp.where(up, LX - i * LX, i * LX), LX)
+        out[i] = (own[pl.ds(base + line, LX), :] + other[pl.ds(line, LX), :]).astype(BF)
+    for sensor in refs[:-1]:
+        line = pl.multiple_of(jnp.where(up, rows - 3 * LX, 0), LX)
         for i in range(2):
             out[2 + i] = sensor[i, pl.ds(line, LX), :].astype(BF)
 
@@ -191,17 +196,23 @@
         in_specs=[VMEM] * (2 + len(sensor)),
         out_specs=VMEM,
         compiler_params=pltpu.CompilerParams(vmem_limit_bytes=16 << 20),
+        cost_estimate=cost(0.3),
         name="edge_rows",
     )(own, other, *sensor)
 
 
-def ratio_planes(own, other, mine, theirs, sensor, halo, planes_ref, pix):
+def ratio_planes(own, other, mine, theirs, sensor, sensor_mine, sensor_theirs, planes_ref, pix):
     rows = own.shape[0]
     lens = rows - 2 * LX
     band = lax.axis_index("band")
     up = upward()
-    upper = [jnp.where(up, mine[i].astype(F32), theirs[i].astype(F32)) for i in range(2)]
-    lower = [jnp.where(up, theirs[i].astype(F32), mine[i].astype(F32)) for i in range(2)]
+
+    def both(a, b, start):
+        pair = [(a[i].astype(F32), b[i].astype(F32)) for i in (start, start + 1)]
+        return [jnp.where(up, x, y) for x, y in pair], [jnp.where(up, y, x) for x, y in pair]
+
+    upper, lower = both(mine, theirs, 0)
+    sensor_up, sensor_low = both(sensor_mine, sensor_theirs, 2)
     below = band > 0
     above = band < lax.axis_size("band") - 1
     lane = lax.broadcasted_iota(jnp.int32, (1, PADW), 1) < pix
@@ -214,11 +225,11 @@
         return jnp.where(keep, measured / (total + background), 0.0).astype(BF).astype(F32)
 
     parts = [
-        ratio(0, LX, lower[1], halo[0], halo[1], below),
+        ratio(0, LX, lower[1], sensor_low[0], sensor_low[1], below),
         ratio(LX, LX, jnp.where(below, lower[0], 0.0), sensor[0, 0:LX], sensor[1, 0:LX], None),
         ratio(2 * LX, lens - 2 * LX, None, sensor[0, LX : lens - LX], sensor[1, LX : lens - LX], None),
         ratio(lens, LX, jnp.where(above, upper[0], 0.0), sensor[0, lens - LX : lens], sensor[1, lens - LX : lens], None),
-        ratio(lens + LX, LX, upper[1], halo[2], halo[3], above),
+        ratio(lens + LX, LX, upper[1], sensor_up[0], sensor_up[1], above),
     ]
     whole = jnp.concatenate(parts, axis=0)
     col = column_of(rows, PADW)
@@ -275,14 +286,11 @@
     )(ids, counts, kp, after)
 
 
-def middle_kernel(pix, ids, counts, own, other, mine, theirs, sensor, est, inv, kp, part_out, vol_out, halo_out, ratios, xs, back, acc):
-    up = upward()
-    for i in range(2):
-        a = mine[2 + i].astype(F32)
-        b = theirs[2 + i].astype(F32)
-        halo_out[i] = jnp.where(up, b, a)
-        halo_out[2 + i] = jnp.where(up, a, b)
-    ratio_planes(own, other, mine, theirs, sensor, halo_out, ratios, pix)
+def middle_kernel(
+    pix, ids, counts, own, other, mine, theirs, sensor, est, inv, kp,
+    part_out, send_out, vol_out, ratios, xs, back, acc,
+):
+    ratio_planes(own, other, mine, theirs, sensor, mine, theirs, ratios, pix)
     acc[0:3] = jnp.zeros((3,) + acc.shape[1:], F32)
 
     def body(z):
@@ -293,7 +301,7 @@
         project_slab((ids, counts), z, xs, kp, acc)
 
     each_plane(est.shape[0], body)
-    part_out[...] = fold_dx(acc)
+    keep_part(fold_dx(acc), part_out, send_out)
 
 
 def middle_call(pix, ids, counts, own, other, mine, theirs, sensor, est, inv, kp):
@@ -303,8 +311,8 @@
         functools.partial(middle_kernel, pix),
         out_shape=(
             jax.ShapeDtypeStruct((rows, PADW), F32),
+            jax.ShapeDtypeStruct((2 * LX, PADW), F32),
             jax.ShapeDtypeStruct((planes, lens, vox), F32),
-            jax.ShapeDtypeStruct((4, LX, PADW), F32),
         ),
         in_specs=[SMEM, SMEM] + [VMEM] * 8,
         out_specs=(VMEM,) * 3,
@@ -320,32 +328,42 @@
     )(ids, counts, own, other, mine, theirs, sensor, est, inv, kp)
 
 
-def last_kernel(pix, ids, counts, own, other, mine, theirs, sensor, halo, vol, inv, kp, out, ratios, back):
-    ratio_planes(own, other, mine, theirs, sensor, halo, ratios, pix)
+def last_kernel(
+    pix, ids, counts, own, other, mine, theirs, sensor, sensor_mine, sensor_theirs, vol, inv, kp,
+    out, ratios, back, turned, sem,
+):
+    ratio_planes(own, other, mine, theirs, sensor, sensor_mine, sensor_theirs, ratios, pix)
+
+    def copy(z):
+        return pltpu.make_async_copy(turned.at[z], out.at[z], sem.at[z])
 
     def body(z):
         back_slab((ids, counts), z, ratios, kp, back)
-        out[z] = (vol[z] * back[...] * inv[z]).T
+        turned[z] = (vol[z] * back[...] * inv[z]).T
+        copy(z).start()
 
     each_plane(vol.shape[0], body)
-
-
-def last_call(pix, ids, counts, own, other, mine, theirs, sensor, halo, vol, inv, kp):
+    each_plane(vol.shape[0], lambda z: copy(z).wait())
+
+
+def last_call(pix, ids, counts, own, other, mine, theirs, sensors, vol, inv, kp):
     planes, lens, vox = vol.shape
     rows = own.shape[0]
     return pl.pallas_call(
         functools.partial(last_kernel, pix),
         out_shape=jax.ShapeDtypeStruct((planes, vox, lens), F32),
-        in_specs=[SMEM, SMEM] + [VMEM] * 9,
-        out_specs=VMEM,
+        in_specs=[SMEM, SMEM] + [VMEM] * 10,
+        out_specs=ANY,
         scratch_shapes=[
             pltpu.VMEM((4, rows, PADW), BF),
             pltpu.VMEM((lens, vox), F32),
+            pltpu.VMEM((planes, vox, lens), F32),
+            pltpu.SemaphoreType.DMA((planes,)),
         ],
         compiler_params=pltpu.CompilerParams(vmem_limit_bytes=36 << 20),
         cost_estimate=cost(6),
         name="back_last",
-    )(ids, counts, own, other, mine, theirs, sensor, halo, vol, inv, kp)
+    )(ids, counts, own, other, mine, theirs, *sensors, vol, inv, kp)
 
 
 def swap(x):
@@ -358,7 +376,7 @@
     for p in range(parts):
         for b in range(bands):
             for d in range(depth):
-                q, c = p, b + (1 if (b + d) % 2 == 0 else -1)
+                q, c = p, b + (1 if (b + d) % 2 == 1 else -1)
                 if c < 0 or c == bands:
                     q, c = min(p ^ 1, parts - 1), b
                 pairs.append(((p * bands + b) * depth + d, (q * bands + c) * depth + d))
@@ -368,19 +386,23 @@
 def per_device(estimate, psf_blocks, offset_ids, block_counts, measured, background):
     pix, lens = measured.shape
     kp = split_call(psf_blocks)
-    part, est = first_call(estimate, kp, offset_ids, block_counts)
-    other = swap(part)
+    part, send, est = first_call(estimate, kp, offset_ids, block_counts)
+    sum_edge = swap(send)
     sensor = sensor_call(measured, background)
-    edges = edge_call(part, other, sensor)
+    edges, part = lax.optimization_barrier((edge_call(part, sum_edge, sensor), part))
     mine = edge_exchange(edges)
     inv = sensitivity_call(offset_ids, block_counts, kp, lens, edges)
+    other = swap(part)
     mine, inv = lax.optimization_barrier((mine, inv))
     theirs = swap(mine)
-    part, vol, halo = middle_call(pix, offset_ids, block_counts, part, other, mine, theirs, sensor, est, inv, kp)
+    sensors = (sensor, mine, theirs)
+    part, send, vol = middle_call(
+        pix, offset_ids, block_counts, part, other, mine, theirs, sensor, est, inv, kp
+    )
+    edges, part = lax.optimization_barrier((edge_call(part, swap(send)), part))
+    mine = edge_exchange(edges)
     other = swap(part)
-    mine = edge_exchange(edge_call(part, other))
-    theirs = swap(mine)
-    return last_call(pix, offset_ids, block_counts, part, other, mine, theirs, sensor, halo, vol, inv, kp)
+    return last_call(pix, offset_ids, block_counts, part, other, mine, swap(mine), sensors, vol, inv, kp)
 
 
 def solution(mesh):

time: 48.7 us -> 47.4 us (0.973)
  starting transfers between devices: 7.79 us -> 4.21 us
  Pallas kernels: 24.2 us -> 25.7 us
  waiting for transfers between devices: 13.6 us -> 14.5 us
    ppermute x4 -> x6, starting transfers between devices: 5.44 us -> 2.97 us  [swap(): return lax.ppermute(x, 'depth', [(0, 1), (1, 0)])]
    ppermute x2, waiting for transfers between devices: 6.94 us -> 9.17 us  [edge_exchange(): return lax.ppermute(x, ('parts', 'band', 'depth'), pairs)]
    ppermute x4 -> x6, waiting for transfers between devices: 6.65 us -> 5.34 us  [swap(): return lax.ppermute(x, 'depth', [(0, 1), (1, 0)])]
    ppermute x2, starting transfers between devices: 2.35 us -> 1.24 us  [edge_exchange(): return lax.ppermute(x, ('parts', 'band', 'depth'), pairs)]
    pallas_call x1, Pallas kernels: 8.49 us -> 9.24 us  [middle_call(): pl.pallas_call(functools.partial(middle_kernel, pix), out_shape=(jax.Shap...]
    pallas_call x1, Pallas kernels: 4.73 us -> 5.38 us  [first_call(): pl.pallas_call(first_kernel, out_shape=(jax.ShapeDtypeStruct((rows, PADW)...]
  transfers between devices with their start and end apart: 6 -> 8, of which waited for: 6 -> 6; matrix products, arithmetic and copies ran while one was open for 0% -> 0% of each run, Pallas kernels for 6% -> 6%
where the time goes in v3:
time: 47.4 us; the launch traced here: 47.6 us
  Pallas kernels  25.7 us (54%)
  waiting for transfers between devices  14.5 us (31%)
  starting transfers between devices  4.21 us (9%)
  local copies, waits for them, and re-layouts  2.91 us (6%)
    pallas_call x1, Pallas kernels, middle_call(): pl.pallas_call(functools.partial(middle_kernel, pix), out_shape=(jax.Shap...  9.24 us
    ppermute x2, waiting for transfers between devices, edge_exchange(): return lax.ppermute(x, ('parts', 'band', 'depth'), pairs)  9.17 us
    pallas_call x1, Pallas kernels, last_call(): pl.pallas_call(functools.partial(last_kernel, pix), out_shape=jax.ShapeDt...  5.92 us
    pallas_call x1, Pallas kernels, first_call(): pl.pallas_call(first_kernel, out_shape=(jax.ShapeDtypeStruct((rows, PADW)...  5.38 us
    ppermute x6, waiting for transfers between devices, swap(): return lax.ppermute(x, 'depth', [(0, 1), (1, 0)])  5.34 us
    ppermute x6, starting transfers between devices, swap(): return lax.ppermute(x, 'depth', [(0, 1), (1, 0)])  2.97 us
    unnamed x12, local copies, waits for them, and re-layouts  2.91 us
    pallas_call x1, Pallas kernels, split_call(): pl.pallas_call(split_kernel, out_shape=jax.ShapeDtypeStruct((planes, slot...  2.36 us
  transfers between devices with their start and end apart: 8, of which 6 were waited for; matrix products, arithmetic and copies ran while one was open for 0% of the time, Pallas kernels for 6%

profile of v3, /device:TPU:25, one launch (start us, length us, event | category | flops | bytes accessed | tf_op | source)
XLA Modules:
  0.0 47.6 jit_solution(2684814579736306254)
XLA Ops:
  0.0 2.9 %copy-done = bf16[2,9,361,512]{3,0,2,1:T(2,128)(2,1)S(1)} copy-done((bf16[2,9,361,512]{3,0,2,1:T(2,128)(2,1)S(1)}, bf16[2,9,361,512]{3,0,2,1:T(2,128)(2,1)}, u32[]{:S(2)}) %copy-start) | copy-done | bytes 6653976
  2.9 2.4 %split_planes.1.kp = bf16[2,9,384,512]{3,2,1,0:T(8,128)(2,1)S(1)} custom-call(bf16[9,361,2,512]{3,2,1,0:T(2,128)(2,1)S(1)} %bitcast.1), custom_call_target="tpu_custom_call" | custom-call | flops 5000000000 | bytes 15000000 | tf_op jit(solution)/shard_map/split_planes/pallas_call | solution.py:97
  5.3 0.0 copy-done.1
  5.3 0.0 copy-done.4
  5.3 0.0 copy-done.5
  5.3 0.0 copy-start.2
  5.3 0.0 copy-start.3
  5.3 5.4 %project_first.1 = (f32[576,384]{1,0:T(8,128)S(1)}, f32[192,384]{1,0:T(8,128)S(1)}, f32[2,384,512]{2,1,0:T(8,128)S(1)}) custom-call(s32[2,9]{1,0:T(2,128)S(1)} %copy-done.4, s32[2]{0:T(128)S(1)} %copy-done.5, f32[2,512,384]{2,1,0:T(8,128)S(1)} %copy-done.1, bf16[2,9,384,512]{3,2,1,0:T(8,128)(2,1)S(1)} %split_planes.1.kp), custom_call_target="tpu_custom_call" | custom-call | flops 5000000000 | bytes 15000000 | tf_op jit(solution)/shard_map/project_first/pallas_call | solution.py:124
  10.7 0.1 collective-permute-start
  10.8 0.0 copy-done.2
  10.8 0.0 copy-done.3
  10.8 0.4 sensor_turn.1.refs_0_.sensor
  11.2 1.2 %collective-permute-done.other = f32[192,384]{1,0:T(8,128)S(1)} collective-permute-done((f32[192,384]{1,0:T(8,128)S(1)}, f32[192,384]{1,0:T(8,128)S(1)}, u32[]{:S(2)}, u32[]{:S(2)}) %collective-permute-start) | collective-permute-done | bytes 294944 | tf_op jit(solution)/shard_map/ppermute | solution.py:370
  12.4 0.1 edge_rows.2.after
  12.4 0.2 collective-permute-start.1
  12.6 1.2 %collective-permute-start.2 = (bf16[4,96,384]{2,1,0:T(8,128)(2,1)S(1)}, bf16[4,96,384]{2,1,0:T(8,128)(2,1)S(1)}, u32[]{:S(2)}, u32[]{:S(2)}) collective-permute-start(bf16[4,96,384]{2,1,0:T(8,128)(2,1)S(1)} %edge_rows.2.after), channel_id=1, source_target_pairs={{0,16},{1,3},{2,4},{3,1},{4,2},{5,7},{6,8},{7,5},{8,6},{9,11},{10,... | collective-permute-start | bytes 884744 | tf_op jit(solution)/shard_map/ppermute | solution.py:383
  13.9 2.3 %sensitivity.1.inv = f32[2,384,512]{2,1,0:T(8,128)S(1)} custom-call(s32[2,9]{1,0:T(2,128)S(1)} %copy-done.4, s32[2]{0:T(128)S(1)} %copy-done.5, bf16[2,9,384,512]{3,2,1,0:T(8,128)(2,1)S(1)} %split_planes.1.kp, bf16[4,96,384]{2,1,0:T(8,128)(2,1)S(1)} %edge_rows.2.after), custom_call_target="tpu_custom_call" | custom-call | flops 3000000000 | bytes 9000000 | tf_op jit(solution)/shard_map/sensitivity/pallas_call | solution.py:278
  16.2 5.2 %collective-permute-done.2.mine.sensor_mine = bf16[4,96,384]{2,1,0:T(8,128)(2,1)S(1)} collective-permute-done((bf16[4,96,384]{2,1,0:T(8,128)(2,1)S(1)}, bf16[4,96,384]{2,1,0:T(8,128)(2,1)S(1)}, u32[]{:S(2)}, u32[]{:S(2)}) %collective-permute-start.2) | collective-permute-done | bytes 294944 | tf_op jit(solution)/shard_map/ppermute | solution.py:383
  21.4 0.0 collective-permute-start.3
  21.4 1.6 %collective-permute-done.3.theirs.sensor_theirs = bf16[4,96,384]{2,1,0:T(8,128)(2,1)S(1)} collective-permute-done((bf16[4,96,384]{2,1,0:T(8,128)(2,1)S(1)}, bf16[4,96,384]{2,1,0:T(8,128)(2,1)S(1)}, u32[]{:S(2)}, u32[]{:S(2)}) %collective-permute-start.3) | collective-permute-done | bytes 294944 | tf_op jit(solution)/shard_map/ppermute | solution.py:370
  22.9 0.0 collective-permute-done.1.other
  22.9 9.2 %back_and_project.1 = (f32[576,384]{1,0:T(8,128)S(1)}, f32[192,384]{1,0:T(8,128)S(1)}, f32[2,384,512]{2,1,0:T(8,128)S(1)}) custom-call(s32[2,9]{1,0:T(2,128)S(1)} %copy-done.4, s32[2]{0:T(128)S(1)} %copy-done.5, f32[576,384]{1,0:T(8,128)S(1)} %get-tuple-element.19.own, f32[576,384]{1,0:T(8,128)S(1)} %collective-permute-done.1.other, ...), custom_call_target="tpu_custom_call" | custom-call | flops 10000000000 | bytes 30000000 | tf_op jit(solution)/shard_map/back_and_project/pallas_call | solution.py:310
  32.2 0.1 collective-permute-start.4
  32.3 1.6 %collective-permute-done.4.other = f32[192,384]{1,0:T(8,128)S(1)} collective-permute-done((f32[192,384]{1,0:T(8,128)S(1)}, f32[192,384]{1,0:T(8,128)S(1)}, u32[]{:S(2)}, u32[]{:S(2)}) %collective-permute-start.4) | collective-permute-done | bytes 294944 | tf_op jit(solution)/shard_map/ppermute | solution.py:370
  33.8 0.1 edge_rows.3
  33.9 0.2 collective-permute-start.5
  34.1 0.0 collective-permute-start.6
  34.1 4.0 %collective-permute-done.6.mine = bf16[2,96,384]{2,1,0:T(8,128)(2,1)S(1)} collective-permute-done((bf16[2,96,384]{2,1,0:T(8,128)(2,1)S(1)}, bf16[2,96,384]{2,1,0:T(8,128)(2,1)S(1)}, u32[]{:S(2)}, u32[]{:S(2)}) %collective-permute-start.6) | collective-permute-done | bytes 147488 | tf_op jit(solution)/shard_map/ppermute | solution.py:383
  38.1 2.4 %collective-permute-start.7 = (bf16[2,96,384]{2,1,0:T(8,128)(2,1)S(1)}, bf16[2,96,384]{2,1,0:T(8,128)(2,1)S(1)}, u32[]{:S(2)}, u32[]{:S(2)}) collective-permute-start(bf16[2,96,384]{2,1,0:T(8,128)(2,1)S(1)} %collective-permute-done.6.mine), channel_id=1, source_target_pairs={{0,1},{1,0},{2,3},{3,2},{4,5},{5,4},{6,7},{7,6},{8,9},{9,8},{10,11... | collective-permute-start | bytes 442376 | tf_op jit(solution)/shard_map/ppermute | solution.py:370
  40.5 1.0 %collective-permute-done.7.theirs = bf16[2,96,384]{2,1,0:T(8,128)(2,1)S(1)} collective-permute-done((bf16[2,96,384]{2,1,0:T(8,128)(2,1)S(1)}, bf16[2,96,384]{2,1,0:T(8,128)(2,1)S(1)}, u32[]{:S(2)}, u32[]{:S(2)}) %collective-permute-start.7) | collective-permute-done | bytes 147488 | tf_op jit(solution)/shard_map/ppermute | solution.py:370
  41.5 0.0 collective-permute-done.5.other
  41.5 5.9 %back_last.1 = f32[2,512,384]{2,1,0:T(8,128)} custom-call(s32[2,9]{1,0:T(2,128)S(1)} %copy-done.4, s32[2]{0:T(128)S(1)} %copy-done.5, f32[576,384]{1,0:T(8,128)S(1)} %get-tuple-element.26.own, f32[576,384]{1,0:T(8,128)S(1)} %collective-permute-done.5.other, bf16[2,96,384]{2,1,0:T(8,128)(2,1)S(1)} %collective-permute-done.6.mine, ...), custom_call_target="tpu_custom_call" | custom-call | flops 6000000000 | bytes 18000000 | tf_op jit(solution)/shard_map/back_last/pallas_call | solution.py:352
  (4 shorter events, 0.0 us)
Async XLA Ops:
  0.0 2.9 %copy-start = (bf16[2,9,361,512]{3,0,2,1:T(2,128)(2,1)S(1)}, bf16[2,9,361,512]{3,0,2,1:T(2,128)(2,1)}, u32[]{:S(2)}) copy-start(bf16[2,9,361,512]{3,0,2,1:T(2,128)(2,1)} %param.7) | copy-start | bytes 19961860
  2.9 2.4 %copy-start.1 = (f32[2,512,384]{2,1,0:T(8,128)S(1)}, f32[2,512,384]{2,1,0:T(8,128)}, u32[]{:S(2)}) copy-start(f32[2,512,384]{2,1,0:T(8,128)} %est.1) | copy-start | bytes 4718596
  2.9 2.4 %copy-start.4 = (s32[2,9]{1,0:T(2,128)S(1)}, s32[2,9]{1,0:T(2,128)}, u32[]{:S(2)}) copy-start(s32[2,9]{1,0:T(2,128)} %ids.7) | copy-start | bytes 220
  2.9 2.4 %copy-start.5 = (s32[2]{0:T(128)S(1)}, s32[2]{0:T(128)}, u32[]{:S(2)}) copy-start(s32[2]{0:T(128)} %counts.7) | copy-start | bytes 28
  5.3 5.5 %copy-start.2 = (f32[361,384]{1,0:T(8,128)S(1)}, f32[361,384]{1,0:T(8,128)}, u32[]{:S(2)}) copy-start(f32[361,384]{1,0:T(8,128)} %meas.1) | copy-start | bytes 1663492
  5.3 5.5 %copy-start.3 = (f32[361,384]{1,0:T(8,128)S(1)}, f32[361,384]{1,0:T(8,128)}, u32[]{:S(2)}) copy-start(f32[361,384]{1,0:T(8,128)} %bg.1) | copy-start | bytes 1663492
  10.7 1.6 %collective-permute-start = (f32[192,384]{1,0:T(8,128)S(1)}, f32[192,384]{1,0:T(8,128)S(1)}, u32[]{:S(2)}, u32[]{:S(2)}) collective-permute-start(f32[192,384]{1,0:T(8,128)S(1)} %get-tuple-element.18), channel_id=1, source_target_pairs={{0,1},{1,0},{2,3},{3,2},{4,5},{5,4},{6,7},{7,6},{8,9},{9,8},{10,11... | collective-permute-start | bytes 884744 | tf_op jit(solution)/shard_map/ppermute | solution.py:370
  12.4 10.5 %collective-permute-start.1 = (f32[576,384]{1,0:T(8,128)S(1)}, f32[576,384]{1,0:T(8,128)S(1)}, u32[]{:S(2)}, u32[]{:S(2)}) collective-permute-start(f32[576,384]{1,0:T(8,128)S(1)} %get-tuple-element.19.own), channel_id=1, source_target_pairs={{0,1},{1,0},{2,3},{3,2},{4,5},{5,4},{6,7},{7,6},{8,9},{9,8},{10,11... | collective-permute-start | bytes 2654216 | tf_op jit(solution)/shard_map/ppermute | solution.py:370
  12.6 8.7 %collective-permute-start.2 = (bf16[4,96,384]{2,1,0:T(8,128)(2,1)S(1)}, bf16[4,96,384]{2,1,0:T(8,128)(2,1)S(1)}, u32[]{:S(2)}, u32[]{:S(2)}) collective-permute-start(bf16[4,96,384]{2,1,0:T(8,128)(2,1)S(1)} %edge_rows.2.after), channel_id=1, source_target_pairs={{0,16},{1,3},{2,4},{3,1},{4,2},{5,7},{6,8},{7,5},{8,6},{9,11},{10,... | collective-permute-start | bytes 884744 | tf_op jit(solution)/shard_map/ppermute | solution.py:383
  21.4 1.6 %collective-permute-start.3 = (bf16[4,96,384]{2,1,0:T(8,128)(2,1)S(1)}, bf16[4,96,384]{2,1,0:T(8,128)(2,1)S(1)}, u32[]{:S(2)}, u32[]{:S(2)}) collective-permute-start(bf16[4,96,384]{2,1,0:T(8,128)(2,1)S(1)} %collective-permute-done.2.mine.sensor_mine), channel_id=1, source_target_pairs={{0,1},{1,0},{2,3},{3,2},{4,5},{5,4},{6,7},{7,6},{8,9},{9,8},{10,11... | collective-permute-start | bytes 884744 | tf_op jit(solution)/shard_map/ppermute | solution.py:370
  32.2 1.6 %collective-permute-start.4 = (f32[192,384]{1,0:T(8,128)S(1)}, f32[192,384]{1,0:T(8,128)S(1)}, u32[]{:S(2)}, u32[]{:S(2)}) collective-permute-start(f32[192,384]{1,0:T(8,128)S(1)} %get-tuple-element.25), channel_id=1, source_target_pairs={{0,1},{1,0},{2,3},{3,2},{4,5},{5,4},{6,7},{7,6},{8,9},{9,8},{10,11... | collective-permute-start | bytes 884744 | tf_op jit(solution)/shard_map/ppermute | solution.py:370
  33.9 7.6 %collective-permute-start.5 = (f32[576,384]{1,0:T(8,128)S(1)}, f32[576,384]{1,0:T(8,128)S(1)}, u32[]{:S(2)}, u32[]{:S(2)}) collective-permute-start(f32[576,384]{1,0:T(8,128)S(1)} %get-tuple-element.26.own), channel_id=1, source_target_pairs={{0,1},{1,0},{2,3},{3,2},{4,5},{5,4},{6,7},{7,6},{8,9},{9,8},{10,11... | collective-permute-start | bytes 2654216 | tf_op jit(solution)/shard_map/ppermute | solution.py:370
  34.1 4.0 %collective-permute-start.6 = (bf16[2,96,384]{2,1,0:T(8,128)(2,1)S(1)}, bf16[2,96,384]{2,1,0:T(8,128)(2,1)S(1)}, u32[]{:S(2)}, u32[]{:S(2)}) collective-permute-start(bf16[2,96,384]{2,1,0:T(8,128)(2,1)S(1)} %edge_rows.3), channel_id=1, source_target_pairs={{0,16},{1,3},{2,4},{3,1},{4,2},{5,7},{6,8},{7,5},{8,6},{9,11},{10,... | collective-permute-start | bytes 442376 | tf_op jit(solution)/shard_map/ppermute | solution.py:383
  38.1 3.4 %collective-permute-start.7 = (bf16[2,96,384]{2,1,0:T(8,128)(2,1)S(1)}, bf16[2,96,384]{2,1,0:T(8,128)(2,1)S(1)}, u32[]{:S(2)}, u32[]{:S(2)}) collective-permute-start(bf16[2,96,384]{2,1,0:T(8,128)(2,1)S(1)} %collective-permute-done.6.mine), channel_id=1, source_target_pairs={{0,1},{1,0},{2,3},{3,2},{4,5},{5,4},{6,7},{7,6},{8,9},{9,8},{10,11... | collective-permute-start | bytes 442376 | tf_op jit(solution)/shard_map/ppermute | solution.py:370

commit v4 on v3

--- a/solution.py
+++ b/solution.py
@@ -82,7 +82,7 @@
     return acc[1] + left + right
 
 
-def split_kernel(psf, kp):
+def split_kernel(psf, after, kp):
     slots, pix, planes, vox = psf.shape
     full = pix // 16 * 16
     kp[:, :, full:PADW, :] = jnp.zeros((planes, slots, PADW - full, vox), BF)
@@ -92,17 +92,17 @@
             kp[z, s, 0:pix, :] = both[z]
 
 
-def split_call(psf):
+def split_call(psf, after):
     planes, slots, pix, vox = psf.shape
     return pl.pallas_call(
         split_kernel,
         out_shape=jax.ShapeDtypeStruct((planes, slots, PADW, vox), BF),
-        in_specs=[VMEM],
+        in_specs=[VMEM, ANY],
         out_specs=VMEM,
         compiler_params=pltpu.CompilerParams(vmem_limit_bytes=SPLIT_VMEM),
         cost_estimate=cost(5),
         name="split_planes",
-    )(jnp.transpose(psf, (1, 2, 0, 3)))
+    )(jnp.transpose(psf, (1, 2, 0, 3)), after)
 
 
 def first_kernel(ids, counts, est, kp, part_out, send_out, est_out, xs, acc):
@@ -148,22 +148,28 @@
     return lax.rem(lax.axis_index("band") + lax.axis_index("depth"), 2) == 1
 
 
-def sensor_kernel(meas, bg, out):
-    pix = meas.shape[0]
+def sensor_kernel(meas, bg, out, edge):
+    pix, lens = meas.shape
     out[...] = jnp.zeros(out.shape, F32)
     out[0, :, 0:pix] = meas[...].T
     out[1, :, 0:pix] = bg[...].T
+    line = pl.multiple_of(jnp.where(upward(), lens - LX, 0), LX)
+    edge[:, 0:LX] = out[:, pl.ds(line, LX), :]
+    edge[:, LX:] = jnp.zeros((2, edge.shape[1] - LX, PADW), F32)
 
 
 def sensor_call(measured, background):
     lens = measured.shape[1]
     return pl.pallas_call(
         sensor_kernel,
-        out_shape=jax.ShapeDtypeStruct((2, lens, PADW), F32),
+        out_shape=(
+            jax.ShapeDtypeStruct((2, lens, PADW), F32),
+            jax.ShapeDtypeStruct((2, LX + 8, PADW), F32),
+        ),
         in_specs=[VMEM, VMEM],
-        out_specs=VMEM,
+        out_specs=(VMEM, VMEM),
         compiler_params=pltpu.CompilerParams(vmem_limit_bytes=16 << 20),
-        cost_estimate=cost(1),
+        cost_estimate=cost(8),
         name="sensor_turn",
     )(measured, background)
 
@@ -175,30 +181,25 @@
     send_out[...] = part_out[pl.ds(start, 2 * LX), :]
 
 
-def edge_kernel(own, other, *refs):
-    out = refs[-1]
+def edge_kernel(own, other, out):
     rows = own.shape[0]
     up = upward()
     base = pl.multiple_of(jnp.where(up, rows - 2 * LX, 0), LX)
     for i in range(2):
         line = pl.multiple_of(jnp.where(up, LX - i * LX, i * LX), LX)
         out[i] = (own[pl.ds(base + line, LX), :] + other[pl.ds(line, LX), :]).astype(BF)
-    for sensor in refs[:-1]:
-        line = pl.multiple_of(jnp.where(up, rows - 3 * LX, 0), LX)
-        for i in range(2):
-            out[2 + i] = sensor[i, pl.ds(line, LX), :].astype(BF)
-
-
-def edge_call(own, other, *sensor):
+
+
+def edge_call(own, other):
     return pl.pallas_call(
         edge_kernel,
-        out_shape=jax.ShapeDtypeStruct((2 + 2 * len(sensor), LX, PADW), BF),
-        in_specs=[VMEM] * (2 + len(sensor)),
+        out_shape=jax.ShapeDtypeStruct((2, LX, PADW), BF),
+        in_specs=[VMEM, VMEM],
         out_specs=VMEM,
         compiler_params=pltpu.CompilerParams(vmem_limit_bytes=16 << 20),
         cost_estimate=cost(0.3),
         name="edge_rows",
-    )(own, other, *sensor)
+    )(own, other)
 
 
 def ratio_planes(own, other, mine, theirs, sensor, sensor_mine, sensor_theirs, planes_ref, pix):
@@ -207,12 +208,12 @@
     band = lax.axis_index("band")
     up = upward()
 
-    def both(a, b, start):
-        pair = [(a[i].astype(F32), b[i].astype(F32)) for i in (start, start + 1)]
+    def both(a, b):
+        pair = [(a[i, 0:LX].astype(F32), b[i, 0:LX].astype(F32)) for i in range(2)]
         return [jnp.where(up, x, y) for x, y in pair], [jnp.where(up, y, x) for x, y in pair]
 
-    upper, lower = both(mine, theirs, 0)
-    sensor_up, sensor_low = both(sensor_mine, sensor_theirs, 2)
+    upper, lower = both(mine, theirs)
+    sensor_up, sensor_low = both(sensor_mine, sensor_theirs)
     below = band > 0
     above = band < lax.axis_size("band") - 1
     lane = lax.broadcasted_iota(jnp.int32, (1, PADW), 1) < pix
@@ -287,10 +288,10 @@
 
 
 def middle_kernel(
-    pix, ids, counts, own, other, mine, theirs, sensor, est, inv, kp,
+    pix, ids, counts, own, other, mine, theirs, sensor, sensor_mine, sensor_theirs, est, inv, kp,
     part_out, send_out, vol_out, ratios, xs, back, acc,
 ):
-    ratio_planes(own, other, mine, theirs, sensor, mine, theirs, ratios, pix)
+    ratio_planes(own, other, mine, theirs, sensor, sensor_mine, sensor_theirs, ratios, pix)
     acc[0:3] = jnp.zeros((3,) + acc.shape[1:], F32)
 
     def body(z):
@@ -304,7 +305,7 @@
     keep_part(fold_dx(acc), part_out, send_out)
 
 
-def middle_call(pix, ids, counts, own, other, mine, theirs, sensor, est, inv, kp):
+def middle_call(pix, ids, counts, own, other, mine, theirs, sensors, est, inv, kp):
     planes, lens, vox = est.shape
     rows = own.shape[0]
     return pl.pallas_call(
@@ -314,7 +315,7 @@
             jax.ShapeDtypeStruct((2 * LX, PADW), F32),
             jax.ShapeDtypeStruct((planes, lens, vox), F32),
         ),
-        in_specs=[SMEM, SMEM] + [VMEM] * 8,
+        in_specs=[SMEM, SMEM] + [VMEM] * 10,
         out_specs=(VMEM,) * 3,
         scratch_shapes=[
             pltpu.VMEM((4, rows, PADW), BF),
@@ -325,7 +326,7 @@
         compiler_params=pltpu.CompilerParams(vmem_limit_bytes=36 << 20),
         cost_estimate=cost(10),
         name="back_and_project",
-    )(ids, counts, own, other, mine, theirs, sensor, est, inv, kp)
+    )(ids, counts, own, other, mine, theirs, *sensors, est, inv, kp)
 
 
 def last_kernel(
@@ -385,19 +386,19 @@
 
 def per_device(estimate, psf_blocks, offset_ids, block_counts, measured, background):
     pix, lens = measured.shape
-    kp = split_call(psf_blocks)
+    sensor, sensor_edge = sensor_call(measured, background)
+    sensor_mine = edge_exchange(sensor_edge)
+    kp = split_call(psf_blocks, sensor_edge)
     part, send, est = first_call(estimate, kp, offset_ids, block_counts)
-    sum_edge = swap(send)
-    sensor = sensor_call(measured, background)
-    edges, part = lax.optimization_barrier((edge_call(part, sum_edge, sensor), part))
+    sum_edge, sensor_mine = lax.optimization_barrier((swap(send), sensor_mine))
+    edges, part = lax.optimization_barrier((edge_call(part, sum_edge), part))
     mine = edge_exchange(edges)
     inv = sensitivity_call(offset_ids, block_counts, kp, lens, edges)
     other = swap(part)
+    sensors = (sensor, sensor_mine, swap(sensor_mine))
     mine, inv = lax.optimization_barrier((mine, inv))
-    theirs = swap(mine)
-    sensors = (sensor, mine, theirs)
     part, send, vol = middle_call(
-        pix, offset_ids, block_counts, part, other, mine, theirs, sensor, est, inv, kp
+        pix, offset_ids, block_counts, part, other, mine, swap(mine), sensors, est, inv, kp
     )
     edges, part = lax.optimization_barrier((edge_call(part, swap(send)), part))
     mine = edge_exchange(edges)

time: 47.4 us -> 45.2 us (0.954)
  waiting for transfers between devices: 14.5 us -> 9.65 us
  starting transfers between devices: 4.21 us -> 7.86 us
  Pallas kernels: 25.7 us -> 24.8 us
    ppermute x2 -> x3, waiting for transfers between devices: 9.17 us -> 4.49 us  [edge_exchange(): return lax.ppermute(x, ('parts', 'band', 'depth'), pairs)]
    ppermute x6 -> x7, starting transfers between devices: 2.97 us -> 5.71 us  [swap(): return lax.ppermute(x, 'depth', [(0, 1), (1, 0)])]
    ppermute x2 -> x3, starting transfers between devices: 1.24 us -> 2.15 us  [edge_exchange(): return lax.ppermute(x, ('parts', 'band', 'depth'), pairs)]
    pallas_call x1, Pallas kernels: 9.24 us -> 8.71 us  [middle_call(): pl.pallas_call(functools.partial(middle_kernel, pix), out_shape=(jax.Shap...]
    ppermute x6 -> x7, waiting for transfers between devices: 5.34 us -> 5.16 us  [swap(): return lax.ppermute(x, 'depth', [(0, 1), (1, 0)])]
  transfers between devices with their start and end apart: 8 -> 10, of which waited for: 6 -> 6; matrix products, arithmetic and copies ran while one was open for 0% -> 0% of each run, Pallas kernels for 6% -> 22%
where the time goes in v4:
time: 45.2 us; the launch traced here: 45 us
  Pallas kernels  24.8 us (55%)
  waiting for transfers between devices  9.65 us (21%)
  starting transfers between devices  7.86 us (17%)
  local copies, waits for them, and re-layouts  2.5 us (6%)
    pallas_call x1, Pallas kernels, middle_call(): pl.pallas_call(functools.partial(middle_kernel, pix), out_shape=(jax.Shap...  8.71 us
    ppermute x7, starting transfers between devices, swap(): return lax.ppermute(x, 'depth', [(0, 1), (1, 0)])  5.71 us
    pallas_call x1, Pallas kernels, last_call(): pl.pallas_call(functools.partial(last_kernel, pix), out_shape=jax.ShapeDt...  5.67 us
    pallas_call x1, Pallas kernels, first_call(): pl.pallas_call(first_kernel, out_shape=(jax.ShapeDtypeStruct((rows, PADW)...  5.19 us
    ppermute x7, waiting for transfers between devices, swap(): return lax.ppermute(x, 'depth', [(0, 1), (1, 0)])  5.16 us
    ppermute x3, waiting for transfers between devices, edge_exchange(): return lax.ppermute(x, ('parts', 'band', 'depth'), pairs)  4.49 us
    unnamed x12, local copies, waits for them, and re-layouts  2.5 us
    pallas_call x1, Pallas kernels, split_call(): pl.pallas_call(split_kernel, out_shape=jax.ShapeDtypeStruct((planes, slot...  2.37 us
  transfers between devices with their start and end apart: 10, of which 6 were waited for; matrix products, arithmetic and copies ran while one was open for 0% of the time, Pallas kernels for 22%

profile of v4, /device:TPU:25, one launch (start us, length us, event | category | flops | bytes accessed | tf_op | source)
XLA Modules:
  0.0 45.0 jit_solution(6139632291774790916)
XLA Ops:
  0.0 1.2 %copy-done.2 = f32[361,384]{1,0:T(8,128)S(1)} copy-done((f32[361,384]{1,0:T(8,128)S(1)}, f32[361,384]{1,0:T(8,128)}, u32[]{:S(2)}) %copy-start.2) | copy-done | bytes 554520
  1.2 1.3 %copy-done.3 = f32[361,384]{1,0:T(8,128)S(1)} copy-done((f32[361,384]{1,0:T(8,128)S(1)}, f32[361,384]{1,0:T(8,128)}, u32[]{:S(2)}) %copy-start.3) | copy-done | bytes 554520
  2.5 0.4 sensor_turn.1
  2.9 1.3 %collective-permute-start.1 = (f32[2,104,384]{2,1,0:T(8,128)S(1)}, f32[2,104,384]{2,1,0:T(8,128)S(1)}, u32[]{:S(2)}, u32[]{:S(2)}) collective-permute-start(f32[2,104,384]{2,1,0:T(8,128)S(1)} %get-tuple-element.21.after), channel_id=1, source_target_pairs={{0,16},{1,3},{2,4},{3,1},{4,2},{5,7},{6,8},{7,5},{8,6},{9,11},{10,... | collective-permute-start | bytes 958472 | tf_op jit(solution)/shard_map/ppermute | solution.py:384
  4.2 0.0 copy-done
  4.2 2.4 %split_planes.1.kp = bf16[2,9,384,512]{3,2,1,0:T(8,128)(2,1)S(1)} custom-call(bf16[9,361,2,512]{3,2,1,0:T(2,128)(2,1)S(1)} %bitcast.1, f32[2,104,384]{2,1,0:T(8,128)S(1)} %get-tuple-element.21.after), custom_call_target="tpu_custom_call" | custom-call | flops 5000000000 | bytes 15000000 | tf_op jit(solution)/shard_map/split_planes/pallas_call | solution.py:97
  6.6 0.0 copy-done.1
  6.7 5.2 %project_first.1 = (f32[576,384]{1,0:T(8,128)S(1)}, f32[192,384]{1,0:T(8,128)S(1)}, f32[2,384,512]{2,1,0:T(8,128)S(1)}) custom-call(s32[2,9]{1,0:T(2,128)S(1)} %copy-done.4, s32[2]{0:T(128)S(1)} %copy-done.5, f32[2,512,384]{2,1,0:T(8,128)S(1)} %copy-done.1, bf16[2,9,384,512]{3,2,1,0:T(8,128)(2,1)S(1)} %split_planes.1.kp), custom_call_target="tpu_custom_call" | custom-call | flops 5000000000 | bytes 15000000 | tf_op jit(solution)/shard_map/project_first/pallas_call | solution.py:124
  11.8 0.1 collective-permute-start
  11.9 1.6 %collective-permute-done.other = f32[192,384]{1,0:T(8,128)S(1)} collective-permute-done((f32[192,384]{1,0:T(8,128)S(1)}, f32[192,384]{1,0:T(8,128)S(1)}, u32[]{:S(2)}, u32[]{:S(2)}) %collective-permute-start) | collective-permute-done | bytes 294944 | tf_op jit(solution)/shard_map/ppermute | solution.py:371
  13.5 0.0 collective-permute-done.1.sensor_mine
  13.5 0.1 edge_rows.2.after
  13.6 0.2 collective-permute-start.2
  13.8 0.9 %collective-permute-start.3 = (bf16[2,96,384]{2,1,0:T(8,128)(2,1)S(1)}, bf16[2,96,384]{2,1,0:T(8,128)(2,1)S(1)}, u32[]{:S(2)}, u32[]{:S(2)}) collective-permute-start(bf16[2,96,384]{2,1,0:T(8,128)(2,1)S(1)} %edge_rows.2.after), channel_id=1, source_target_pairs={{0,16},{1,3},{2,4},{3,1},{4,2},{5,7},{6,8},{7,5},{8,6},{9,11},{10,... | collective-permute-start | bytes 442376 | tf_op jit(solution)/shard_map/ppermute | solution.py:384
  14.6 0.3 collective-permute-start.5
  14.9 2.3 %sensitivity.1.inv = f32[2,384,512]{2,1,0:T(8,128)S(1)} custom-call(s32[2,9]{1,0:T(2,128)S(1)} %copy-done.4, s32[2]{0:T(128)S(1)} %copy-done.5, bf16[2,9,384,512]{3,2,1,0:T(8,128)(2,1)S(1)} %split_planes.1.kp, bf16[2,96,384]{2,1,0:T(8,128)(2,1)S(1)} %edge_rows.2.after), custom_call_target="tpu_custom_call" | custom-call | flops 3000000000 | bytes 9000000 | tf_op jit(solution)/shard_map/sensitivity/pallas_call | solution.py:279
  17.2 0.5 %collective-permute-done.3.mine = bf16[2,96,384]{2,1,0:T(8,128)(2,1)S(1)} collective-permute-done((bf16[2,96,384]{2,1,0:T(8,128)(2,1)S(1)}, bf16[2,96,384]{2,1,0:T(8,128)(2,1)S(1)}, u32[]{:S(2)}, u32[]{:S(2)}) %collective-permute-start.3) | collective-permute-done | bytes 147488 | tf_op jit(solution)/shard_map/ppermute | solution.py:384
  17.7 2.4 %collective-permute-start.4 = (bf16[2,96,384]{2,1,0:T(8,128)(2,1)S(1)}, bf16[2,96,384]{2,1,0:T(8,128)(2,1)S(1)}, u32[]{:S(2)}, u32[]{:S(2)}) collective-permute-start(bf16[2,96,384]{2,1,0:T(8,128)(2,1)S(1)} %collective-permute-done.3.mine), channel_id=1, source_target_pairs={{0,1},{1,0},{2,3},{3,2},{4,5},{5,4},{6,7},{7,6},{8,9},{9,8},{10,11... | collective-permute-start | bytes 442376 | tf_op jit(solution)/shard_map/ppermute | solution.py:371
  20.2 1.0 %collective-permute-done.4.theirs = bf16[2,96,384]{2,1,0:T(8,128)(2,1)S(1)} collective-permute-done((bf16[2,96,384]{2,1,0:T(8,128)(2,1)S(1)}, bf16[2,96,384]{2,1,0:T(8,128)(2,1)S(1)}, u32[]{:S(2)}, u32[]{:S(2)}) %collective-permute-start.4) | collective-permute-done | bytes 147488 | tf_op jit(solution)/shard_map/ppermute | solution.py:371
  21.2 0.0 collective-permute-done.5.sensor_theirs
  21.2 0.0 collective-permute-done.2.other
  21.2 8.7 %back_and_project.1 = (f32[576,384]{1,0:T(8,128)S(1)}, f32[192,384]{1,0:T(8,128)S(1)}, f32[2,384,512]{2,1,0:T(8,128)S(1)}) custom-call(s32[2,9]{1,0:T(2,128)S(1)} %copy-done.4, s32[2]{0:T(128)S(1)} %copy-done.5, f32[576,384]{1,0:T(8,128)S(1)} %get-tuple-element.25.own, f32[576,384]{1,0:T(8,128)S(1)} %collective-permute-done.2.other, ...), custom_call_target="tpu_custom_call" | custom-call | flops 10000000000 | bytes 30000000 | tf_op jit(solution)/shard_map/back_and_project/pallas_call | solution.py:311
  29.9 0.1 collective-permute-start.6
  30.0 1.6 %collective-permute-done.6.other = f32[192,384]{1,0:T(8,128)S(1)} collective-permute-done((f32[192,384]{1,0:T(8,128)S(1)}, f32[192,384]{1,0:T(8,128)S(1)}, u32[]{:S(2)}, u32[]{:S(2)}) %collective-permute-start.6) | collective-permute-done | bytes 294944 | tf_op jit(solution)/shard_map/ppermute | solution.py:371
  31.5 0.1 edge_rows.3
  31.6 0.2 collective-permute-start.7
  31.8 0.0 collective-permute-start.8
  31.8 4.0 %collective-permute-done.8.mine = bf16[2,96,384]{2,1,0:T(8,128)(2,1)S(1)} collective-permute-done((bf16[2,96,384]{2,1,0:T(8,128)(2,1)S(1)}, bf16[2,96,384]{2,1,0:T(8,128)(2,1)S(1)}, u32[]{:S(2)}, u32[]{:S(2)}) %collective-permute-start.8) | collective-permute-done | bytes 147488 | tf_op jit(solution)/shard_map/ppermute | solution.py:384
  35.8 2.4 %collective-permute-start.9 = (bf16[2,96,384]{2,1,0:T(8,128)(2,1)S(1)}, bf16[2,96,384]{2,1,0:T(8,128)(2,1)S(1)}, u32[]{:S(2)}, u32[]{:S(2)}) collective-permute-start(bf16[2,96,384]{2,1,0:T(8,128)(2,1)S(1)} %collective-permute-done.8.mine), channel_id=1, source_target_pairs={{0,1},{1,0},{2,3},{3,2},{4,5},{5,4},{6,7},{7,6},{8,9},{9,8},{10,11... | collective-permute-start | bytes 442376 | tf_op jit(solution)/shard_map/ppermute | solution.py:371
  38.2 1.0 %collective-permute-done.9.theirs = bf16[2,96,384]{2,1,0:T(8,128)(2,1)S(1)} collective-permute-done((bf16[2,96,384]{2,1,0:T(8,128)(2,1)S(1)}, bf16[2,96,384]{2,1,0:T(8,128)(2,1)S(1)}, u32[]{:S(2)}, u32[]{:S(2)}) %collective-permute-start.9) | collective-permute-done | bytes 147488 | tf_op jit(solution)/shard_map/ppermute | solution.py:371
  39.2 0.0 collective-permute-done.7.other
  39.2 5.7 %back_last.1 = f32[2,512,384]{2,1,0:T(8,128)} custom-call(s32[2,9]{1,0:T(2,128)S(1)} %copy-done.4, s32[2]{0:T(128)S(1)} %copy-done.5, f32[576,384]{1,0:T(8,128)S(1)} %get-tuple-element.34.own, f32[576,384]{1,0:T(8,128)S(1)} %collective-permute-done.7.other, bf16[2,96,384]{2,1,0:T(8,128)(2,1)S(1)} %collective-permute-done.8.mine, ...), custom_call_target="tpu_custom_call" | custom-call | flops 6000000000 | bytes 18000000 | tf_op jit(solution)/shard_map/back_last/pallas_call | solution.py:353
  (8 shorter events, 0.0 us)
Async XLA Ops:
  0.0 4.2 %copy-start = (bf16[2,9,361,512]{3,0,2,1:T(2,128)(2,1)S(1)}, bf16[2,9,361,512]{3,0,2,1:T(2,128)(2,1)}, u32[]{:S(2)}) copy-start(bf16[2,9,361,512]{3,0,2,1:T(2,128)(2,1)} %param.7) | copy-start | bytes 19961860
  0.0 1.2 %copy-start.2 = (f32[361,384]{1,0:T(8,128)S(1)}, f32[361,384]{1,0:T(8,128)}, u32[]{:S(2)}) copy-start(f32[361,384]{1,0:T(8,128)} %meas.1) | copy-start | bytes 1663492
  1.2 1.3 %copy-start.3 = (f32[361,384]{1,0:T(8,128)S(1)}, f32[361,384]{1,0:T(8,128)}, u32[]{:S(2)}) copy-start(f32[361,384]{1,0:T(8,128)} %bg.1) | copy-start | bytes 1663492
  2.9 10.6 %collective-permute-start.1 = (f32[2,104,384]{2,1,0:T(8,128)S(1)}, f32[2,104,384]{2,1,0:T(8,128)S(1)}, u32[]{:S(2)}, u32[]{:S(2)}) collective-permute-start(f32[2,104,384]{2,1,0:T(8,128)S(1)} %get-tuple-element.21.after), channel_id=1, source_target_pairs={{0,16},{1,3},{2,4},{3,1},{4,2},{5,7},{6,8},{7,5},{8,6},{9,11},{10,... | collective-permute-start | bytes 958472 | tf_op jit(solution)/shard_map/ppermute | solution.py:384
  4.2 2.4 %copy-start.1 = (f32[2,512,384]{2,1,0:T(8,128)S(1)}, f32[2,512,384]{2,1,0:T(8,128)}, u32[]{:S(2)}) copy-start(f32[2,512,384]{2,1,0:T(8,128)} %est.1) | copy-start | bytes 4718596
  4.2 2.4 %copy-start.4 = (s32[2,9]{1,0:T(2,128)S(1)}, s32[2,9]{1,0:T(2,128)}, u32[]{:S(2)}) copy-start(s32[2,9]{1,0:T(2,128)} %ids.7) | copy-start | bytes 220
  4.2 2.4 %copy-start.5 = (s32[2]{0:T(128)S(1)}, s32[2]{0:T(128)}, u32[]{:S(2)}) copy-start(s32[2]{0:T(128)} %counts.7) | copy-start | bytes 28
  11.8 1.6 %collective-permute-start = (f32[192,384]{1,0:T(8,128)S(1)}, f32[192,384]{1,0:T(8,128)S(1)}, u32[]{:S(2)}, u32[]{:S(2)}) collective-permute-start(f32[192,384]{1,0:T(8,128)S(1)} %get-tuple-element.23), channel_id=1, source_target_pairs={{0,1},{1,0},{2,3},{3,2},{4,5},{5,4},{6,7},{7,6},{8,9},{9,8},{10,11... | collective-permute-start | bytes 884744 | tf_op jit(solution)/shard_map/ppermute | solution.py:371
  13.6 7.6 %collective-permute-start.2 = (f32[576,384]{1,0:T(8,128)S(1)}, f32[576,384]{1,0:T(8,128)S(1)}, u32[]{:S(2)}, u32[]{:S(2)}) collective-permute-start(f32[576,384]{1,0:T(8,128)S(1)} %get-tuple-element.25.own), channel_id=1, source_target_pairs={{0,1},{1,0},{2,3},{3,2},{4,5},{5,4},{6,7},{7,6},{8,9},{9,8},{10,11... | collective-permute-start | bytes 2654216 | tf_op jit(solution)/shard_map/ppermute | solution.py:371
  13.8 4.0 %collective-permute-start.3 = (bf16[2,96,384]{2,1,0:T(8,128)(2,1)S(1)}, bf16[2,96,384]{2,1,0:T(8,128)(2,1)S(1)}, u32[]{:S(2)}, u32[]{:S(2)}) collective-permute-start(bf16[2,96,384]{2,1,0:T(8,128)(2,1)S(1)} %edge_rows.2.after), channel_id=1, source_target_pairs={{0,16},{1,3},{2,4},{3,1},{4,2},{5,7},{6,8},{7,5},{8,6},{9,11},{10,... | collective-permute-start | bytes 442376 | tf_op jit(solution)/shard_map/ppermute | solution.py:384
  14.6 6.6 %collective-permute-start.5 = (f32[2,104,384]{2,1,0:T(8,128)S(1)}, f32[2,104,384]{2,1,0:T(8,128)S(1)}, u32[]{:S(2)}, u32[]{:S(2)}) collective-permute-start(f32[2,104,384]{2,1,0:T(8,128)S(1)} %collective-permute-done.1.sensor_mine), channel_id=1, source_target_pairs={{0,1},{1,0},{2,3},{3,2},{4,5},{5,4},{6,7},{7,6},{8,9},{9,8},{10,11... | collective-permute-start | bytes 958472 | tf_op jit(solution)/shard_map/ppermute | solution.py:371
  17.7 3.4 %collective-permute-start.4 = (bf16[2,96,384]{2,1,0:T(8,128)(2,1)S(1)}, bf16[2,96,384]{2,1,0:T(8,128)(2,1)S(1)}, u32[]{:S(2)}, u32[]{:S(2)}) collective-permute-start(bf16[2,96,384]{2,1,0:T(8,128)(2,1)S(1)} %collective-permute-done.3.mine), channel_id=1, source_target_pairs={{0,1},{1,0},{2,3},{3,2},{4,5},{5,4},{6,7},{7,6},{8,9},{9,8},{10,11... | collective-permute-start | bytes 442376 | tf_op jit(solution)/shard_map/ppermute | solution.py:371
  29.9 1.6 %collective-permute-start.6 = (f32[192,384]{1,0:T(8,128)S(1)}, f32[192,384]{1,0:T(8,128)S(1)}, u32[]{:S(2)}, u32[]{:S(2)}) collective-permute-start(f32[192,384]{1,0:T(8,128)S(1)} %get-tuple-element.33), channel_id=1, source_target_pairs={{0,1},{1,0},{2,3},{3,2},{4,5},{5,4},{6,7},{7,6},{8,9},{9,8},{10,11... | collective-permute-start | bytes 884744 | tf_op jit(solution)/shard_map/ppermute | solution.py:371
  31.6 7.6 %collective-permute-start.7 = (f32[576,384]{1,0:T(8,128)S(1)}, f32[576,384]{1,0:T(8,128)S(1)}, u32[]{:S(2)}, u32[]{:S(2)}) collective-permute-start(f32[576,384]{1,0:T(8,128)S(1)} %get-tuple-element.34.own), channel_id=1, source_target_pairs={{0,1},{1,0},{2,3},{3,2},{4,5},{5,4},{6,7},{7,6},{8,9},{9,8},{10,11... | collective-permute-start | bytes 2654216 | tf_op jit(solution)/shard_map/ppermute | solution.py:371
  31.8 4.0 %collective-permute-start.8 = (bf16[2,96,384]{2,1,0:T(8,128)(2,1)S(1)}, bf16[2,96,384]{2,1,0:T(8,128)(2,1)S(1)}, u32[]{:S(2)}, u32[]{:S(2)}) collective-permute-start(bf16[2,96,384]{2,1,0:T(8,128)(2,1)S(1)} %edge_rows.3), channel_id=1, source_target_pairs={{0,16},{1,3},{2,4},{3,1},{4,2},{5,7},{6,8},{7,5},{8,6},{9,11},{10,... | collective-permute-start | bytes 442376 | tf_op jit(solution)/shard_map/ppermute | solution.py:384
  35.8 3.4 %collective-permute-start.9 = (bf16[2,96,384]{2,1,0:T(8,128)(2,1)S(1)}, bf16[2,96,384]{2,1,0:T(8,128)(2,1)S(1)}, u32[]{:S(2)}, u32[]{:S(2)}) collective-permute-start(bf16[2,96,384]{2,1,0:T(8,128)(2,1)S(1)} %collective-permute-done.8.mine), channel_id=1, source_target_pairs={{0,1},{1,0},{2,3},{3,2},{4,5},{5,4},{6,7},{7,6},{8,9},{9,8},{10,11... | collective-permute-start | bytes 442376 | tf_op jit(solution)/shard_map/ppermute | solution.py:371

commit v5 on v4

--- a/solution.py
+++ b/solution.py
@@ -25,6 +25,20 @@
     return lax.dot_general(a, b, (((1,), (1,)), ((), ())), preferred_element_type=F32)
 
 
+def fetch(ids_in, counts_in, ids, counts, sem):
+    copies = [
+        pltpu.make_async_copy(ids_in, ids, sem.at[0]),
+        pltpu.make_async_copy(counts_in, counts, sem.at[1]),
+    ]
+    for c in copies:
+        c.start()
+    return copies
+
+
+def list_scratch(ids, counts):
+    return [pltpu.SMEM(ids.shape, ids.dtype), pltpu.SMEM(counts.shape, counts.dtype), pltpu.SemaphoreType.DMA((2,))]
+
+
 def count_of(info, plane):
     return info[1][plane]
 
@@ -53,15 +67,15 @@
     by_pairs(info, plane, kp.shape[1], body)
 
 
-def back_slab(info, plane, ratios, kp, acc):
-    lens, vox = acc.shape
+def back_slab(info, plane, ratios, kp, lens, finish):
+    vox = kp.shape[3]
 
     def body(used):
         left = []
         for s in range(used):
             row, dx = place(info, plane, s)
             left.append(ratios[dx, pl.ds(row, lens), :])
-        acc[...] = dot(jnp.concatenate(left, axis=1), kp[plane, 0:used].reshape(used * PADW, vox))
+        finish(dot(jnp.concatenate(left, axis=1), kp[plane, 0:used].reshape(used * PADW, vox)))
 
     by_pairs(info, plane, kp.shape[1], body)
 
@@ -105,7 +119,8 @@
     )(jnp.transpose(psf, (1, 2, 0, 3)), after)
 
 
-def first_kernel(ids, counts, est, kp, part_out, send_out, est_out, xs, acc):
+def first_kernel(ids_in, counts_in, est, kp, part_out, send_out, est_out, xs, acc, ids, counts, sem):
+    copies = fetch(ids_in, counts_in, ids, counts, sem)
     acc[0:3] = jnp.zeros((3,) + acc.shape[1:], F32)
 
     def body(z):
@@ -114,6 +129,8 @@
         xs[...] = t.astype(BF)
         project_slab((ids, counts), z, xs, kp, acc)
 
+    for c in copies:
+        c.wait()
     each_plane(est.shape[0], body)
     keep_part(fold_dx(acc), part_out, send_out)
 
@@ -125,15 +142,16 @@
         first_kernel,
         out_shape=(
             jax.ShapeDtypeStruct((rows, PADW), F32),
-            jax.ShapeDtypeStruct((2 * LX, PADW), F32),
+            jax.ShapeDtypeStruct((2 * LX, PADW), BF),
             jax.ShapeDtypeStruct((planes, lens, vox), F32),
         ),
-        in_specs=[SMEM, SMEM, VMEM, VMEM],
+        in_specs=[ANY, ANY, VMEM, VMEM],
         out_specs=(VMEM, VMEM, VMEM),
         scratch_shapes=[
             pltpu.VMEM((lens, vox), BF),
             pltpu.VMEM((4, rows, PADW), F32),
-        ],
+        ]
+        + list_scratch(ids, counts),
         compiler_params=pltpu.CompilerParams(vmem_limit_bytes=36 << 20),
         cost_estimate=cost(5),
         name="project_first",
@@ -178,7 +196,7 @@
     part_out[...] = total
     rows = part_out.shape[0]
     start = pl.multiple_of(jnp.where(upward(), 0, rows - 2 * LX), LX)
-    send_out[...] = part_out[pl.ds(start, 2 * LX), :]
+    send_out[...] = part_out[pl.ds(start, 2 * LX), :].astype(BF)
 
 
 def edge_kernel(own, other, out):
@@ -187,7 +205,7 @@
     base = pl.multiple_of(jnp.where(up, rows - 2 * LX, 0), LX)
     for i in range(2):
         line = pl.multiple_of(jnp.where(up, LX - i * LX, i * LX), LX)
-        out[i] = (own[pl.ds(base + line, LX), :] + other[pl.ds(line, LX), :]).astype(BF)
+        out[i] = (own[pl.ds(base + line, LX), :] + other[pl.ds(line, LX), :].astype(F32)).astype(BF)
 
 
 def edge_call(own, other):
@@ -202,7 +220,45 @@
     )(own, other)
 
 
-def ratio_planes(own, other, mine, theirs, sensor, sensor_mine, sensor_theirs, planes_ref, pix):
+def ratio_rows(own, other, start, size, extra, measured, background, keep):
+    total = own[start : start + size, :] + other[start : start + size, :]
+    if extra is not None:
+        total = total + extra
+    return jnp.where(keep, measured / (total + background), 0.0).astype(BF).astype(F32)
+
+
+def spread(planes_ref, start, whole):
+    rows = whole.shape[0]
+    col = column_of(rows, PADW)
+    here = pl.ds(start, rows)
+    planes_ref[1, here, :] = whole.astype(BF)
+    planes_ref[2, here, :] = jnp.where(col > 0, pltpu.roll(whole, 1, 0), 0.0).astype(BF)
+    planes_ref[0, here, :] = jnp.where(col < LX - 1, pltpu.roll(whole, rows - 1, 0), 0.0).astype(BF)
+
+
+def real_lanes(pix):
+    return lax.broadcasted_iota(jnp.int32, (1, PADW), 1) < pix
+
+
+def inner_kernel(pix, own, other, sensor, out):
+    size = out.shape[1]
+    measured, background = (sensor[i, LX : LX + size] for i in range(2))
+    spread(out, 0, ratio_rows(own, other, 2 * LX, size, None, measured, background, real_lanes(pix)))
+
+
+def inner_call(pix, own, other, sensor):
+    return pl.pallas_call(
+        functools.partial(inner_kernel, pix),
+        out_shape=jax.ShapeDtypeStruct((3, own.shape[0] - 4 * LX, PADW), BF),
+        in_specs=[VMEM] * 3,
+        out_specs=VMEM,
+        compiler_params=pltpu.CompilerParams(vmem_limit_bytes=16 << 20),
+        cost_estimate=cost(1),
+        name="inner_ratio",
+    )(own, other, sensor)
+
+
+def ratio_planes(own, other, mine, theirs, inner, sensor, sensor_mine, sensor_theirs, planes_ref, pix):
     rows = own.shape[0]
     lens = rows - 2 * LX
     band = lax.axis_index("band")
@@ -216,28 +272,23 @@
     sensor_up, sensor_low = both(sensor_mine, sensor_theirs)
     below = band > 0
     above = band < lax.axis_size("band") - 1
-    lane = lax.broadcasted_iota(jnp.int32, (1, PADW), 1) < pix
-
-    def ratio(start, size, extra, measured, background, there):
-        total = own[start : start + size, :] + other[start : start + size, :]
-        if extra is not None:
-            total = total + extra
-        keep = lane if there is None else jnp.logical_and(lane, there)
-        return jnp.where(keep, measured / (total + background), 0.0).astype(BF).astype(F32)
-
-    parts = [
-        ratio(0, LX, lower[1], sensor_low[0], sensor_low[1], below),
-        ratio(LX, LX, jnp.where(below, lower[0], 0.0), sensor[0, 0:LX], sensor[1, 0:LX], None),
-        ratio(2 * LX, lens - 2 * LX, None, sensor[0, LX : lens - LX], sensor[1, LX : lens - LX], None),
-        ratio(lens, LX, jnp.where(above, upper[0], 0.0), sensor[0, lens - LX : lens], sensor[1, lens - LX : lens], None),
-        ratio(lens + LX, LX, upper[1], sensor_up[0], sensor_up[1], above),
+    lane = real_lanes(pix)
+
+    def ratio(start, extra, measured, background, keep):
+        return ratio_rows(own, other, start, LX, extra, measured, background, keep)
+
+    planes_ref[0:3, 2 * LX : lens, :] = inner[...]
+    planes_ref[3] = jnp.zeros((rows, PADW), BF)
+    low = [
+        ratio(0, lower[1], sensor_low[0], sensor_low[1], lane & below),
+        ratio(LX, jnp.where(below, lower[0], 0.0), sensor[0, 0:LX], sensor[1, 0:LX], lane),
     ]
-    whole = jnp.concatenate(parts, axis=0)
-    col = column_of(rows, PADW)
-    planes_ref[1] = whole.astype(BF)
-    planes_ref[2] = jnp.where(col > 0, pltpu.roll(whole, 1, 0), 0.0).astype(BF)
-    planes_ref[0] = jnp.where(col < LX - 1, pltpu.roll(whole, rows - 1, 0), 0.0).astype(BF)
-    planes_ref[3] = jnp.zeros((rows, PADW), BF)
+    spread(planes_ref, 0, jnp.concatenate(low, axis=0))
+    high = [
+        ratio(lens, jnp.where(above, upper[0], 0.0), sensor[0, lens - LX :], sensor[1, lens - LX :], lane),
+        ratio(lens + LX, upper[1], sensor_up[0], sensor_up[1], lane & above),
+    ]
+    spread(planes_ref, lens, jnp.concatenate(high, axis=0))
 
 
 def sensitivity_kernel(ids, counts, kp, after, inv_out):
@@ -288,83 +339,100 @@
 
 
 def middle_kernel(
-    pix, ids, counts, own, other, mine, theirs, sensor, sensor_mine, sensor_theirs, est, inv, kp,
-    part_out, send_out, vol_out, ratios, xs, back, acc,
+    pix, ids_in, counts_in, own, other, mine, theirs, inner, sensor, sensor_mine, sensor_theirs, est, inv, kp,
+    part_out, send_out, vol_out, ratios, xs, acc, ids, counts, sem,
 ):
-    ratio_planes(own, other, mine, theirs, sensor, sensor_mine, sensor_theirs, ratios, pix)
+    copies = fetch(ids_in, counts_in, ids, counts, sem)
+    ratio_planes(own, other, mine, theirs, inner, sensor, sensor_mine, sensor_theirs, ratios, pix)
     acc[0:3] = jnp.zeros((3,) + acc.shape[1:], F32)
 
     def body(z):
-        back_slab((ids, counts), z, ratios, kp, back)
-        vol = est[z] * back[...] * inv[z]
-        vol_out[z] = vol
-        xs[...] = vol.astype(BF)
+        def finish(back):
+            vol = est[z] * back * inv[z]
+            vol_out[z] = vol
+            xs[...] = vol.astype(BF)
+
+        back_slab((ids, counts), z, ratios, kp, est.shape[1], finish)
         project_slab((ids, counts), z, xs, kp, acc)
 
+    for c in copies:
+        c.wait()
     each_plane(est.shape[0], body)
     keep_part(fold_dx(acc), part_out, send_out)
 
 
-def middle_call(pix, ids, counts, own, other, mine, theirs, sensors, est, inv, kp):
+def middle_call(pix, ids, counts, own, other, mine, theirs, inner, sensors, est, inv, kp):
     planes, lens, vox = est.shape
     rows = own.shape[0]
     return pl.pallas_call(
         functools.partial(middle_kernel, pix),
         out_shape=(
             jax.ShapeDtypeStruct((rows, PADW), F32),
-            jax.ShapeDtypeStruct((2 * LX, PADW), F32),
+            jax.ShapeDtypeStruct((2 * LX, PADW), BF),
             jax.ShapeDtypeStruct((planes, lens, vox), F32),
         ),
-        in_specs=[SMEM, SMEM] + [VMEM] * 10,
+        in_specs=[ANY, ANY] + [VMEM] * 11,
         out_specs=(VMEM,) * 3,
         scratch_shapes=[
             pltpu.VMEM((4, rows, PADW), BF),
             pltpu.VMEM((lens, vox), BF),
-            pltpu.VMEM((lens, vox), F32),
             pltpu.VMEM((4, rows, PADW), F32),
-        ],
+        ]
+        + list_scratch(ids, counts),
         compiler_params=pltpu.CompilerParams(vmem_limit_bytes=36 << 20),
         cost_estimate=cost(10),
         name="back_and_project",
-    )(ids, counts, own, other, mine, theirs, *sensors, est, inv, kp)
+    )(ids, counts, own, other, mine, theirs, inner, *sensors, est, inv, kp)
 
 
 def last_kernel(
-    pix, ids, counts, own, other, mine, theirs, sensor, sensor_mine, sensor_theirs, vol, inv, kp,
-    out, ratios, back, turned, sem,
+    pix, ids_in, counts_in, own, other, mine, theirs, inner, sensor, sensor_mine, sensor_theirs, vol, inv, kp,
+    out, ratios, turned, sem, ids, counts, list_sem,
 ):
-    ratio_planes(own, other, mine, theirs, sensor, sensor_mine, sensor_theirs, ratios, pix)
-
-    def copy(z):
-        return pltpu.make_async_copy(turned.at[z], out.at[z], sem.at[z])
+    copies = fetch(ids_in, counts_in, ids, counts, list_sem)
+    ratio_planes(own, other, mine, theirs, inner, sensor, sensor_mine, sensor_theirs, ratios, pix)
+
+    vox = vol.shape[2]
+
+    def copy(z, v):
+        here = pl.ds(v * 128, 128)
+        return pltpu.make_async_copy(turned.at[z, here], out.at[z, here], sem.at[z, v])
 
     def body(z):
-        back_slab((ids, counts), z, ratios, kp, back)
-        turned[z] = (vol[z] * back[...] * inv[z]).T
-        copy(z).start()
-
+        def finish(back):
+            for v in range(vox // 128):
+                here = slice(v * 128, (v + 1) * 128)
+                turned[z, here, :] = (vol[z, :, here] * back[:, here] * inv[z, :, here]).T
+                copy(z, v).start()
+
+        back_slab((ids, counts), z, ratios, kp, vol.shape[1], finish)
+
+    for c in copies:
+        c.wait()
     each_plane(vol.shape[0], body)
-    each_plane(vol.shape[0], lambda z: copy(z).wait())
-
-
-def last_call(pix, ids, counts, own, other, mine, theirs, sensors, vol, inv, kp):
+    for z in range(vol.shape[0]):
+        for v in range(vox // 128):
+            copy(z, v).wait()
+
+
+def last_call(pix, ids, counts, own, other, mine, theirs, inner, sensors, vol, inv, kp):
     planes, lens, vox = vol.shape
     rows = own.shape[0]
     return pl.pallas_call(
         functools.partial(last_kernel, pix),
         out_shape=jax.ShapeDtypeStruct((planes, vox, lens), F32),
-        in_specs=[SMEM, SMEM] + [VMEM] * 10,
+        in_specs=[ANY, ANY] + [VMEM] * 11,
         out_specs=ANY,
         scratch_shapes=[
             pltpu.VMEM((4, rows, PADW), BF),
-            pltpu.VMEM((lens, vox), F32),
             pltpu.VMEM((planes, vox, lens), F32),
-            pltpu.SemaphoreType.DMA((planes,)),
-        ],
+            pltpu.SemaphoreType.DMA((planes, vox // 128)),
+        ]
+        + list_scratch(ids, counts),
         compiler_params=pltpu.CompilerParams(vmem_limit_bytes=36 << 20),
         cost_estimate=cost(6),
         name="back_last",
-    )(ids, counts, own, other, mine, theirs, *sensors, vol, inv, kp)
+    )(ids, counts, own, other, mine, theirs, inner, *sensors, vol, inv, kp)
 
 
 def swap(x):
@@ -396,14 +464,17 @@
     inv = sensitivity_call(offset_ids, block_counts, kp, lens, edges)
     other = swap(part)
     sensors = (sensor, sensor_mine, swap(sensor_mine))
-    mine, inv = lax.optimization_barrier((mine, inv))
+    inner = inner_call(pix, part, other, sensor)
+    mine, inv, inner = lax.optimization_barrier((mine, inv, inner))
     part, send, vol = middle_call(
-        pix, offset_ids, block_counts, part, other, mine, swap(mine), sensors, est, inv, kp
+        pix, offset_ids, block_counts, part, other, mine, swap(mine), inner, sensors, est, inv, kp
     )
     edges, part = lax.optimization_barrier((edge_call(part, swap(send)), part))
     mine = edge_exchange(edges)
     other = swap(part)
-    return last_call(pix, offset_ids, block_counts, part, other, mine, swap(mine), sensors, vol, inv, kp)
+    inner = inner_call(pix, part, other, sensor)
+    mine, inner = lax.optimization_barrier((mine, inner))
+    return last_call(pix, offset_ids, block_counts, part, other, mine, swap(mine), inner, sensors, vol, inv, kp)
 
 
 def solution(mesh):

time: 45.2 us -> 40.2 us (0.89); the launches traced: 45 us -> 39.4 us
  Pallas kernels: 24.8 us -> 19.8 us
  waiting for transfers between devices: 9.65 us -> 8.11 us
  starting transfers between devices: 7.86 us -> 8.74 us
    ppermute x3, waiting for transfers between devices: 4.49 us -> 1.67 us  [edge_exchange(): return lax.ppermute(x, ('parts', 'band', 'depth'), pairs)]
    pallas_call x1, Pallas kernels: 8.71 us -> 6.06 us  [middle_call(): pl.pallas_call(functools.partial(middle_kernel, pix), out_shape=(jax.Shap...]
    pallas_call x1, Pallas kernels: 5.67 us -> 4.15 us  [last_call(): pl.pallas_call(functools.partial(last_kernel, pix), out_shape=jax.ShapeDt...]
    ppermute x7, waiting for transfers between devices: 5.16 us -> 6.45 us  [swap(): return lax.ppermute(x, 'depth', [(0, 1), (1, 0)])]
    pallas_call x1, Pallas kernels: 5.19 us -> 4.05 us  [first_call(): pl.pallas_call(first_kernel, out_shape=(jax.ShapeDtypeStruct((rows, PADW)...]
    ppermute x3, starting transfers between devices: 2.15 us -> 2.87 us  [edge_exchange(): return lax.ppermute(x, ('parts', 'band', 'depth'), pairs)]
  transfers between devices with their start and end apart: 10 -> 10, of which waited for: 6 -> 7; matrix products, arithmetic and copies ran while one was open for 0% -> 0% of each run, Pallas kernels for 22% -> 23%
where the time goes in v5:
time: 40.2 us; the launch traced here: 39.4 us
  Pallas kernels  19.8 us (49%)
  starting transfers between devices  8.74 us (22%)
  waiting for transfers between devices  8.11 us (20%)
  local copies, waits for them, and re-layouts  2.5 us (6%)
    ppermute x7, waiting for transfers between devices, swap(): return lax.ppermute(x, 'depth', [(0, 1), (1, 0)])  6.45 us
    pallas_call x1, Pallas kernels, middle_call(): pl.pallas_call(functools.partial(middle_kernel, pix), out_shape=(jax.Shap...  6.06 us
    ppermute x7, starting transfers between devices, swap(): return lax.ppermute(x, 'depth', [(0, 1), (1, 0)])  5.87 us
    pallas_call x1, Pallas kernels, last_call(): pl.pallas_call(functools.partial(last_kernel, pix), out_shape=jax.ShapeDt...  4.15 us
    pallas_call x1, Pallas kernels, first_call(): pl.pallas_call(first_kernel, out_shape=(jax.ShapeDtypeStruct((rows, PADW)...  4.05 us
    ppermute x3, starting transfers between devices, edge_exchange(): return lax.ppermute(x, ('parts', 'band', 'depth'), pairs)  2.87 us
    unnamed x12, local copies, waits for them, and re-layouts  2.5 us
    pallas_call x1, Pallas kernels, split_call(): pl.pallas_call(split_kernel, out_shape=jax.ShapeDtypeStruct((planes, slot...  2.38 us
  transfers between devices with their start and end apart: 10, of which 7 were waited for; matrix products, arithmetic and copies ran while one was open for 0% of the time, Pallas kernels for 23%

profile of v5, /device:TPU:25, one launch (start us, length us, event | category | flops | bytes accessed | tf_op | source)
XLA Modules:
  0.0 39.4 jit_solution(5263986006866533939)
XLA Ops:
  0.0 1.2 %copy-done.2 = f32[361,384]{1,0:T(8,128)S(1)} copy-done((f32[361,384]{1,0:T(8,128)S(1)}, f32[361,384]{1,0:T(8,128)}, u32[]{:S(2)}) %copy-start.2) | copy-done | bytes 554520
  1.2 1.3 %copy-done.3 = f32[361,384]{1,0:T(8,128)S(1)} copy-done((f32[361,384]{1,0:T(8,128)S(1)}, f32[361,384]{1,0:T(8,128)}, u32[]{:S(2)}) %copy-start.3) | copy-done | bytes 554520
  2.5 0.4 %sensor_turn.1 = (f32[2,384,384]{2,1,0:T(8,128)S(1)}, f32[2,104,384]{2,1,0:T(8,128)S(1)}) custom-call(f32[361,384]{1,0:T(8,128)S(1)} %copy-done.2, f32[361,384]{1,0:T(8,128)S(1)} %copy-done.3), custom_call_target="tpu_custom_call" | custom-call | flops 8000000000 | bytes 24000000 | tf_op jit(solution)/shard_map/sensor_turn/pallas_call | solution.py:181
  2.9 1.3 %collective-permute-start.1 = (f32[2,104,384]{2,1,0:T(8,128)S(1)}, f32[2,104,384]{2,1,0:T(8,128)S(1)}, u32[]{:S(2)}, u32[]{:S(2)}) collective-permute-start(f32[2,104,384]{2,1,0:T(8,128)S(1)} %get-tuple-element.24.after), channel_id=1, source_target_pairs={{0,16},{1,3},{2,4},{3,1},{4,2},{5,7},{6,8},{7,5},{8,6},{9,11},{10,... | collective-permute-start | bytes 958472 | tf_op jit(solution)/shard_map/ppermute | solution.py:452
  4.2 0.0 copy-done
  4.2 2.4 %split_planes.1.kp = bf16[2,9,384,512]{3,2,1,0:T(8,128)(2,1)S(1)} custom-call(bf16[9,361,2,512]{3,2,1,0:T(2,128)(2,1)S(1)} %bitcast.1, f32[2,104,384]{2,1,0:T(8,128)S(1)} %get-tuple-element.24.after), custom_call_target="tpu_custom_call" | custom-call | flops 5000000000 | bytes 15000000 | tf_op jit(solution)/shard_map/split_planes/pallas_call | solution.py:111
  6.6 0.0 copy-done.1
  6.7 4.0 %project_first.1 = (f32[576,384]{1,0:T(8,128)S(1)}, bf16[192,384]{1,0:T(8,128)(2,1)S(1)}, f32[2,384,512]{2,1,0:T(8,128)S(1)}) custom-call(s32[2,9]{1,0:T(2,128)S(1)} %copy-done.4, s32[2]{0:T(128)S(1)} %copy-done.5, f32[2,512,384]{2,1,0:T(8,128)S(1)} %copy-done.1, bf16[2,9,384,512]{3,2,1,0:T(8,128)(2,1)S(1)} %split_planes.1.kp), custom_call_target="tpu_custom_call" | custom-call | flops 5000000000 | bytes 15000000 | tf_op jit(solution)/shard_map/project_first/pallas_call | solution.py:141
  10.7 0.4 collective-permute-start
  11.1 1.1 %collective-permute-done.other = bf16[192,384]{1,0:T(8,128)(2,1)S(1)} collective-permute-done((bf16[192,384]{1,0:T(8,128)(2,1)S(1)}, bf16[192,384]{1,0:T(8,128)(2,1)S(1)}, u32[]{:S(2)}, u32[]{:S(2)}) %collective-permute-start) | collective-permute-done | bytes 147488 | tf_op jit(solution)/shard_map/ppermute | solution.py:439
  12.1 0.1 collective-permute-done.1.sensor_mine
  12.3 0.3 collective-permute-start.2
  12.6 1.3 %collective-permute-start.3 = (bf16[2,96,384]{2,1,0:T(8,128)(2,1)S(1)}, bf16[2,96,384]{2,1,0:T(8,128)(2,1)S(1)}, u32[]{:S(2)}, u32[]{:S(2)}) collective-permute-start(bf16[2,96,384]{2,1,0:T(8,128)(2,1)S(1)} %edge_rows.2.after), channel_id=1, source_target_pairs={{0,16},{1,3},{2,4},{3,1},{4,2},{5,7},{6,8},{7,5},{8,6},{9,11},{10,... | collective-permute-start | bytes 442376 | tf_op jit(solution)/shard_map/ppermute | solution.py:452
  13.9 0.4 collective-permute-start.5
  14.3 2.3 %sensitivity.1.inv = f32[2,384,512]{2,1,0:T(8,128)S(1)} custom-call(s32[2,9]{1,0:T(2,128)S(1)} %copy-done.4, s32[2]{0:T(128)S(1)} %copy-done.5, bf16[2,9,384,512]{3,2,1,0:T(8,128)(2,1)S(1)} %split_planes.1.kp, bf16[2,96,384]{2,1,0:T(8,128)(2,1)S(1)} %edge_rows.2.after), custom_call_target="tpu_custom_call" | custom-call | flops 3000000000 | bytes 9000000 | tf_op jit(solution)/shard_map/sensitivity/pallas_call | solution.py:330
  16.6 0.0 collective-permute-done.2.other
  16.6 0.2 inner_ratio.2.inner
  16.8 0.0 collective-permute-done.3.mine
  16.8 2.1 %collective-permute-start.4 = (bf16[2,96,384]{2,1,0:T(8,128)(2,1)S(1)}, bf16[2,96,384]{2,1,0:T(8,128)(2,1)S(1)}, u32[]{:S(2)}, u32[]{:S(2)}) collective-permute-start(bf16[2,96,384]{2,1,0:T(8,128)(2,1)S(1)} %collective-permute-done.3.mine), channel_id=1, source_target_pairs={{0,1},{1,0},{2,3},{3,2},{4,5},{5,4},{6,7},{7,6},{8,9},{9,8},{10,11... | collective-permute-start | bytes 442376 | tf_op jit(solution)/shard_map/ppermute | solution.py:439
  18.9 0.0 collective-permute-done.5.sensor_theirs
  18.9 1.0 %collective-permute-done.4.theirs = bf16[2,96,384]{2,1,0:T(8,128)(2,1)S(1)} collective-permute-done((bf16[2,96,384]{2,1,0:T(8,128)(2,1)S(1)}, bf16[2,96,384]{2,1,0:T(8,128)(2,1)S(1)}, u32[]{:S(2)}, u32[]{:S(2)}) %collective-permute-start.4) | collective-permute-done | bytes 147488 | tf_op jit(solution)/shard_map/ppermute | solution.py:439
  19.9 6.1 %back_and_project.1 = (f32[576,384]{1,0:T(8,128)S(1)}, bf16[192,384]{1,0:T(8,128)(2,1)S(1)}, f32[2,384,512]{2,1,0:T(8,128)S(1)}) custom-call(s32[2,9]{1,0:T(2,128)S(1)} %copy-done.4, s32[2]{0:T(128)S(1)} %copy-done.5, f32[576,384]{1,0:T(8,128)S(1)} %get-tuple-element.28.own, f32[576,384]{1,0:T(8,128)S(1)} %collective-permute-done.2.other, ...), custom_call_target="tpu_custom_call" | custom-call | flops 10000000000 | bytes 30000000 | tf_op jit(solution)/shard_map/back_and_project/pallas_call | solution.py:367
  26.0 0.1 collective-permute-start.6
  26.1 1.4 %collective-permute-done.6.other = bf16[192,384]{1,0:T(8,128)(2,1)S(1)} collective-permute-done((bf16[192,384]{1,0:T(8,128)(2,1)S(1)}, bf16[192,384]{1,0:T(8,128)(2,1)S(1)}, u32[]{:S(2)}, u32[]{:S(2)}) %collective-permute-start.6) | collective-permute-done | bytes 147488 | tf_op jit(solution)/shard_map/ppermute | solution.py:439
  27.5 0.2 collective-permute-start.7
  27.7 0.3 collective-permute-start.8
  27.9 2.0 %collective-permute-done.7.other = f32[576,384]{1,0:T(8,128)S(1)} collective-permute-done((f32[576,384]{1,0:T(8,128)S(1)}, f32[576,384]{1,0:T(8,128)S(1)}, u32[]{:S(2)}, u32[]{:S(2)}) %collective-permute-start.7) | collective-permute-done | bytes 884768 | tf_op jit(solution)/shard_map/ppermute | solution.py:439
  30.0 0.2 inner_ratio.3.inner
  30.1 1.5 %collective-permute-done.8.mine = bf16[2,96,384]{2,1,0:T(8,128)(2,1)S(1)} collective-permute-done((bf16[2,96,384]{2,1,0:T(8,128)(2,1)S(1)}, bf16[2,96,384]{2,1,0:T(8,128)(2,1)S(1)}, u32[]{:S(2)}, u32[]{:S(2)}) %collective-permute-start.8) | collective-permute-done | bytes 147488 | tf_op jit(solution)/shard_map/ppermute | solution.py:452
  31.7 2.4 %collective-permute-start.9 = (bf16[2,96,384]{2,1,0:T(8,128)(2,1)S(1)}, bf16[2,96,384]{2,1,0:T(8,128)(2,1)S(1)}, u32[]{:S(2)}, u32[]{:S(2)}) collective-permute-start(bf16[2,96,384]{2,1,0:T(8,128)(2,1)S(1)} %collective-permute-done.8.mine), channel_id=1, source_target_pairs={{0,1},{1,0},{2,3},{3,2},{4,5},{5,4},{6,7},{7,6},{8,9},{9,8},{10,11... | collective-permute-start | bytes 442376 | tf_op jit(solution)/shard_map/ppermute | solution.py:439
  34.1 1.0 %collective-permute-done.9.theirs = bf16[2,96,384]{2,1,0:T(8,128)(2,1)S(1)} collective-permute-done((bf16[2,96,384]{2,1,0:T(8,128)(2,1)S(1)}, bf16[2,96,384]{2,1,0:T(8,128)(2,1)S(1)}, u32[]{:S(2)}, u32[]{:S(2)}) %collective-permute-start.9) | collective-permute-done | bytes 147488 | tf_op jit(solution)/shard_map/ppermute | solution.py:439
  35.1 4.1 %back_last.1 = f32[2,512,384]{2,1,0:T(8,128)} custom-call(s32[2,9]{1,0:T(2,128)S(1)} %copy-done.4, s32[2]{0:T(128)S(1)} %copy-done.5, f32[576,384]{1,0:T(8,128)S(1)} %get-tuple-element.38.own, f32[576,384]{1,0:T(8,128)S(1)} %collective-permute-done.7.other, bf16[2,96,384]{2,1,0:T(8,128)(2,1)S(1)} %collective-permute-done.8.mine, ...), custom_call_target="tpu_custom_call" | custom-call | flops 6000000000 | bytes 18000000 | tf_op jit(solution)/shard_map/back_last/pallas_call | solution.py:421
  (10 shorter events, 0.1 us)
Async XLA Ops:
  0.0 4.2 %copy-start = (bf16[2,9,361,512]{3,0,2,1:T(2,128)(2,1)S(1)}, bf16[2,9,361,512]{3,0,2,1:T(2,128)(2,1)}, u32[]{:S(2)}) copy-start(bf16[2,9,361,512]{3,0,2,1:T(2,128)(2,1)} %param.7) | copy-start | bytes 19961860
  0.0 1.2 %copy-start.2 = (f32[361,384]{1,0:T(8,128)S(1)}, f32[361,384]{1,0:T(8,128)}, u32[]{:S(2)}) copy-start(f32[361,384]{1,0:T(8,128)} %meas.1) | copy-start | bytes 1663492
  1.2 1.3 %copy-start.3 = (f32[361,384]{1,0:T(8,128)S(1)}, f32[361,384]{1,0:T(8,128)}, u32[]{:S(2)}) copy-start(f32[361,384]{1,0:T(8,128)} %bg.1) | copy-start | bytes 1663492
  2.9 9.3 %collective-permute-start.1 = (f32[2,104,384]{2,1,0:T(8,128)S(1)}, f32[2,104,384]{2,1,0:T(8,128)S(1)}, u32[]{:S(2)}, u32[]{:S(2)}) collective-permute-start(f32[2,104,384]{2,1,0:T(8,128)S(1)} %get-tuple-element.24.after), channel_id=1, source_target_pairs={{0,16},{1,3},{2,4},{3,1},{4,2},{5,7},{6,8},{7,5},{8,6},{9,11},{10,... | collective-permute-start | bytes 958472 | tf_op jit(solution)/shard_map/ppermute | solution.py:452
  4.2 2.4 %copy-start.1 = (f32[2,512,384]{2,1,0:T(8,128)S(1)}, f32[2,512,384]{2,1,0:T(8,128)}, u32[]{:S(2)}) copy-start(f32[2,512,384]{2,1,0:T(8,128)} %est.1) | copy-start | bytes 4718596
  4.2 2.4 %copy-start.4 = (s32[2,9]{1,0:T(2,128)S(1)}, s32[2,9]{1,0:T(2,128)}, u32[]{:S(2)}) copy-start(s32[2,9]{1,0:T(2,128)} %ids_in.5) | copy-start | bytes 220
  4.2 2.4 %copy-start.5 = (s32[2]{0:T(128)S(1)}, s32[2]{0:T(128)}, u32[]{:S(2)}) copy-start(s32[2]{0:T(128)} %counts_in.5) | copy-start | bytes 28
  10.7 1.4 %collective-permute-start = (bf16[192,384]{1,0:T(8,128)(2,1)S(1)}, bf16[192,384]{1,0:T(8,128)(2,1)S(1)}, u32[]{:S(2)}, u32[]{:S(2)}) collective-permute-start(bf16[192,384]{1,0:T(8,128)(2,1)S(1)} %get-tuple-element.26), channel_id=1, source_target_pairs={{0,1},{1,0},{2,3},{3,2},{4,5},{5,4},{6,7},{7,6},{8,9},{9,8},{10,11... | collective-permute-start | bytes 442376 | tf_op jit(solution)/shard_map/ppermute | solution.py:439
  12.3 4.3 %collective-permute-start.2 = (f32[576,384]{1,0:T(8,128)S(1)}, f32[576,384]{1,0:T(8,128)S(1)}, u32[]{:S(2)}, u32[]{:S(2)}) collective-permute-start(f32[576,384]{1,0:T(8,128)S(1)} %get-tuple-element.28.own), channel_id=1, source_target_pairs={{0,1},{1,0},{2,3},{3,2},{4,5},{5,4},{6,7},{7,6},{8,9},{9,8},{10,11... | collective-permute-start | bytes 2654216 | tf_op jit(solution)/shard_map/ppermute | solution.py:439
  12.6 4.2 %collective-permute-start.3 = (bf16[2,96,384]{2,1,0:T(8,128)(2,1)S(1)}, bf16[2,96,384]{2,1,0:T(8,128)(2,1)S(1)}, u32[]{:S(2)}, u32[]{:S(2)}) collective-permute-start(bf16[2,96,384]{2,1,0:T(8,128)(2,1)S(1)} %edge_rows.2.after), channel_id=1, source_target_pairs={{0,16},{1,3},{2,4},{3,1},{4,2},{5,7},{6,8},{7,5},{8,6},{9,11},{10,... | collective-permute-start | bytes 442376 | tf_op jit(solution)/shard_map/ppermute | solution.py:452
  13.9 5.0 %collective-permute-start.5 = (f32[2,104,384]{2,1,0:T(8,128)S(1)}, f32[2,104,384]{2,1,0:T(8,128)S(1)}, u32[]{:S(2)}, u32[]{:S(2)}) collective-permute-start(f32[2,104,384]{2,1,0:T(8,128)S(1)} %collective-permute-done.1.sensor_mine), channel_id=1, source_target_pairs={{0,1},{1,0},{2,3},{3,2},{4,5},{5,4},{6,7},{7,6},{8,9},{9,8},{10,11... | collective-permute-start | bytes 958472 | tf_op jit(solution)/shard_map/ppermute | solution.py:439
  16.8 3.2 %collective-permute-start.4 = (bf16[2,96,384]{2,1,0:T(8,128)(2,1)S(1)}, bf16[2,96,384]{2,1,0:T(8,128)(2,1)S(1)}, u32[]{:S(2)}, u32[]{:S(2)}) collective-permute-start(bf16[2,96,384]{2,1,0:T(8,128)(2,1)S(1)} %collective-permute-done.3.mine), channel_id=1, source_target_pairs={{0,1},{1,0},{2,3},{3,2},{4,5},{5,4},{6,7},{7,6},{8,9},{9,8},{10,11... | collective-permute-start | bytes 442376 | tf_op jit(solution)/shard_map/ppermute | solution.py:439
  26.0 1.4 %collective-permute-start.6 = (bf16[192,384]{1,0:T(8,128)(2,1)S(1)}, bf16[192,384]{1,0:T(8,128)(2,1)S(1)}, u32[]{:S(2)}, u32[]{:S(2)}) collective-permute-start(bf16[192,384]{1,0:T(8,128)(2,1)S(1)} %get-tuple-element.37), channel_id=1, source_target_pairs={{0,1},{1,0},{2,3},{3,2},{4,5},{5,4},{6,7},{7,6},{8,9},{9,8},{10,11... | collective-permute-start | bytes 442376 | tf_op jit(solution)/shard_map/ppermute | solution.py:439
  27.5 2.5 %collective-permute-start.7 = (f32[576,384]{1,0:T(8,128)S(1)}, f32[576,384]{1,0:T(8,128)S(1)}, u32[]{:S(2)}, u32[]{:S(2)}) collective-permute-start(f32[576,384]{1,0:T(8,128)S(1)} %get-tuple-element.38.own), channel_id=1, source_target_pairs={{0,1},{1,0},{2,3},{3,2},{4,5},{5,4},{6,7},{7,6},{8,9},{9,8},{10,11... | collective-permute-start | bytes 2654216 | tf_op jit(solution)/shard_map/ppermute | solution.py:439
  27.7 4.0 %collective-permute-start.8 = (bf16[2,96,384]{2,1,0:T(8,128)(2,1)S(1)}, bf16[2,96,384]{2,1,0:T(8,128)(2,1)S(1)}, u32[]{:S(2)}, u32[]{:S(2)}) collective-permute-start(bf16[2,96,384]{2,1,0:T(8,128)(2,1)S(1)} %edge_rows.3), channel_id=1, source_target_pairs={{0,16},{1,3},{2,4},{3,1},{4,2},{5,7},{6,8},{7,5},{8,6},{9,11},{10,... | collective-permute-start | bytes 442376 | tf_op jit(solution)/shard_map/ppermute | solution.py:452
  31.7 3.4 %collective-permute-start.9 = (bf16[2,96,384]{2,1,0:T(8,128)(2,1)S(1)}, bf16[2,96,384]{2,1,0:T(8,128)(2,1)S(1)}, u32[]{:S(2)}, u32[]{:S(2)}) collective-permute-start(bf16[2,96,384]{2,1,0:T(8,128)(2,1)S(1)} %collective-permute-done.8.mine), channel_id=1, source_target_pairs={{0,1},{1,0},{2,3},{3,2},{4,5},{5,4},{6,7},{7,6},{8,9},{9,8},{10,11... | collective-permute-start | bytes 442376 | tf_op jit(solution)/shard_map/ppermute | solution.py:439

commit v6 on v5

--- a/solution.py
+++ b/solution.py
@@ -49,10 +49,9 @@
     return start, jnp.where(slot < count_of(info, plane), ident % 3, 3)
 
 
-def by_pairs(info, plane, slots, body):
-    pairs = (count_of(info, plane) + 1) // 2
-    for k in range(1, (slots + 1) // 2 + 1):
-        pl.when(pairs == k)(functools.partial(body, min(2 * k, slots)))
+def by_count(info, plane, slots, body):
+    for k in range(1, slots + 1):
+        pl.when(count_of(info, plane) == k)(functools.partial(body, k))
 
 
 def project_slab(info, plane, x, kp, acc):
@@ -64,7 +63,7 @@
             row, dx = place(info, plane, s)
             acc[dx, pl.ds(row, rows), :] += out[:, s * PADW : (s + 1) * PADW]
 
-    by_pairs(info, plane, kp.shape[1], body)
+    by_count(info, plane, kp.shape[1], body)
 
 
 def back_slab(info, plane, ratios, kp, lens, finish):
@@ -77,7 +76,7 @@
             left.append(ratios[dx, pl.ds(row, lens), :])
         finish(dot(jnp.concatenate(left, axis=1), kp[plane, 0:used].reshape(used * PADW, vox)))
 
-    by_pairs(info, plane, kp.shape[1], body)
+    by_count(info, plane, kp.shape[1], body)
 
 
 def each_plane(planes, body):

time: 40.2 us -> 43 us (1.070)
  Pallas kernels: 19.8 us -> 22.9 us
    pallas_call x1, Pallas kernels: 6.06 us -> 7.8 us  [middle_call(): pl.pallas_call(functools.partial(middle_kernel, pix), out_shape=(jax.Shap...]
    pallas_call x1, Pallas kernels: 4.05 us -> 4.99 us  [first_call(): pl.pallas_call(first_kernel, out_shape=(jax.ShapeDtypeStruct((rows, PADW)...]
    pallas_call x1, Pallas kernels: 4.15 us -> 4.61 us  [last_call(): pl.pallas_call(functools.partial(last_kernel, pix), out_shape=jax.ShapeDt...]
  transfers between devices with their start and end apart: 10 -> 10, of which waited for: 7 -> 6; matrix products, arithmetic and copies ran while one was open for 0% -> 0% of each run, Pallas kernels for 23% -> 24%
where the time goes in v6:
time: 43 us; the launch traced here: 42.5 us
  Pallas kernels  22.9 us (53%)
  starting transfers between devices  8.5 us (20%)
  waiting for transfers between devices  8.24 us (19%)
  local copies, waits for them, and re-layouts  2.5 us (6%)
    pallas_call x1, Pallas kernels, middle_call(): pl.pallas_call(functools.partial(middle_kernel, pix), out_shape=(jax.Shap...  7.8 us
    ppermute x7, waiting for transfers between devices, swap(): return lax.ppermute(x, 'depth', [(0, 1), (1, 0)])  6.69 us
    ppermute x7, starting transfers between devices, swap(): return lax.ppermute(x, 'depth', [(0, 1), (1, 0)])  5.69 us
    pallas_call x1, Pallas kernels, first_call(): pl.pallas_call(first_kernel, out_shape=(jax.ShapeDtypeStruct((rows, PADW)...  4.99 us
    pallas_call x1, Pallas kernels, last_call(): pl.pallas_call(functools.partial(last_kernel, pix), out_shape=jax.ShapeDt...  4.61 us
    ppermute x3, starting transfers between devices, edge_exchange(): return lax.ppermute(x, ('parts', 'band', 'depth'), pairs)  2.81 us
    unnamed x12, local copies, waits for them, and re-layouts  2.5 us
    pallas_call x1, Pallas kernels, split_call(): pl.pallas_call(split_kernel, out_shape=jax.ShapeDtypeStruct((planes, slot...  2.38 us
  transfers between devices with their start and end apart: 10, of which 6 were waited for; matrix products, arithmetic and copies ran while one was open for 0% of the time, Pallas kernels for 24%

profile of v6, /device:TPU:25, one launch (start us, length us, event | category | flops | bytes accessed | tf_op | source)
XLA Modules:
  0.0 42.5 jit_solution(1838901101465612742)
XLA Ops:
  0.0 1.2 %copy-done.2 = f32[361,384]{1,0:T(8,128)S(1)} copy-done((f32[361,384]{1,0:T(8,128)S(1)}, f32[361,384]{1,0:T(8,128)}, u32[]{:S(2)}) %copy-start.2) | copy-done | bytes 554520
  1.2 1.3 %copy-done.3 = f32[361,384]{1,0:T(8,128)S(1)} copy-done((f32[361,384]{1,0:T(8,128)S(1)}, f32[361,384]{1,0:T(8,128)}, u32[]{:S(2)}) %copy-start.3) | copy-done | bytes 554520
  2.5 0.4 %sensor_turn.1 = (f32[2,384,384]{2,1,0:T(8,128)S(1)}, f32[2,104,384]{2,1,0:T(8,128)S(1)}) custom-call(f32[361,384]{1,0:T(8,128)S(1)} %copy-done.2, f32[361,384]{1,0:T(8,128)S(1)} %copy-done.3), custom_call_target="tpu_custom_call" | custom-call | flops 8000000000 | bytes 24000000 | tf_op jit(solution)/shard_map/sensor_turn/pallas_call | solution.py:180
  2.9 1.3 %collective-permute-start.1 = (f32[2,104,384]{2,1,0:T(8,128)S(1)}, f32[2,104,384]{2,1,0:T(8,128)S(1)}, u32[]{:S(2)}, u32[]{:S(2)}) collective-permute-start(f32[2,104,384]{2,1,0:T(8,128)S(1)} %get-tuple-element.24.after), channel_id=1, source_target_pairs={{0,16},{1,3},{2,4},{3,1},{4,2},{5,7},{6,8},{7,5},{8,6},{9,11},{10,... | collective-permute-start | bytes 958472 | tf_op jit(solution)/shard_map/ppermute | solution.py:451
  4.2 0.0 copy-done
  4.2 2.4 %split_planes.1.kp = bf16[2,9,384,512]{3,2,1,0:T(8,128)(2,1)S(1)} custom-call(bf16[9,361,2,512]{3,2,1,0:T(2,128)(2,1)S(1)} %bitcast.1, f32[2,104,384]{2,1,0:T(8,128)S(1)} %get-tuple-element.24.after), custom_call_target="tpu_custom_call" | custom-call | flops 5000000000 | bytes 15000000 | tf_op jit(solution)/shard_map/split_planes/pallas_call | solution.py:110
  6.6 0.0 copy-done.1
  6.7 5.0 %project_first.1 = (f32[576,384]{1,0:T(8,128)S(1)}, bf16[192,384]{1,0:T(8,128)(2,1)S(1)}, f32[2,384,512]{2,1,0:T(8,128)S(1)}) custom-call(s32[2,9]{1,0:T(2,128)S(1)} %copy-done.4, s32[2]{0:T(128)S(1)} %copy-done.5, f32[2,512,384]{2,1,0:T(8,128)S(1)} %copy-done.1, bf16[2,9,384,512]{3,2,1,0:T(8,128)(2,1)S(1)} %split_planes.1.kp), custom_call_target="tpu_custom_call" | custom-call | flops 5000000000 | bytes 15000000 | tf_op jit(solution)/shard_map/project_first/pallas_call | solution.py:140
  11.6 0.2 collective-permute-start
  11.9 1.2 %collective-permute-done.other = bf16[192,384]{1,0:T(8,128)(2,1)S(1)} collective-permute-done((bf16[192,384]{1,0:T(8,128)(2,1)S(1)}, bf16[192,384]{1,0:T(8,128)(2,1)S(1)}, u32[]{:S(2)}, u32[]{:S(2)}) %collective-permute-start) | collective-permute-done | bytes 147488 | tf_op jit(solution)/shard_map/ppermute | solution.py:438
  13.1 0.0 collective-permute-done.1.sensor_mine
  13.1 0.2 collective-permute-start.2
  13.3 1.3 %collective-permute-start.3 = (bf16[2,96,384]{2,1,0:T(8,128)(2,1)S(1)}, bf16[2,96,384]{2,1,0:T(8,128)(2,1)S(1)}, u32[]{:S(2)}, u32[]{:S(2)}) collective-permute-start(bf16[2,96,384]{2,1,0:T(8,128)(2,1)S(1)} %edge_rows.2.after), channel_id=1, source_target_pairs={{0,16},{1,3},{2,4},{3,1},{4,2},{5,7},{6,8},{7,5},{8,6},{9,11},{10,... | collective-permute-start | bytes 442376 | tf_op jit(solution)/shard_map/ppermute | solution.py:451
  14.7 0.3 collective-permute-start.5
  15.0 2.3 %sensitivity.1.inv = f32[2,384,512]{2,1,0:T(8,128)S(1)} custom-call(s32[2,9]{1,0:T(2,128)S(1)} %copy-done.4, s32[2]{0:T(128)S(1)} %copy-done.5, bf16[2,9,384,512]{3,2,1,0:T(8,128)(2,1)S(1)} %split_planes.1.kp, bf16[2,96,384]{2,1,0:T(8,128)(2,1)S(1)} %edge_rows.2.after), custom_call_target="tpu_custom_call" | custom-call | flops 3000000000 | bytes 9000000 | tf_op jit(solution)/shard_map/sensitivity/pallas_call | solution.py:329
  17.3 0.0 collective-permute-done.2.other
  17.3 0.2 inner_ratio.2.inner
  17.5 0.0 collective-permute-done.3.mine
  17.5 2.3 %collective-permute-start.4 = (bf16[2,96,384]{2,1,0:T(8,128)(2,1)S(1)}, bf16[2,96,384]{2,1,0:T(8,128)(2,1)S(1)}, u32[]{:S(2)}, u32[]{:S(2)}) collective-permute-start(bf16[2,96,384]{2,1,0:T(8,128)(2,1)S(1)} %collective-permute-done.3.mine), channel_id=1, source_target_pairs={{0,1},{1,0},{2,3},{3,2},{4,5},{5,4},{6,7},{7,6},{8,9},{9,8},{10,11... | collective-permute-start | bytes 442376 | tf_op jit(solution)/shard_map/ppermute | solution.py:438
  19.7 0.0 collective-permute-done.5.sensor_theirs
  19.7 1.0 %collective-permute-done.4.theirs = bf16[2,96,384]{2,1,0:T(8,128)(2,1)S(1)} collective-permute-done((bf16[2,96,384]{2,1,0:T(8,128)(2,1)S(1)}, bf16[2,96,384]{2,1,0:T(8,128)(2,1)S(1)}, u32[]{:S(2)}, u32[]{:S(2)}) %collective-permute-start.4) | collective-permute-done | bytes 147488 | tf_op jit(solution)/shard_map/ppermute | solution.py:438
  20.8 7.8 %back_and_project.1 = (f32[576,384]{1,0:T(8,128)S(1)}, bf16[192,384]{1,0:T(8,128)(2,1)S(1)}, f32[2,384,512]{2,1,0:T(8,128)S(1)}) custom-call(s32[2,9]{1,0:T(2,128)S(1)} %copy-done.4, s32[2]{0:T(128)S(1)} %copy-done.5, f32[576,384]{1,0:T(8,128)S(1)} %get-tuple-element.28.own, f32[576,384]{1,0:T(8,128)S(1)} %collective-permute-done.2.other, ...), custom_call_target="tpu_custom_call" | custom-call | flops 10000000000 | bytes 30000000 | tf_op jit(solution)/shard_map/back_and_project/pallas_call | solution.py:366
  28.6 0.1 collective-permute-start.6
  28.6 1.4 %collective-permute-done.6.other = bf16[192,384]{1,0:T(8,128)(2,1)S(1)} collective-permute-done((bf16[192,384]{1,0:T(8,128)(2,1)S(1)}, bf16[192,384]{1,0:T(8,128)(2,1)S(1)}, u32[]{:S(2)}, u32[]{:S(2)}) %collective-permute-start.6) | collective-permute-done | bytes 147488 | tf_op jit(solution)/shard_map/ppermute | solution.py:438
  30.0 0.2 collective-permute-start.7
  30.2 0.2 collective-permute-start.8
  30.4 2.1 %collective-permute-done.7.other = f32[576,384]{1,0:T(8,128)S(1)} collective-permute-done((f32[576,384]{1,0:T(8,128)S(1)}, f32[576,384]{1,0:T(8,128)S(1)}, u32[]{:S(2)}, u32[]{:S(2)}) %collective-permute-start.7) | collective-permute-done | bytes 884768 | tf_op jit(solution)/shard_map/ppermute | solution.py:438
  32.5 0.2 inner_ratio.3.inner
  32.7 1.5 %collective-permute-done.8.mine = bf16[2,96,384]{2,1,0:T(8,128)(2,1)S(1)} collective-permute-done((bf16[2,96,384]{2,1,0:T(8,128)(2,1)S(1)}, bf16[2,96,384]{2,1,0:T(8,128)(2,1)S(1)}, u32[]{:S(2)}, u32[]{:S(2)}) %collective-permute-start.8) | collective-permute-done | bytes 147488 | tf_op jit(solution)/shard_map/ppermute | solution.py:451
  34.2 2.4 %collective-permute-start.9 = (bf16[2,96,384]{2,1,0:T(8,128)(2,1)S(1)}, bf16[2,96,384]{2,1,0:T(8,128)(2,1)S(1)}, u32[]{:S(2)}, u32[]{:S(2)}) collective-permute-start(bf16[2,96,384]{2,1,0:T(8,128)(2,1)S(1)} %collective-permute-done.8.mine), channel_id=1, source_target_pairs={{0,1},{1,0},{2,3},{3,2},{4,5},{5,4},{6,7},{7,6},{8,9},{9,8},{10,11... | collective-permute-start | bytes 442376 | tf_op jit(solution)/shard_map/ppermute | solution.py:438
  36.7 1.0 %collective-permute-done.9.theirs = bf16[2,96,384]{2,1,0:T(8,128)(2,1)S(1)} collective-permute-done((bf16[2,96,384]{2,1,0:T(8,128)(2,1)S(1)}, bf16[2,96,384]{2,1,0:T(8,128)(2,1)S(1)}, u32[]{:S(2)}, u32[]{:S(2)}) %collective-permute-start.9) | collective-permute-done | bytes 147488 | tf_op jit(solution)/shard_map/ppermute | solution.py:438
  37.7 4.6 %back_last.1 = f32[2,512,384]{2,1,0:T(8,128)} custom-call(s32[2,9]{1,0:T(2,128)S(1)} %copy-done.4, s32[2]{0:T(128)S(1)} %copy-done.5, f32[576,384]{1,0:T(8,128)S(1)} %get-tuple-element.38.own, f32[576,384]{1,0:T(8,128)S(1)} %collective-permute-done.7.other, bf16[2,96,384]{2,1,0:T(8,128)(2,1)S(1)} %collective-permute-done.8.mine, ...), custom_call_target="tpu_custom_call" | custom-call | flops 6000000000 | bytes 18000000 | tf_op jit(solution)/shard_map/back_last/pallas_call | solution.py:420
  (10 shorter events, 0.1 us)
Async XLA Ops:
  0.0 4.2 %copy-start = (bf16[2,9,361,512]{3,0,2,1:T(2,128)(2,1)S(1)}, bf16[2,9,361,512]{3,0,2,1:T(2,128)(2,1)}, u32[]{:S(2)}) copy-start(bf16[2,9,361,512]{3,0,2,1:T(2,128)(2,1)} %param.7) | copy-start | bytes 19961860
  0.0 1.2 %copy-start.2 = (f32[361,384]{1,0:T(8,128)S(1)}, f32[361,384]{1,0:T(8,128)}, u32[]{:S(2)}) copy-start(f32[361,384]{1,0:T(8,128)} %meas.1) | copy-start | bytes 1663492
  1.2 1.3 %copy-start.3 = (f32[361,384]{1,0:T(8,128)S(1)}, f32[361,384]{1,0:T(8,128)}, u32[]{:S(2)}) copy-start(f32[361,384]{1,0:T(8,128)} %bg.1) | copy-start | bytes 1663492
  2.9 10.1 %collective-permute-start.1 = (f32[2,104,384]{2,1,0:T(8,128)S(1)}, f32[2,104,384]{2,1,0:T(8,128)S(1)}, u32[]{:S(2)}, u32[]{:S(2)}) collective-permute-start(f32[2,104,384]{2,1,0:T(8,128)S(1)} %get-tuple-element.24.after), channel_id=1, source_target_pairs={{0,16},{1,3},{2,4},{3,1},{4,2},{5,7},{6,8},{7,5},{8,6},{9,11},{10,... | collective-permute-start | bytes 958472 | tf_op jit(solution)/shard_map/ppermute | solution.py:451
  4.2 2.4 %copy-start.1 = (f32[2,512,384]{2,1,0:T(8,128)S(1)}, f32[2,512,384]{2,1,0:T(8,128)}, u32[]{:S(2)}) copy-start(f32[2,512,384]{2,1,0:T(8,128)} %est.1) | copy-start | bytes 4718596
  4.2 2.4 %copy-start.4 = (s32[2,9]{1,0:T(2,128)S(1)}, s32[2,9]{1,0:T(2,128)}, u32[]{:S(2)}) copy-start(s32[2,9]{1,0:T(2,128)} %ids_in.5) | copy-start | bytes 220
  4.2 2.4 %copy-start.5 = (s32[2]{0:T(128)S(1)}, s32[2]{0:T(128)}, u32[]{:S(2)}) copy-start(s32[2]{0:T(128)} %counts_in.5) | copy-start | bytes 28
  11.6 1.4 %collective-permute-start = (bf16[192,384]{1,0:T(8,128)(2,1)S(1)}, bf16[192,384]{1,0:T(8,128)(2,1)S(1)}, u32[]{:S(2)}, u32[]{:S(2)}) collective-permute-start(bf16[192,384]{1,0:T(8,128)(2,1)S(1)} %get-tuple-element.26), channel_id=1, source_target_pairs={{0,1},{1,0},{2,3},{3,2},{4,5},{5,4},{6,7},{7,6},{8,9},{9,8},{10,11... | collective-permute-start | bytes 442376 | tf_op jit(solution)/shard_map/ppermute | solution.py:438
  13.1 4.2 %collective-permute-start.2 = (f32[576,384]{1,0:T(8,128)S(1)}, f32[576,384]{1,0:T(8,128)S(1)}, u32[]{:S(2)}, u32[]{:S(2)}) collective-permute-start(f32[576,384]{1,0:T(8,128)S(1)} %get-tuple-element.28.own), channel_id=1, source_target_pairs={{0,1},{1,0},{2,3},{3,2},{4,5},{5,4},{6,7},{7,6},{8,9},{9,8},{10,11... | collective-permute-start | bytes 2654216 | tf_op jit(solution)/shard_map/ppermute | solution.py:438
  13.3 4.1 %collective-permute-start.3 = (bf16[2,96,384]{2,1,0:T(8,128)(2,1)S(1)}, bf16[2,96,384]{2,1,0:T(8,128)(2,1)S(1)}, u32[]{:S(2)}, u32[]{:S(2)}) collective-permute-start(bf16[2,96,384]{2,1,0:T(8,128)(2,1)S(1)} %edge_rows.2.after), channel_id=1, source_target_pairs={{0,16},{1,3},{2,4},{3,1},{4,2},{5,7},{6,8},{7,5},{8,6},{9,11},{10,... | collective-permute-start | bytes 442376 | tf_op jit(solution)/shard_map/ppermute | solution.py:451
  14.7 5.1 %collective-permute-start.5 = (f32[2,104,384]{2,1,0:T(8,128)S(1)}, f32[2,104,384]{2,1,0:T(8,128)S(1)}, u32[]{:S(2)}, u32[]{:S(2)}) collective-permute-start(f32[2,104,384]{2,1,0:T(8,128)S(1)} %collective-permute-done.1.sensor_mine), channel_id=1, source_target_pairs={{0,1},{1,0},{2,3},{3,2},{4,5},{5,4},{6,7},{7,6},{8,9},{9,8},{10,11... | collective-permute-start | bytes 958472 | tf_op jit(solution)/shard_map/ppermute | solution.py:438
  17.5 3.3 %collective-permute-start.4 = (bf16[2,96,384]{2,1,0:T(8,128)(2,1)S(1)}, bf16[2,96,384]{2,1,0:T(8,128)(2,1)S(1)}, u32[]{:S(2)}, u32[]{:S(2)}) collective-permute-start(bf16[2,96,384]{2,1,0:T(8,128)(2,1)S(1)} %collective-permute-done.3.mine), channel_id=1, source_target_pairs={{0,1},{1,0},{2,3},{3,2},{4,5},{5,4},{6,7},{7,6},{8,9},{9,8},{10,11... | collective-permute-start | bytes 442376 | tf_op jit(solution)/shard_map/ppermute | solution.py:438
  28.6 1.4 %collective-permute-start.6 = (bf16[192,384]{1,0:T(8,128)(2,1)S(1)}, bf16[192,384]{1,0:T(8,128)(2,1)S(1)}, u32[]{:S(2)}, u32[]{:S(2)}) collective-permute-start(bf16[192,384]{1,0:T(8,128)(2,1)S(1)} %get-tuple-element.37), channel_id=1, source_target_pairs={{0,1},{1,0},{2,3},{3,2},{4,5},{5,4},{6,7},{7,6},{8,9},{9,8},{10,11... | collective-permute-start | bytes 442376 | tf_op jit(solution)/shard_map/ppermute | solution.py:438
  30.0 2.5 %collective-permute-start.7 = (f32[576,384]{1,0:T(8,128)S(1)}, f32[576,384]{1,0:T(8,128)S(1)}, u32[]{:S(2)}, u32[]{:S(2)}) collective-permute-start(f32[576,384]{1,0:T(8,128)S(1)} %get-tuple-element.38.own), channel_id=1, source_target_pairs={{0,1},{1,0},{2,3},{3,2},{4,5},{5,4},{6,7},{7,6},{8,9},{9,8},{10,11... | collective-permute-start | bytes 2654216 | tf_op jit(solution)/shard_map/ppermute | solution.py:438
  30.2 4.0 %collective-permute-start.8 = (bf16[2,96,384]{2,1,0:T(8,128)(2,1)S(1)}, bf16[2,96,384]{2,1,0:T(8,128)(2,1)S(1)}, u32[]{:S(2)}, u32[]{:S(2)}) collective-permute-start(bf16[2,96,384]{2,1,0:T(8,128)(2,1)S(1)} %edge_rows.3), channel_id=1, source_target_pairs={{0,16},{1,3},{2,4},{3,1},{4,2},{5,7},{6,8},{7,5},{8,6},{9,11},{10,... | collective-permute-start | bytes 442376 | tf_op jit(solution)/shard_map/ppermute | solution.py:451
  34.2 3.4 %collective-permute-start.9 = (bf16[2,96,384]{2,1,0:T(8,128)(2,1)S(1)}, bf16[2,96,384]{2,1,0:T(8,128)(2,1)S(1)}, u32[]{:S(2)}, u32[]{:S(2)}) collective-permute-start(bf16[2,96,384]{2,1,0:T(8,128)(2,1)S(1)} %collective-permute-done.8.mine), channel_id=1, source_target_pairs={{0,1},{1,0},{2,3},{3,2},{4,5},{5,4},{6,7},{7,6},{8,9},{9,8},{10,11... | collective-permute-start | bytes 442376 | tf_op jit(solution)/shard_map/ppermute | solution.py:438
